TPU v7x, 32 devices: a whole 2x2x4 slice. The times are simulated.
32 devices in a mesh: groups: 2 (over y), brow: 4 (over z), bcol: 2 (over x), mpo: 2 (over core).
Axes of the slice: x: 2, y: 2, z: 4, core: 2. Of those that a mesh axis runs over, the one named last changes fastest.
Arguments:
- amplitudes: bfloat16 [512, 16, 256], P(('groups', 'brow'), None, 'bcol'), parts along dimension 0, may hold values from -18 to 18
- left_env: bfloat16 [52, 256, 192], P(('groups', 'mpo'), 'brow'), parts along dimension 0, may hold values from -1 to 2
- right_env: bfloat16 [52, 256, 128], P('groups', 'bcol'), parts along dimension 0, may hold values from -1 to 2
- mpo_left: float32 [26, 26, 4, 4], replicated, may hold values from -1 to 1
- mpo_right: float32 [26, 26, 4, 4], replicated, may hold values from -1 to 1
- sector_table: int32 [512], P('groups'), parts along dimension 0, may hold values from 0 to 3, never falling along the last dimension, each value on 1 to 128 neighbouring positions
Outputs:
- image_two: bfloat16 [512, 16, 256], P(('groups', 'brow'), 'mpo', 'bcol'), parts along dimension 0
- basis_two: bfloat16 [512, 16, 256], P(('groups', 'brow'), 'mpo', 'bcol'), parts along dimension 0
- projected: float32 [4, 2], P('groups'), parts along dimension 0
There are 2 independent parts, one for each index of `groups`. A program takes and returns all parts, laid end to end along the dimension named above; an argument that names none is the same for every part. Nothing has to cross between parts.
Inputs may be any that keep to these rules, and one draw needn't show every extreme that they name: `sector_table`: sector labels never fall along the rows; each sector covers 1 to 128 consecutive rows.
All inputs are finite; a program needn't handle non-finite values.
Results may differ from a plain program's by a relative error of at most 0.0095.
Values may be sent and summed in bfloat16 or wider, within the bound.
No kernel may reach another device: no remote copies, remote signals or barrier semaphores. Data moves between devices by JAX's collectives and lax.ppermute only.
A program may use at most 64 MiB of HBM per device.

v0:
```python
import jax
import jax.numpy as jnp
from jax import lax
from jax.sharding import PartitionSpec as P

EPSILON = 1e-06


def extended_2(x, sides, width):
    for axis, dim in sides:
        peers, length = (lax.axis_size(axis), x.shape[dim])
        up = [(i, (i + 1) % peers) for i in range(peers - 1)]
        down = [(j, i) for i, j in up]
        last = lax.slice_in_dim(x, length - width, length, axis=dim)
        first = lax.slice_in_dim(x, 0, width, axis=dim)
        before = lax.ppermute(last, axis, up)
        after = lax.ppermute(first, axis, down)
        x = jnp.concatenate([before, x, after], axis=dim)
    return x


def per_device(amplitudes, left_env, right_env, mpo_left, mpo_right, sector_table):
    row_count = amplitudes.shape[0]
    phys_dim = amplitudes.shape[1]
    col_count = amplitudes.shape[2]
    bond_local = left_env.shape[0]
    bond_full = mpo_left.shape[0]
    local_dim = mpo_left.shape[2]
    block_index = lax.axis_index("brow")
    group_index = lax.axis_index("mpo")
    entries = float(
        row_count * lax.axis_size("brow") * phys_dim * col_count * lax.axis_size("bcol")
    )
    half_phys = phys_dim // lax.axis_size("mpo")
    outside = jnp.full((row_count,), -1, dtype=jnp.int32)
    padded = jnp.concatenate([outside, sector_table, outside])
    own_labels = lax.dynamic_slice_in_dim(padded, (block_index + 1) * row_count, row_count, 0)
    partner = lax.dynamic_slice_in_dim(padded, block_index * row_count, 3 * row_count, 0)
    band_mask = own_labels[:, None] == partner[None, :]
    joined = jnp.einsum("wmik,mvjl->wklvij", mpo_left, mpo_right, precision=lax.Precision.HIGHEST)
    combined = joined.reshape(
        bond_full, local_dim * local_dim, bond_full, local_dim * local_dim
    ).astype(jnp.bfloat16)
    coupling = lax.dynamic_slice_in_dim(combined, group_index * bond_local, bond_local, 0)
    masked_env = jnp.where(band_mask[None], left_env, jnp.zeros((), left_env.dtype))

    def apply_operator(vector):
        extended = extended_2(vector, (("brow", 0),), row_count)
        flat_rows = extended.reshape(3 * row_count, phys_dim * col_count)
        contracted = jnp.dot(
            masked_env.reshape(bond_local * row_count, 3 * row_count),
            flat_rows,
            preferred_element_type=jnp.float32,
        )
        contracted = contracted.astype(jnp.bfloat16).reshape(
            bond_local, row_count, phys_dim, col_count
        )

        def add_pair(pair_index, running):
            weights_pair = lax.dynamic_slice_in_dim(coupling, pair_index * 2, 2, 2)
            mixed_rows = jnp.einsum(
                "wtvs,watb->vasb", weights_pair, contracted, preferred_element_type=jnp.float32
            ).astype(jnp.bfloat16)
            env_pair = lax.dynamic_slice_in_dim(right_env, pair_index * 2, 2, 0)
            return running + jnp.einsum(
                "vasb,vbc->asc", mixed_rows, env_pair, preferred_element_type=jnp.float32
            )

        start_value = jnp.zeros((row_count, phys_dim, col_count), jnp.float32)
        return lax.fori_loop(0, bond_full // 2, add_pair, start_value)

    def own_half(array):
        return lax.dynamic_slice_in_dim(array, group_index * half_phys, half_phys, 1)

    wide = amplitudes.astype(jnp.float32)
    square_sum = lax.psum(jnp.sum(wide * wide), ("brow", "bcol"))
    scale = jnp.sqrt(square_sum / entries + EPSILON)
    basis_one = (wide / scale).astype(jnp.bfloat16)
    partial_one = apply_operator(basis_one)
    first_basis = own_half(basis_one).astype(jnp.float32)
    image_whole = lax.psum(partial_one, "mpo")
    image_mine = own_half(image_whole)
    correlation = lax.psum(jnp.sum(first_basis * image_mine), ("brow", "bcol", "mpo")) / entries
    residual_mine = image_mine - correlation * first_basis
    residual_sq = lax.psum(jnp.sum(residual_mine * residual_mine), ("brow", "bcol", "mpo"))
    residual_norm = jnp.sqrt(residual_sq / entries + EPSILON)
    basis_two_mine = (residual_mine / residual_norm).astype(jnp.bfloat16)
    residual_whole = image_whole - correlation * basis_one.astype(jnp.float32)
    basis_two_whole = (residual_whole / residual_norm).astype(jnp.bfloat16)
    partial_two = apply_operator(basis_two_whole)
    image_two = lax.psum_scatter(partial_two, "mpo", scatter_dimension=1, tiled=True)
    final_correlation = (
        lax.psum(jnp.sum(basis_two_mine.astype(jnp.float32) * image_two), ("brow", "bcol", "mpo"))
        / entries
    )
    projected = jnp.stack(
        [jnp.stack([correlation, residual_norm]), jnp.stack([residual_norm, final_correlation])]
    )
    return (image_two.astype(jnp.bfloat16), basis_two_mine, projected)


def solution(mesh):
    return jax.shard_map(
        per_device,
        mesh=mesh,
        in_specs=(
            P(("groups", "brow"), None, "bcol"),
            P(("groups", "mpo"), "brow", None),
            P("groups", "bcol", None),
            P(),
            P(),
            P("groups"),
        ),
        out_specs=(
            P(("groups", "brow"), "mpo", "bcol"),
            P(("groups", "brow"), "mpo", "bcol"),
            P("groups", None),
        ),
        check_vma=False,
    )
```

profile of v0, /device:TPU:0, one launch (start us, length us, event | category | flops | bytes accessed | tf_op | source)
XLA Modules:
  0.0 338.3 jit_solution(6339804993307108678)
XLA Ops:
  7.2 1.7 fusion.40
  9.0 23.7 %psum.35 = f32[]{:T(128)} all-reduce(f32[]{:T(128)} %fusion.40), channel_id=1, replica_groups=mesh['groups'=2,'brow'=4,'bcol'=2,'mpo'=2] {'brow','bcol'}, use_global_device_ids=true, to_apply=%region_1.2 | all-reduce | flops 1 | bytes 8 | tf_op jit(solution)/shard_map/psum | solution.py:76
  34.4 2.0 collective-permute-start
  38.6 4.6 %convert_bitcast_fusion = bf16[26,4,4,26,4,4]{3,0,1,4,2,5:T(8,128)(2,1)S(1)} fusion(f32[26,26,4,4,1,1]{1,3,2,0,5,4:T(4,128)S(1)} %bitcast.117, f32[26,26,4,4,1,1]{1,3,2,0,5,4:T(4,128)} %bitcast.125), kind=kOutput, calls=%fused_computation.24 | convolution fusion | flops 54166528 | bytes 432640 | tf_op jit(solution)/shard_map/wmik,mvjl->wklvij/dot_general | solution.py:40
  43.2 1.3 copy.13
  47.2 2.8 copy.29
  50.0 65.9 %while.28 = (s32[]{:T(128)}, f32[64,16,128]{2,1,0:T(8,128)S(1)}, bf16[13,16,26,16]{2,3,1,0:T(8,128)(2,1)S(1)}, bf16[13,64,16,128]{3,2,1,0:T(8,128)(2,1)}, bf16[2...) while((s32[]{:T(128)}, f32[64,16,128]{2,1,0:T(8,128)S(1)}, ...), condition=%wide.region_3.4_spmd.clone, body=%wide.region_2.3_spmd.clone.sunk | while | flops 176685056 | bytes 4588701 | solution.py:70
  50.3 1.3 copy.69
  51.6 3.4 %fusion.66 = f32[64,16,128]{2,1,0:T(8,128)S(1)} fusion(bf16[13,16,2,16,1]{1,3,0,2,4:T(8,128)(2,1)S(1)} %copy.69, f32[64,16,128]{2,1,0:T(8,128)S(1)} %get-tuple-element.324, pred[]{:T(512)S(6)} %compare.6, bf16[26,128,128]{2,1,0:T(8,128)(2,1)} %get-tuple-element.336, s32[]{:T(128)S(6)} %select_n.43, bf16[13,64,16,128]{3,2,1,0:T(8,128)(2,1)} %get-tuple-element.335), kind=kOutput, calls=%fused_computation.6.clone.1 | convolution fusion | flops 176685056 | bytes 4535301 | tf_op jit(solution)/shard_map/while/body/eval_jaxpr/vasb,vbc->asc/dot_general | solution.py:65
  55.4 1.3 copy.69
  56.7 3.4 %fusion.66 = f32[64,16,128]{2,1,0:T(8,128)S(1)} fusion(bf16[13,16,2,16,1]{1,3,0,2,4:T(8,128)(2,1)S(1)} %copy.69, f32[64,16,128]{2,1,0:T(8,128)S(1)} %get-tuple-element.324, pred[]{:T(512)S(6)} %compare.6, bf16[26,128,128]{2,1,0:T(8,128)(2,1)} %get-tuple-element.336, s32[]{:T(128)S(6)} %select_n.43, bf16[13,64,16,128]{3,2,1,0:T(8,128)(2,1)} %get-tuple-element.335), kind=kOutput, calls=%fused_computation.6.clone.1 | convolution fusion | flops 176685056 | bytes 4535301 | tf_op jit(solution)/shard_map/while/body/eval_jaxpr/vasb,vbc->asc/dot_general | solution.py:65
  60.5 1.3 copy.69
  61.8 3.4 %fusion.66 = f32[64,16,128]{2,1,0:T(8,128)S(1)} fusion(bf16[13,16,2,16,1]{1,3,0,2,4:T(8,128)(2,1)S(1)} %copy.69, f32[64,16,128]{2,1,0:T(8,128)S(1)} %get-tuple-element.324, pred[]{:T(512)S(6)} %compare.6, bf16[26,128,128]{2,1,0:T(8,128)(2,1)} %get-tuple-element.336, s32[]{:T(128)S(6)} %select_n.43, bf16[13,64,16,128]{3,2,1,0:T(8,128)(2,1)} %get-tuple-element.335), kind=kOutput, calls=%fused_computation.6.clone.1 | convolution fusion | flops 176685056 | bytes 4535301 | tf_op jit(solution)/shard_map/while/body/eval_jaxpr/vasb,vbc->asc/dot_general | solution.py:65
  65.5 1.3 copy.69
  66.9 3.4 %fusion.66 = f32[64,16,128]{2,1,0:T(8,128)S(1)} fusion(bf16[13,16,2,16,1]{1,3,0,2,4:T(8,128)(2,1)S(1)} %copy.69, f32[64,16,128]{2,1,0:T(8,128)S(1)} %get-tuple-element.324, pred[]{:T(512)S(6)} %compare.6, bf16[26,128,128]{2,1,0:T(8,128)(2,1)} %get-tuple-element.336, s32[]{:T(128)S(6)} %select_n.43, bf16[13,64,16,128]{3,2,1,0:T(8,128)(2,1)} %get-tuple-element.335), kind=kOutput, calls=%fused_computation.6.clone.1 | convolution fusion | flops 176685056 | bytes 4535301 | tf_op jit(solution)/shard_map/while/body/eval_jaxpr/vasb,vbc->asc/dot_general | solution.py:65
  70.6 1.3 copy.69
  71.9 3.4 %fusion.66 = f32[64,16,128]{2,1,0:T(8,128)S(1)} fusion(bf16[13,16,2,16,1]{1,3,0,2,4:T(8,128)(2,1)S(1)} %copy.69, f32[64,16,128]{2,1,0:T(8,128)S(1)} %get-tuple-element.324, pred[]{:T(512)S(6)} %compare.6, bf16[26,128,128]{2,1,0:T(8,128)(2,1)} %get-tuple-element.336, s32[]{:T(128)S(6)} %select_n.43, bf16[13,64,16,128]{3,2,1,0:T(8,128)(2,1)} %get-tuple-element.335), kind=kOutput, calls=%fused_computation.6.clone.1 | convolution fusion | flops 176685056 | bytes 4535301 | tf_op jit(solution)/shard_map/while/body/eval_jaxpr/vasb,vbc->asc/dot_general | solution.py:65
  75.7 1.3 copy.69
  77.0 3.4 %fusion.66 = f32[64,16,128]{2,1,0:T(8,128)S(1)} fusion(bf16[13,16,2,16,1]{1,3,0,2,4:T(8,128)(2,1)S(1)} %copy.69, f32[64,16,128]{2,1,0:T(8,128)S(1)} %get-tuple-element.324, pred[]{:T(512)S(6)} %compare.6, bf16[26,128,128]{2,1,0:T(8,128)(2,1)} %get-tuple-element.336, s32[]{:T(128)S(6)} %select_n.43, bf16[13,64,16,128]{3,2,1,0:T(8,128)(2,1)} %get-tuple-element.335), kind=kOutput, calls=%fused_computation.6.clone.1 | convolution fusion | flops 176685056 | bytes 4535301 | tf_op jit(solution)/shard_map/while/body/eval_jaxpr/vasb,vbc->asc/dot_general | solution.py:65
  80.7 1.3 copy.69
  82.0 3.4 %fusion.66 = f32[64,16,128]{2,1,0:T(8,128)S(1)} fusion(bf16[13,16,2,16,1]{1,3,0,2,4:T(8,128)(2,1)S(1)} %copy.69, f32[64,16,128]{2,1,0:T(8,128)S(1)} %get-tuple-element.324, pred[]{:T(512)S(6)} %compare.6, bf16[26,128,128]{2,1,0:T(8,128)(2,1)} %get-tuple-element.336, s32[]{:T(128)S(6)} %select_n.43, bf16[13,64,16,128]{3,2,1,0:T(8,128)(2,1)} %get-tuple-element.335), kind=kOutput, calls=%fused_computation.6.clone.1 | convolution fusion | flops 176685056 | bytes 4535301 | tf_op jit(solution)/shard_map/while/body/eval_jaxpr/vasb,vbc->asc/dot_general | solution.py:65
  85.8 1.3 copy.69
  87.1 3.4 %fusion.66 = f32[64,16,128]{2,1,0:T(8,128)S(1)} fusion(bf16[13,16,2,16,1]{1,3,0,2,4:T(8,128)(2,1)S(1)} %copy.69, f32[64,16,128]{2,1,0:T(8,128)S(1)} %get-tuple-element.324, pred[]{:T(512)S(6)} %compare.6, bf16[26,128,128]{2,1,0:T(8,128)(2,1)} %get-tuple-element.336, s32[]{:T(128)S(6)} %select_n.43, bf16[13,64,16,128]{3,2,1,0:T(8,128)(2,1)} %get-tuple-element.335), kind=kOutput, calls=%fused_computation.6.clone.1 | convolution fusion | flops 176685056 | bytes 4535301 | tf_op jit(solution)/shard_map/while/body/eval_jaxpr/vasb,vbc->asc/dot_general | solution.py:65
  90.9 1.3 copy.69
  92.2 3.4 %fusion.66 = f32[64,16,128]{2,1,0:T(8,128)S(1)} fusion(bf16[13,16,2,16,1]{1,3,0,2,4:T(8,128)(2,1)S(1)} %copy.69, f32[64,16,128]{2,1,0:T(8,128)S(1)} %get-tuple-element.324, pred[]{:T(512)S(6)} %compare.6, bf16[26,128,128]{2,1,0:T(8,128)(2,1)} %get-tuple-element.336, s32[]{:T(128)S(6)} %select_n.43, bf16[13,64,16,128]{3,2,1,0:T(8,128)(2,1)} %get-tuple-element.335), kind=kOutput, calls=%fused_computation.6.clone.1 | convolution fusion | flops 176685056 | bytes 4535301 | tf_op jit(solution)/shard_map/while/body/eval_jaxpr/vasb,vbc->asc/dot_general | solution.py:65
  96.0 1.3 copy.69
  97.3 3.4 %fusion.66 = f32[64,16,128]{2,1,0:T(8,128)S(1)} fusion(bf16[13,16,2,16,1]{1,3,0,2,4:T(8,128)(2,1)S(1)} %copy.69, f32[64,16,128]{2,1,0:T(8,128)S(1)} %get-tuple-element.324, pred[]{:T(512)S(6)} %compare.6, bf16[26,128,128]{2,1,0:T(8,128)(2,1)} %get-tuple-element.336, s32[]{:T(128)S(6)} %select_n.43, bf16[13,64,16,128]{3,2,1,0:T(8,128)(2,1)} %get-tuple-element.335), kind=kOutput, calls=%fused_computation.6.clone.1 | convolution fusion | flops 176685056 | bytes 4535301 | tf_op jit(solution)/shard_map/while/body/eval_jaxpr/vasb,vbc->asc/dot_general | solution.py:65
  101.0 1.3 copy.69
  102.3 3.4 %fusion.66 = f32[64,16,128]{2,1,0:T(8,128)S(1)} fusion(bf16[13,16,2,16,1]{1,3,0,2,4:T(8,128)(2,1)S(1)} %copy.69, f32[64,16,128]{2,1,0:T(8,128)S(1)} %get-tuple-element.324, pred[]{:T(512)S(6)} %compare.6, bf16[26,128,128]{2,1,0:T(8,128)(2,1)} %get-tuple-element.336, s32[]{:T(128)S(6)} %select_n.43, bf16[13,64,16,128]{3,2,1,0:T(8,128)(2,1)} %get-tuple-element.335), kind=kOutput, calls=%fused_computation.6.clone.1 | convolution fusion | flops 176685056 | bytes 4535301 | tf_op jit(solution)/shard_map/while/body/eval_jaxpr/vasb,vbc->asc/dot_general | solution.py:65
  106.1 1.3 copy.69
  107.4 3.4 %fusion.66 = f32[64,16,128]{2,1,0:T(8,128)S(1)} fusion(bf16[13,16,2,16,1]{1,3,0,2,4:T(8,128)(2,1)S(1)} %copy.69, f32[64,16,128]{2,1,0:T(8,128)S(1)} %get-tuple-element.324, pred[]{:T(512)S(6)} %compare.6, bf16[26,128,128]{2,1,0:T(8,128)(2,1)} %get-tuple-element.336, s32[]{:T(128)S(6)} %select_n.43, bf16[13,64,16,128]{3,2,1,0:T(8,128)(2,1)} %get-tuple-element.335), kind=kOutput, calls=%fused_computation.6.clone.1 | convolution fusion | flops 176685056 | bytes 4535301 | tf_op jit(solution)/shard_map/while/body/eval_jaxpr/vasb,vbc->asc/dot_general | solution.py:65
  111.1 1.3 copy.69
  112.5 3.4 %fusion.66 = f32[64,16,128]{2,1,0:T(8,128)S(1)} fusion(bf16[13,16,2,16,1]{1,3,0,2,4:T(8,128)(2,1)S(1)} %copy.69, f32[64,16,128]{2,1,0:T(8,128)S(1)} %get-tuple-element.324, pred[]{:T(512)S(6)} %compare.6, bf16[26,128,128]{2,1,0:T(8,128)(2,1)} %get-tuple-element.336, s32[]{:T(128)S(6)} %select_n.43, bf16[13,64,16,128]{3,2,1,0:T(8,128)(2,1)} %get-tuple-element.335), kind=kOutput, calls=%fused_computation.6.clone.1 | convolution fusion | flops 176685056 | bytes 4535301 | tf_op jit(solution)/shard_map/while/body/eval_jaxpr/vasb,vbc->asc/dot_general | solution.py:65
  116.8 18.5 %all-reduce.2.cloned.1.call-done = f32[64,16,128]{2,1,0:T(8,128)} async-done(((f32[64,16,128]{2,1,0:T(8,128)}), f32[64,16,128]{2,1,0:T(8,128)}) %all-reduce.2.cloned.1.call-update) | async-done | bytes 524304 | tf_op jit(solution)/shard_map/psum | solution.py:81
  135.3 1.6 fusion.42
  136.9 34.5 %psum.37 = f32[]{:T(128)} all-reduce(f32[]{:T(128)} %fusion.42), channel_id=1, replica_groups=mesh['groups'=2,'brow'=4,'bcol'=2,'mpo'=2] {'brow','bcol','mpo'}, use_global_device_ids=true, to_apply=%region_6.7 | all-reduce | flops 1 | bytes 8 | tf_op jit(solution)/shard_map/psum | solution.py:83
  172.1 1.6 multiply_reduce_fusion.1
  173.7 30.1 %psum.38 = f32[]{:T(128)} all-reduce(f32[]{:T(128)} %multiply_reduce_fusion.1), channel_id=1, replica_groups=mesh['groups'=2,'brow'=4,'bcol'=2,'mpo'=2] {'brow','bcol','mpo'}, use_global_device_ids=true, to_apply=%region_8.9 | all-reduce | flops 1 | bytes 8 | tf_op jit(solution)/shard_map/psum | solution.py:85
  207.0 1.5 collective-permute-start.3
  208.5 4.3 %collective-permute-done.2 = bf16[64,16,128]{2,1,0:T(8,128)(2,1)S(1)} collective-permute-done((bf16[64,16,128]{2,1,0:T(8,128)(2,1)S(1)}, bf16[64,16,128]{2,1,0:T(8,128)(2,1)S(1)}, u32[]{:S(2)}, u32[]{:S(2)}) %collective-permute-start.2) | collective-permute-done | bytes 262176 | tf_op jit(solution)/shard_map/ppermute | solution.py:16
  212.8 4.1 %collective-permute-done.3 = bf16[64,16,128]{2,1,0:T(8,128)(2,1)S(1)} collective-permute-done((bf16[64,16,128]{2,1,0:T(8,128)(2,1)S(1)}, bf16[64,16,128]{2,1,0:T(8,128)(2,1)S(1)}, u32[]{:S(2)}, u32[]{:S(2)}) %collective-permute-start.3) | collective-permute-done | bytes 262176 | tf_op jit(solution)/shard_map/ppermute | solution.py:17
  218.1 2.8 copy.31
  220.9 65.9 %while.29 = (s32[]{:T(128)}, f32[64,16,128]{2,1,0:T(8,128)S(1)}, bf16[13,16,26,16]{2,3,1,0:T(8,128)(2,1)S(1)}, bf16[13,64,16,128]{3,2,1,0:T(8,128)(2,1)}, bf16[2...) while((s32[]{:T(128)}, f32[64,16,128]{2,1,0:T(8,128)S(1)}, ...), condition=%wide.region_10.11_spmd.clone, body=%wide.region_9.10_spmd.clone.sunk | while | flops 176685056 | bytes 4588701 | solution.py:70
  222.6 3.4 %fusion.71 = f32[64,16,128]{2,1,0:T(8,128)S(1)} fusion(bf16[13,16,2,16,1]{1,3,0,2,4:T(8,128)(2,1)S(1)} %copy.71, f32[64,16,128]{2,1,0:T(8,128)S(1)} %get-tuple-element.351, pred[]{:T(512)S(6)} %compare.7, bf16[26,128,128]{2,1,0:T(8,128)(2,1)} %get-tuple-element.363, s32[]{:T(128)S(6)} %select_n.44, bf16[13,64,16,128]{3,2,1,0:T(8,128)(2,1)} %get-tuple-element.362), kind=kOutput, calls=%fused_computation.17.clone.1 | convolution fusion | flops 176685056 | bytes 4535301 | tf_op jit(solution)/shard_map/while/body/eval_jaxpr/vasb,vbc->asc/dot_general | solution.py:65
  227.6 3.4 %fusion.71 = f32[64,16,128]{2,1,0:T(8,128)S(1)} fusion(bf16[13,16,2,16,1]{1,3,0,2,4:T(8,128)(2,1)S(1)} %copy.71, f32[64,16,128]{2,1,0:T(8,128)S(1)} %get-tuple-element.351, pred[]{:T(512)S(6)} %compare.7, bf16[26,128,128]{2,1,0:T(8,128)(2,1)} %get-tuple-element.363, s32[]{:T(128)S(6)} %select_n.44, bf16[13,64,16,128]{3,2,1,0:T(8,128)(2,1)} %get-tuple-element.362), kind=kOutput, calls=%fused_computation.17.clone.1 | convolution fusion | flops 176685056 | bytes 4535301 | tf_op jit(solution)/shard_map/while/body/eval_jaxpr/vasb,vbc->asc/dot_general | solution.py:65
  232.7 3.4 %fusion.71 = f32[64,16,128]{2,1,0:T(8,128)S(1)} fusion(bf16[13,16,2,16,1]{1,3,0,2,4:T(8,128)(2,1)S(1)} %copy.71, f32[64,16,128]{2,1,0:T(8,128)S(1)} %get-tuple-element.351, pred[]{:T(512)S(6)} %compare.7, bf16[26,128,128]{2,1,0:T(8,128)(2,1)} %get-tuple-element.363, s32[]{:T(128)S(6)} %select_n.44, bf16[13,64,16,128]{3,2,1,0:T(8,128)(2,1)} %get-tuple-element.362), kind=kOutput, calls=%fused_computation.17.clone.1 | convolution fusion | flops 176685056 | bytes 4535301 | tf_op jit(solution)/shard_map/while/body/eval_jaxpr/vasb,vbc->asc/dot_general | solution.py:65
  237.7 3.4 %fusion.71 = f32[64,16,128]{2,1,0:T(8,128)S(1)} fusion(bf16[13,16,2,16,1]{1,3,0,2,4:T(8,128)(2,1)S(1)} %copy.71, f32[64,16,128]{2,1,0:T(8,128)S(1)} %get-tuple-element.351, pred[]{:T(512)S(6)} %compare.7, bf16[26,128,128]{2,1,0:T(8,128)(2,1)} %get-tuple-element.363, s32[]{:T(128)S(6)} %select_n.44, bf16[13,64,16,128]{3,2,1,0:T(8,128)(2,1)} %get-tuple-element.362), kind=kOutput, calls=%fused_computation.17.clone.1 | convolution fusion | flops 176685056 | bytes 4535301 | tf_op jit(solution)/shard_map/while/body/eval_jaxpr/vasb,vbc->asc/dot_general | solution.py:65
  242.8 3.4 %fusion.71 = f32[64,16,128]{2,1,0:T(8,128)S(1)} fusion(bf16[13,16,2,16,1]{1,3,0,2,4:T(8,128)(2,1)S(1)} %copy.71, f32[64,16,128]{2,1,0:T(8,128)S(1)} %get-tuple-element.351, pred[]{:T(512)S(6)} %compare.7, bf16[26,128,128]{2,1,0:T(8,128)(2,1)} %get-tuple-element.363, s32[]{:T(128)S(6)} %select_n.44, bf16[13,64,16,128]{3,2,1,0:T(8,128)(2,1)} %get-tuple-element.362), kind=kOutput, calls=%fused_computation.17.clone.1 | convolution fusion | flops 176685056 | bytes 4535301 | tf_op jit(solution)/shard_map/while/body/eval_jaxpr/vasb,vbc->asc/dot_general | solution.py:65
  247.9 3.4 %fusion.71 = f32[64,16,128]{2,1,0:T(8,128)S(1)} fusion(bf16[13,16,2,16,1]{1,3,0,2,4:T(8,128)(2,1)S(1)} %copy.71, f32[64,16,128]{2,1,0:T(8,128)S(1)} %get-tuple-element.351, pred[]{:T(512)S(6)} %compare.7, bf16[26,128,128]{2,1,0:T(8,128)(2,1)} %get-tuple-element.363, s32[]{:T(128)S(6)} %select_n.44, bf16[13,64,16,128]{3,2,1,0:T(8,128)(2,1)} %get-tuple-element.362), kind=kOutput, calls=%fused_computation.17.clone.1 | convolution fusion | flops 176685056 | bytes 4535301 | tf_op jit(solution)/shard_map/while/body/eval_jaxpr/vasb,vbc->asc/dot_general | solution.py:65
  251.6 1.3 copy.71
  253.0 3.4 %fusion.71 = f32[64,16,128]{2,1,0:T(8,128)S(1)} fusion(bf16[13,16,2,16,1]{1,3,0,2,4:T(8,128)(2,1)S(1)} %copy.71, f32[64,16,128]{2,1,0:T(8,128)S(1)} %get-tuple-element.351, pred[]{:T(512)S(6)} %compare.7, bf16[26,128,128]{2,1,0:T(8,128)(2,1)} %get-tuple-element.363, s32[]{:T(128)S(6)} %select_n.44, bf16[13,64,16,128]{3,2,1,0:T(8,128)(2,1)} %get-tuple-element.362), kind=kOutput, calls=%fused_computation.17.clone.1 | convolution fusion | flops 176685056 | bytes 4535301 | tf_op jit(solution)/shard_map/while/body/eval_jaxpr/vasb,vbc->asc/dot_general | solution.py:65
  258.0 3.4 %fusion.71 = f32[64,16,128]{2,1,0:T(8,128)S(1)} fusion(bf16[13,16,2,16,1]{1,3,0,2,4:T(8,128)(2,1)S(1)} %copy.71, f32[64,16,128]{2,1,0:T(8,128)S(1)} %get-tuple-element.351, pred[]{:T(512)S(6)} %compare.7, bf16[26,128,128]{2,1,0:T(8,128)(2,1)} %get-tuple-element.363, s32[]{:T(128)S(6)} %select_n.44, bf16[13,64,16,128]{3,2,1,0:T(8,128)(2,1)} %get-tuple-element.362), kind=kOutput, calls=%fused_computation.17.clone.1 | convolution fusion | flops 176685056 | bytes 4535301 | tf_op jit(solution)/shard_map/while/body/eval_jaxpr/vasb,vbc->asc/dot_general | solution.py:65
  261.8 1.3 copy.71
  263.1 3.4 %fusion.71 = f32[64,16,128]{2,1,0:T(8,128)S(1)} fusion(bf16[13,16,2,16,1]{1,3,0,2,4:T(8,128)(2,1)S(1)} %copy.71, f32[64,16,128]{2,1,0:T(8,128)S(1)} %get-tuple-element.351, pred[]{:T(512)S(6)} %compare.7, bf16[26,128,128]{2,1,0:T(8,128)(2,1)} %get-tuple-element.363, s32[]{:T(128)S(6)} %select_n.44, bf16[13,64,16,128]{3,2,1,0:T(8,128)(2,1)} %get-tuple-element.362), kind=kOutput, calls=%fused_computation.17.clone.1 | convolution fusion | flops 176685056 | bytes 4535301 | tf_op jit(solution)/shard_map/while/body/eval_jaxpr/vasb,vbc->asc/dot_general | solution.py:65
  266.8 1.3 copy.71
  268.2 3.4 %fusion.71 = f32[64,16,128]{2,1,0:T(8,128)S(1)} fusion(bf16[13,16,2,16,1]{1,3,0,2,4:T(8,128)(2,1)S(1)} %copy.71, f32[64,16,128]{2,1,0:T(8,128)S(1)} %get-tuple-element.351, pred[]{:T(512)S(6)} %compare.7, bf16[26,128,128]{2,1,0:T(8,128)(2,1)} %get-tuple-element.363, s32[]{:T(128)S(6)} %select_n.44, bf16[13,64,16,128]{3,2,1,0:T(8,128)(2,1)} %get-tuple-element.362), kind=kOutput, calls=%fused_computation.17.clone.1 | convolution fusion | flops 176685056 | bytes 4535301 | tf_op jit(solution)/shard_map/while/body/eval_jaxpr/vasb,vbc->asc/dot_general | solution.py:65
  271.9 1.3 copy.71
  273.2 3.4 %fusion.71 = f32[64,16,128]{2,1,0:T(8,128)S(1)} fusion(bf16[13,16,2,16,1]{1,3,0,2,4:T(8,128)(2,1)S(1)} %copy.71, f32[64,16,128]{2,1,0:T(8,128)S(1)} %get-tuple-element.351, pred[]{:T(512)S(6)} %compare.7, bf16[26,128,128]{2,1,0:T(8,128)(2,1)} %get-tuple-element.363, s32[]{:T(128)S(6)} %select_n.44, bf16[13,64,16,128]{3,2,1,0:T(8,128)(2,1)} %get-tuple-element.362), kind=kOutput, calls=%fused_computation.17.clone.1 | convolution fusion | flops 176685056 | bytes 4535301 | tf_op jit(solution)/shard_map/while/body/eval_jaxpr/vasb,vbc->asc/dot_general | solution.py:65
  278.3 3.4 %fusion.71 = f32[64,16,128]{2,1,0:T(8,128)S(1)} fusion(bf16[13,16,2,16,1]{1,3,0,2,4:T(8,128)(2,1)S(1)} %copy.71, f32[64,16,128]{2,1,0:T(8,128)S(1)} %get-tuple-element.351, pred[]{:T(512)S(6)} %compare.7, bf16[26,128,128]{2,1,0:T(8,128)(2,1)} %get-tuple-element.363, s32[]{:T(128)S(6)} %select_n.44, bf16[13,64,16,128]{3,2,1,0:T(8,128)(2,1)} %get-tuple-element.362), kind=kOutput, calls=%fused_computation.17.clone.1 | convolution fusion | flops 176685056 | bytes 4535301 | tf_op jit(solution)/shard_map/while/body/eval_jaxpr/vasb,vbc->asc/dot_general | solution.py:65
  282.0 1.3 copy.71
  283.4 3.4 %fusion.71 = f32[64,16,128]{2,1,0:T(8,128)S(1)} fusion(bf16[13,16,2,16,1]{1,3,0,2,4:T(8,128)(2,1)S(1)} %copy.71, f32[64,16,128]{2,1,0:T(8,128)S(1)} %get-tuple-element.351, pred[]{:T(512)S(6)} %compare.7, bf16[26,128,128]{2,1,0:T(8,128)(2,1)} %get-tuple-element.363, s32[]{:T(128)S(6)} %select_n.44, bf16[13,64,16,128]{3,2,1,0:T(8,128)(2,1)} %get-tuple-element.362), kind=kOutput, calls=%fused_computation.17.clone.1 | convolution fusion | flops 176685056 | bytes 4535301 | tf_op jit(solution)/shard_map/while/body/eval_jaxpr/vasb,vbc->asc/dot_general | solution.py:65
  287.7 5.6 %reduce-scatter.2.cloned.1.call-done = f32[64,8,128]{2,1,0:T(8,128)} async-done(((f32[64,16,128]{2,1,0:T(8,128)}), f32[64,8,128]{2,1,0:T(8,128)}) %reduce-scatter.2.cloned.1.call-update) | async-done | bytes 262160 | tf_op jit(solution)/shard_map/reduce_scatter | solution.py:91
  293.3 2.4 multiply_reduce_fusion
  295.7 34.5 %psum.39 = f32[]{:T(128)} all-reduce(f32[]{:T(128)} %get-tuple-element.249), channel_id=1, replica_groups=mesh['groups'=2,'brow'=4,'bcol'=2,'mpo'=2] {'brow','bcol','mpo'}, use_global_device_ids=true, to_apply=%region_13.14 | all-reduce | flops 1 | bytes 8 | tf_op jit(solution)/shard_map/psum | solution.py:93
  (76 shorter events, 30.1 us)
Async XLA Ops:
  7.2 31.4 %copy-start = (f32[26,26,4,4]{1,3,2,0:T(4,128)S(1)}, f32[26,26,4,4]{1,3,2,0:T(4,128)}, u32[]{:S(2)}) copy-start(f32[26,26,4,4]{1,3,2,0:T(4,128)} %param.13) | copy-start | bytes 129796
  7.2 128.1 %all-reduce.2.cloned.1.call-start = ((), (), s32[]{:S(2)}) async-start(), calls=%async_computation.1 | async-start | bytes 1048576 | tf_op jit(solution)/shard_map/psum | solution.py:81
  34.4 10.4 %collective-permute-start = (bf16[64,16,128]{2,1,0:T(8,128)(2,1)S(1)}, bf16[64,16,128]{2,1,0:T(8,128)(2,1)}, u32[]{:S(2)}, u32[]{:S(2)}) collective-permute-start(bf16[64,16,128]{2,1,0:T(8,128)(2,1)S(1)} %fusion.41), channel_id=1, source_target_pairs={{0,4},{4,8},{8,12},{1,5},{5,9},{9,13},{2,6},{6,10},{10,14},{3,7},{... | collective-permute-start | bytes 786440 | tf_op jit(solution)/shard_map/ppermute | solution.py:16
  36.4 8.5 %collective-permute-start.1 = (bf16[64,16,128]{2,1,0:T(8,128)(2,1)S(1)}, bf16[64,16,128]{2,1,0:T(8,128)(2,1)}, u32[]{:S(2)}, u32[]{:S(2)}) collective-permute-start(bf16[64,16,128]{2,1,0:T(8,128)(2,1)S(1)} %fusion.41), channel_id=1, source_target_pairs={{4,0},{8,4},{12,8},{5,1},{9,5},{13,9},{6,2},{10,6},{14,10},{7,3},{... | collective-permute-start | bytes 786440 | tf_op jit(solution)/shard_map/ppermute | solution.py:17
  43.2 1.6 copy-start.5
  44.8 2.4 copy-start.6
  50.0 154.5 %copy-start.2 = (bf16[64,16,128]{2,1,0:T(8,128)(2,1)S(1)}, bf16[64,16,128]{2,1,0:T(8,128)(2,1)}, u32[]{:S(2)}) copy-start(bf16[64,16,128]{2,1,0:T(8,128)(2,1)} %param.10) | copy-start | bytes 786436
  115.9 0.8 copy-start.3
  115.9 101.1 %copy-start.7 = (bf16[13,64,192]{2,1,0:T(8,128)(2,1)S(1)}, bf16[13,64,192]{2,1,0:T(8,128)(2,1)}, u32[]{:S(2)}) copy-start(bf16[13,64,192]{2,1,0:T(8,128)(2,1)} %copy-done.6) | copy-start | bytes 958468
  116.7 176.5 %reduce-scatter.2.cloned.1.call-start = ((), (), s32[]{:S(2)}) async-start(), calls=%async_computation.2 | async-start | bytes 786432 | tf_op jit(solution)/shard_map/reduce_scatter | solution.py:91
  205.6 7.2 %collective-permute-start.2 = (bf16[64,16,128]{2,1,0:T(8,128)(2,1)S(1)}, bf16[64,16,128]{2,1,0:T(8,128)(2,1)S(1)}, u32[]{:S(2)}, u32[]{:S(2)}) collective-permute-start(bf16[64,16,128]{2,1,0:T(8,128)(2,1)S(1)} %divide_convert_fusion), channel_id=1, source_target_pairs={{0,4},{4,8},{8,12},{1,5},{5,9},{9,13},{2,6},{6,10},{10,14},{3,7},{... | collective-permute-start | bytes 786440 | tf_op jit(solution)/shard_map/ppermute | solution.py:16
  207.0 10.0 %collective-permute-start.3 = (bf16[64,16,128]{2,1,0:T(8,128)(2,1)S(1)}, bf16[64,16,128]{2,1,0:T(8,128)(2,1)S(1)}, u32[]{:S(2)}, u32[]{:S(2)}) collective-permute-start(bf16[64,16,128]{2,1,0:T(8,128)(2,1)S(1)} %divide_convert_fusion), channel_id=1, source_target_pairs={{4,0},{8,4},{12,8},{5,1},{9,5},{13,9},{6,2},{10,6},{14,10},{7,3},{... | collective-permute-start | bytes 786440 | tf_op jit(solution)/shard_map/ppermute | solution.py:17
  220.9 72.3 %copy-start.1 = (f32[64,16,128]{2,1,0:T(8,128)S(1)}, f32[64,16,128]{2,1,0:T(8,128)}, u32[]{:S(2)}) copy-start(f32[64,16,128]{2,1,0:T(8,128)} %all-reduce.2.cloned.1.call-done) | copy-start | bytes 1572868
  286.8 0.8 copy-start.4
Sparse Core Ops, SparseCore 0:
  116.9 18.3 all-reduce.1
  287.7 5.4 reduce-scatter.1
where the time goes:
time: 339 us; the launch traced here: 338 us
  blocking collectives  123 us (36%)
  matrix products  95.5 us (28%)
  local copies, waits for them, and re-layouts  50.9 us (15%)
  waiting for transfers between devices  32.6 us (10%)
  between operations  17 us (5%)
  other arithmetic  12.5 us (4%)
  starting transfers between devices  6.14 us (2%)
    dot_general x26, matrix products, add_pair(): jnp.einsum('vasb,vbc->asc', mixed_rows, env_pair, preferred_element_type=...  88.8 us
    dynamic_slice x52, local copies, waits for them, and re-layouts, add_pair(): weights_pair = lax.dynamic_slice_in_dim(coupling, pair_index * 2, 2, 2)  42 us
    psum x1, blocking collectives, per_device(): lax.psum(jnp.sum(basis_two_mine.astype(jnp.float32) * image_two), ('brow'...  34.5 us
    psum x1, blocking collectives, per_device(): lax.psum(jnp.sum(first_basis * image_mine), ('brow', 'bcol', 'mpo'))  34.5 us
    psum x1, blocking collectives, per_device(): lax.psum(jnp.sum(residual_mine * residual_mine), ('brow', 'bcol', 'mpo'))  30.1 us
    psum x1, blocking collectives, per_device(): square_sum = lax.psum(jnp.sum(wide * wide), ('brow', 'bcol'))  23.7 us
    psum x1, waiting for transfers between devices, per_device(): image_whole = lax.psum(partial_one, 'mpo')  18.5 us
    unnamed x18, local copies, waits for them, and re-layouts  7.26 us
  transfers between devices with their start and end apart: 6, of which 4 were waited for; matrix products, arithmetic and copies ran while one was open for 2% of the time, Pallas kernels for 0%

commit v1 on v0

v1 whole, which is shorter than its diff:
```python
import functools

import jax
import jax.numpy as jnp
from jax import lax
from jax.experimental import pallas as pl
from jax.experimental.pallas import tpu as pltpu
from jax.sharding import PartitionSpec as P

EPSILON = 1e-06
SHRINK = 2.0**-12
SLOT = 32
VMEM_LIMIT = 48 * 2**20
ANY = pl.BlockSpec(memory_space=pl.ANY)


def swap_cores(x):
    return lax.ppermute(x, "mpo", [(0, 1), (1, 0)])


def swap_blocks(x):
    blocks = lax.axis_size("brow")
    pairs = []
    for i in range(blocks):
        for core, partner in ((0, i ^ 1), (1, i + 1 if i % 2 else i - 1)):
            if 0 <= partner < blocks:
                pairs.append((2 * i + core, 2 * partner + core))
    return lax.ppermute(x, ("brow", "mpo"), pairs)


def halo_places(rows):
    even = lax.rem(lax.axis_index("brow") + lax.axis_index("mpo"), 2) == 0
    direct = jnp.where(even, 2 * rows, 0)
    return pl.multiple_of(direct, rows), pl.multiple_of(2 * rows - direct, rows)


def apply_steps(env, coupling, right, extended, contracted, mixed, image, waits):
    pairs, depth, width = contracted.shape
    lanes = width // 2
    states = depth // SLOT
    bonds = mixed.shape[1] // lanes

    @pl.loop(0, states // 2)
    def _(step):
        columns = pl.ds(pl.multiple_of(step * width, width), width)
        product = jnp.dot(env[...], extended[:, columns], preferred_element_type=jnp.float32)
        product = product.astype(jnp.bfloat16)
        for row in range(2 * pairs):
            for part in range(2):
                place = pl.ds(pl.multiple_of((2 * step + part) * SLOT, SLOT), SLOT)
                contracted[row // 2, place, row % 2 * lanes : (row % 2 + 1) * lanes] = product[
                    row * SLOT : (row + 1) * SLOT, part * lanes : (part + 1) * lanes
                ]

    waits[0]()

    @pl.loop(0, pairs)
    def _(pair):
        product = jnp.dot(coupling[...], contracted[pair], preferred_element_type=jnp.float32)
        product = product.astype(jnp.bfloat16)
        for part in range(2):
            place = pl.ds(pl.multiple_of((2 * pair + part) * states, states), states)
            for bond in range(bonds):
                mixed[place, bond * lanes : (bond + 1) * lanes] = product[
                    bond * states : (bond + 1) * states, part * lanes : (part + 1) * lanes
                ]

    waits[1]()
    chunk = 128

    @pl.loop(0, image.shape[0] // chunk)
    def _(step):
        place = pl.ds(pl.multiple_of(step * chunk, chunk), chunk)
        image[place, :] = SHRINK * jnp.dot(
            mixed[place, :], right[...], preferred_element_type=jnp.float32
        )


def fetch(pairs, sems):
    copies = [pltpu.make_async_copy(s, d, sems.at[i]) for i, (s, d) in enumerate(pairs)]
    for copy in copies:
        copy.start()
    return copies


def column_sum(x):
    return jnp.sum(x, axis=0, keepdims=True)


def first_kernel(
    env_in, coupling_in, right_in, own_in, direct_in, passed_in,
    image, image_rows, sums,
    env, coupling, right, raw, wide, extended, contracted, mixed, sems,
):
    rows = raw.shape[0] // 3
    states = rows // (extended.shape[0] // 3)
    bond_rows = rows // states
    half = image.shape[0]
    direct, passed = halo_places(bond_rows)
    copies = fetch(
        [
            (own_in, raw.at[pl.ds(rows, rows), :]),
            (direct_in, raw.at[pl.ds(pl.multiple_of(direct * states, rows), rows), :]),
            (passed_in, raw.at[pl.ds(pl.multiple_of(passed * states, rows), rows), :]),
            (env_in, env),
            (coupling_in, coupling),
            (right_in, right),
        ],
        sems,
    )
    for copy in copies[:3]:
        copy.wait()
    lanes = raw.shape[1]
    wide[...] = raw[...].astype(jnp.float32)
    for state in range(states):
        extended[:, state * lanes : (state + 1) * lanes] = wide[
            pl.ds(state, 3 * bond_rows, stride=states), :
        ].astype(jnp.bfloat16)
    copies[3].wait()
    apply_steps(
        env, coupling, right, extended, contracted, mixed, image, (copies[4].wait, copies[5].wait)
    )
    for state in range(states):
        image_rows[:, state * lanes : (state + 1) * lanes] = image[
            pl.ds(state, half // states, stride=states), :
        ].astype(jnp.bfloat16)
    start = pl.multiple_of(rows + lax.axis_index("mpo") * half, half)
    own = wide[pl.ds(start, half), :]
    out = image[...]
    sums[...] = jnp.concatenate(
        [column_sum(own * own), column_sum(own * out), column_sum(out * out)]
        + [jnp.zeros((5, lanes), jnp.float32)],
        axis=0,
    )


def second_kernel(
    env_in, coupling_in, right_in, mine_in, other_in, direct_in, passed_in, first_in, vector_in, sums_in,
    image, sums,
    env, coupling, right, extended, first, vector, contracted, mixed, sems,
):
    bond_rows = extended.shape[0] // 3
    part = bond_rows // 2
    core = lax.axis_index("mpo")
    direct, passed = halo_places(bond_rows)
    mine = pl.multiple_of(bond_rows + core * part, part)
    other = pl.multiple_of(bond_rows + (1 - core) * part, part)
    copies = fetch(
        [
            (mine_in, extended.at[pl.ds(mine, part), :]),
            (other_in, extended.at[pl.ds(other, part), :]),
            (direct_in, extended.at[pl.ds(direct, bond_rows), :]),
            (passed_in, extended.at[pl.ds(passed, bond_rows), :]),
            (env_in, env),
            (coupling_in, coupling),
            (right_in, right),
            (first_in, first),
            (vector_in.at[pl.ds(pl.multiple_of(core * vector.shape[0], vector.shape[0]), vector.shape[0]), :], vector),
        ],
        sems,
    )
    for copy in copies[:5]:
        copy.wait()
    apply_steps(
        env, coupling, right, extended, contracted, mixed, image, (copies[5].wait, copies[6].wait)
    )
    for copy in copies[7:]:
        copy.wait()
    out = image[...]
    lanes = out.shape[1]
    sums[...] = sums_in[...] + jnp.concatenate(
        [jnp.zeros((3, lanes), jnp.float32)]
        + [column_sum(vector[...].astype(jnp.float32) * out), column_sum(first[...] * out)]
        + [jnp.zeros((3, lanes), jnp.float32)],
        axis=0,
    )


def per_device(amplitudes, left_env, right_env, mpo_left, mpo_right, sector_table):
    rows, states, columns = amplitudes.shape
    share, _, band = left_env.shape
    bonds = mpo_left.shape[0]
    half = rows // 2
    half_states = states // 2
    block = lax.axis_index("brow")
    core = lax.axis_index("mpo")
    entries = float(rows * lax.axis_size("brow") * states * columns * lax.axis_size("bcol"))
    flat = amplitudes.reshape(rows * states, columns)

    direct_one = swap_blocks(flat)
    env_there = swap_cores(lax.dynamic_slice_in_dim(left_env, (1 - core) * half, half, 1))
    passed_one = swap_cores(direct_one)

    outside = jnp.full((rows,), -1, dtype=jnp.int32)
    padded = jnp.concatenate([outside, sector_table, outside])
    own_labels = lax.dynamic_slice_in_dim(padded, (block + 1) * rows + core * half, half, 0)
    partner = lax.dynamic_slice_in_dim(padded, block * rows, 3 * rows, 0)
    band_mask = own_labels[:, None] == partner[None, :]
    env_here = lax.dynamic_slice_in_dim(left_env, core * half, half, 1)
    spare = ((0, 0), (0, SLOT // 2 - share), (0, 0))
    env = jnp.concatenate(
        [jnp.pad(jnp.transpose(e, (1, 0, 2)), spare) for e in (env_here, env_there)], axis=1
    )
    env = jnp.where(band_mask[:, None, :], env, jnp.zeros((), env.dtype))
    env = env.reshape(half * SLOT, band)

    def share_of(index):
        piece = lax.dynamic_slice_in_dim(mpo_left, index * share, share, 0)
        return jnp.pad(piece, ((0, SLOT // 2 - share), (0, 0), (0, 0), (0, 0)))

    ordered = jnp.concatenate([share_of(core), share_of(1 - core)], axis=0)
    coupling = jnp.einsum("wmik,mvjl->vijklw", ordered, mpo_right, precision=lax.Precision.HIGHEST)
    coupling = coupling.reshape(bonds * states, states * SLOT).astype(jnp.bfloat16)
    right = right_env.reshape(bonds * columns, columns)

    scratch = [
        pltpu.VMEM((half // 2, states * SLOT, 2 * columns), jnp.bfloat16),
        pltpu.VMEM((half * states, bonds * columns), jnp.bfloat16),
    ]
    held = [
        pltpu.VMEM(env.shape, jnp.bfloat16),
        pltpu.VMEM(coupling.shape, jnp.bfloat16),
        pltpu.VMEM(right.shape, jnp.bfloat16),
    ]
    extended = pltpu.VMEM((3 * rows, states * columns), jnp.bfloat16)
    image_shape = jax.ShapeDtypeStruct((half * states, columns), jnp.float32)
    sums_shape = jax.ShapeDtypeStruct((8, columns), jnp.float32)
    params = pltpu.CompilerParams(vmem_limit_bytes=VMEM_LIMIT)
    whole = pl.BlockSpec(memory_space=pltpu.VMEM)

    first, first_rows, sums = pl.pallas_call(
        first_kernel,
        out_shape=(
            image_shape,
            jax.ShapeDtypeStruct((half, states * columns), jnp.bfloat16),
            sums_shape,
        ),
        in_specs=[ANY] * 6,
        out_specs=(whole,) * 3,
        scratch_shapes=held
        + [
            pltpu.VMEM((3 * rows * states, columns), jnp.bfloat16),
            pltpu.VMEM((3 * rows * states, columns), jnp.float32),
            extended,
        ]
        + scratch
        + [pltpu.SemaphoreType.DMA((6,))],
        compiler_params=params,
        name="first_image",
    )(env, coupling, right, flat, direct_one, passed_one)

    other_rows = swap_cores(first_rows)
    mine_first = core == 0
    block_rows = jnp.concatenate(
        [jnp.where(mine_first, first_rows, other_rows), jnp.where(mine_first, other_rows, first_rows)],
        axis=0,
    )
    direct_two = swap_blocks(block_rows)
    passed_two = swap_cores(direct_two)

    second, sums = pl.pallas_call(
        second_kernel,
        out_shape=(image_shape, sums_shape),
        in_specs=[ANY] * 9 + [whole],
        out_specs=(whole,) * 2,
        scratch_shapes=held
        + [
            extended,
            pltpu.VMEM(image_shape.shape, jnp.float32),
            pltpu.VMEM(image_shape.shape, jnp.bfloat16),
        ]
        + scratch
        + [pltpu.SemaphoreType.DMA((9,))],
        compiler_params=params,
        name="second_image",
    )(env, coupling, right, first_rows, other_rows, direct_two, passed_two, first, flat, sums)

    sums = sums + swap_cores(sums)
    for axis in ("bcol", "brow"):
        size, step = lax.axis_size(axis), 1
        while step < size:
            sums = sums + lax.ppermute(sums, axis, [(i, i ^ step) for i in range(size)])
            step *= 2

    def whole_half(image):
        pieces = image.reshape(half, states, columns)
        kept = lax.dynamic_slice_in_dim(pieces, core * half_states, half_states, 1)
        sent = lax.dynamic_slice_in_dim(pieces, (1 - core) * half_states, half_states, 1)
        got = swap_cores(sent)
        return jnp.concatenate(
            [jnp.where(mine_first, kept, got), jnp.where(mine_first, got, kept)], axis=0
        )

    first_half = whole_half(first)
    second_half = whole_half(second)
    vector_half = lax.dynamic_slice_in_dim(amplitudes, core * half_states, half_states, 1)

    totals = jnp.sum(sums, axis=1)
    s_aa, s_ay, s_yy, s_az, s_yz = (totals[i] for i in range(5))
    scale_sq = s_aa / entries + EPSILON
    shrunk = s_ay / entries / scale_sq
    residual_sq = jnp.maximum(s_yy - 2.0 * shrunk * s_ay + shrunk * shrunk * s_aa, 0.0)
    grow = 1.0 / SHRINK
    residual_norm = jnp.sqrt(residual_sq / scale_sq / entries * (grow * grow) + EPSILON)
    correlation = shrunk * grow
    factor = grow / (jnp.sqrt(scale_sq) * residual_norm)
    basis_two = (first_half - shrunk * vector_half.astype(jnp.float32)) * factor
    image_two = (second_half - shrunk * first_half) * (factor * grow)
    final = (s_yz - shrunk * s_yy - shrunk * s_az + shrunk * shrunk * s_ay) / entries
    final_correlation = final * factor * factor * grow
    projected = jnp.stack(
        [jnp.stack([correlation, residual_norm]), jnp.stack([residual_norm, final_correlation])]
    )
    return (image_two.astype(jnp.bfloat16), basis_two.astype(jnp.bfloat16), projected)


def solution(mesh):
    return jax.shard_map(
        per_device,
        mesh=mesh,
        in_specs=(
            P(("groups", "brow"), None, "bcol"),
            P(("groups", "mpo"), "brow", None),
            P("groups", "bcol", None),
            P(),
            P(),
            P("groups"),
        ),
        out_specs=(
            P(("groups", "brow"), "mpo", "bcol"),
            P(("groups", "brow"), "mpo", "bcol"),
            P("groups", None),
        ),
        check_vma=False,
    )
```

time: 339 us -> 75.8 us (0.22)
  blocking collectives: 123 us -> 0 us
  matrix products: 95.5 us -> 3.67 us
  local copies, waits for them, and re-layouts: 50.9 us -> 13.1 us
  waiting for transfers between devices: 32.6 us -> 11.1 us
  Pallas kernels: 0 us -> 19.8 us
  between operations: 17 us -> 6.77 us
  starting transfers between devices: 6.14 us -> 15.6 us
  other arithmetic: 12.5 us -> 5.33 us
    psum x4 -> x0, blocking collectives: 123 us -> none  [the longest x1 34.5 us: per_device(): lax.psum(jnp.sum(basis_two_mine.astype(jnp.float32) * image_two), ('brow'...]
    dot_general x29 -> x1, matrix products: 95.5 us -> 3.67 us  [per_device(): jnp.einsum('wmik,mvjl->vijklw', ordered, mpo_right, precision=lax.Precisi...]
    dynamic_slice x55 -> x5, local copies, waits for them, and re-layouts: 42.3 us -> 2.69 us  [the longest x2 1.58 us: whole_half(): lax.dynamic_slice_in_dim(pieces, (1 - core) * half_states, half_states, 1)]
    pallas_call x0 -> x2, Pallas kernels: none -> 19.8 us  [the longest x1 10.1 us: per_device(): pl.pallas_call(first_kernel, out_shape=(image_shape, jax.ShapeDtypeStruct...]
    psum x1 -> x0, waiting for transfers between devices: 18.5 us -> none  [per_device(): image_whole = lax.psum(partial_one, 'mpo')]
    ppermute x4 -> x12, starting transfers between devices: 6.06 us -> 15.6 us  [the longest x2 8.04 us: swap_blocks(): return lax.ppermute(x, ('brow', 'mpo'), pairs)]
    reduce_sum x4 -> x1, other arithmetic: 7.39 us -> 0.11 us  [per_device(): totals = jnp.sum(sums, axis=1)]
    unnamed x18 -> x10, local copies, waits for them, and re-layouts: 7.26 us -> 0.79 us
  transfers between devices with their start and end apart: 6 -> 12, of which waited for: 4 -> 7; matrix products, arithmetic and copies ran while one was open for 2% -> 24% of each run, Pallas kernels for 0% -> 13%
where the time goes in v1:
time: 75.8 us; the launch traced here: 75.3 us
  Pallas kernels  19.8 us (26%)
  starting transfers between devices  15.6 us (21%)
  local copies, waits for them, and re-layouts  13.1 us (17%)
  waiting for transfers between devices  11.1 us (15%)
  between operations  6.77 us (9%)
  other arithmetic  5.33 us (7%)
  matrix products  3.67 us (5%)
    pallas_call x1, Pallas kernels, per_device(): pl.pallas_call(first_kernel, out_shape=(image_shape, jax.ShapeDtypeStruct...  10.1 us
    pallas_call x1, Pallas kernels, per_device(): pl.pallas_call(second_kernel, out_shape=(image_shape, sums_shape), in_spe...  9.73 us
    ppermute x2, starting transfers between devices, swap_blocks(): return lax.ppermute(x, ('brow', 'mpo'), pairs)  8.04 us
    convert_element_type x2, local copies, waits for them, and re-layouts, per_device(): coupling.reshape(bonds * states, states * SLOT).astype(jnp.bfloat16)  6.82 us
    ppermute x3, starting transfers between devices, per_device(): sums = sums + lax.ppermute(sums, axis, [(i, i ^ step) for i in range(size)])  5.72 us
    ppermute x2, waiting for transfers between devices, swap_blocks(): return lax.ppermute(x, ('brow', 'mpo'), pairs)  4.7 us
    ppermute x3, waiting for transfers between devices, per_device(): sums = sums + lax.ppermute(sums, axis, [(i, i ^ step) for i in range(size)])  4.07 us
    dot_general x1, matrix products, per_device(): jnp.einsum('wmik,mvjl->vijklw', ordered, mpo_right, precision=lax.Precisi...  3.67 us
  transfers between devices with their start and end apart: 12, of which 7 were waited for; matrix products, arithmetic and copies ran while one was open for 24% of the time, Pallas kernels for 13%

profile of v1, /device:TPU:0, one launch (start us, length us, event | category | flops | bytes accessed | tf_op | source)
XLA Modules:
  0.0 75.3 jit_solution(18424126006689888623)
XLA Ops:
  0.6 0.0 copy-start
  0.7 1.8 %dynamic-slice_bitcast_fusion = (bf16[32,13,192]{2,0,1:T(8,128)(2,1)S(1)}, bf16[13,32,192]{2,1,0:T(8,128)(2,1)}) fusion(bf16[13,64,192]{2,1,0:T(8,128)(2,1)} %param.7, s32[]{:T(128)S(6)} %select_n.70, s32[]{:T(128)S(6)} %select_n.71), kind=kLoop, calls=%fused_computation.21 | loop fusion | bytes 638984 | tf_op jit(solution)/shard_map/transpose | solution.py:202
  2.5 0.5 collective-permute-start
  2.9 4.5 %collective-permute-start.1 = (bf16[1024,128]{1,0:T(8,128)(2,1)}, bf16[1024,128]{1,0:T(8,128)(2,1)S(1)}, u32[]{:S(2)}, u32[]{:S(2)}) collective-permute-start(bf16[1024,128]{1,0:T(8,128)(2,1)} %bitcast.33), channel_id=1, source_target_pairs={{0,4},{4,0},{5,9},{8,12},{9,5},{12,8},{2,6},{6,2},{7,11},{10,14},{... | collective-permute-start | bytes 786440 | tf_op jit(solution)/shard_map/ppermute | solution.py:28
  7.4 0.8 %pad_add_fusion = s32[384]{0:T(512)S(1)} fusion(s32[64]{0:T(128)S(1)} %broadcast_in_dim.18, s32[256]{0:T(256)} %param.11), kind=kLoop, calls=%fused_computation.37 | loop fusion | flops 768 | bytes 2816 | tf_op jit(solution)/shard_map/concatenate | solution.py:195
  8.2 0.1 dynamic_slice.33
  8.3 0.1 dynamic_slice.34
  8.3 1.0 %constant_dynamic-slice_fusion.3 = (f32[13,26,4,4]{1,3,2,0:T(4,128)S(1)}, f32[13,26,4,4]{1,3,2,0:T(4,128)S(1)}) fusion(f32[26,26,4,4]{1,3,2,0:T(4,128)} %param.9, s32[]{:T(128)S(6)} %select_n.74, s32[]{:T(128)S(6)} %select_n.75), kind=kLoop, calls=%fused_computation.35 | loop fusion | bytes 86536 | tf_op jit(solution)/shard_map/dynamic_slice | solution.py:208
  9.4 0.0 copy-done
  9.4 3.7 %convert_bitcast_fusion = bf16[26,4,4,4,4,32]{0,5,4,2,3,1:T(8,128)(2,1)S(1)} fusion(f32[13,26,4,4]{1,0,3,2:T(8,128)S(1)} %copy.19, f32[13,26,4,4]{1,0,3,2:T(8,128)S(1)} %copy.18, f32[26,26,4,4,1,1]{1,3,2,0,5,4:T(4,128)S(1)} %bitcast.28), kind=kOutput, calls=%fused_computation | convolution fusion | flops 66733056 | bytes 512512 | tf_op jit(solution)/shard_map/wmik,mvjl->vijklw/dot_general | solution.py:212
  13.1 0.0 collective-permute-done.1.direct_in
  13.1 0.1 collective-permute-start.2
  13.2 0.1 broadcast_compare_fusion
  13.2 4.0 %copy.13 = bf16[26,4,4,4,4,32]{5,4,3,2,1,0:T(4,128)(2,1)} copy(bf16[26,4,4,4,4,32]{0,5,4,2,3,1:T(8,128)(2,1)S(1)} %convert_bitcast_fusion) | data formatting | bytes 851968 | tf_op jit(solution)/shard_map/convert_element_type | solution.py:213
  17.3 0.0 copy-start.1
  17.3 0.0 copy-start.2
  17.3 2.8 %convert_element_type.24.coupling_in = bf16[416,512]{1,0:T(8,128)(2,1)S(1)} reshape(bf16[26,4,4,4,4,32]{5,4,3,2,1,0:T(4,128)(2,1)} %copy.13) | data formatting | bytes 851968 | tf_op jit(solution)/shard_map/convert_element_type | solution.py:213
  20.1 0.0 collective-permute-done
  20.1 1.0 %fusion.3 = bf16[32,32,192]{2,0,1:T(8,128)(2,1)S(1)} fusion(bf16[32,13,192]{2,0,1:T(8,128)(2,1)} %bitcast.1, bf16[32,13,192]{2,0,1:T(8,128)(2,1)S(1)} %get-tuple-element.13, pred[32,192]{1,0:T(8,128)(4,1)S(1)} %broadcast_compare_fusion), kind=kLoop, calls=%fused_computation.6 | loop fusion | flops 1769472 | bytes 718848 | tf_op jit(solution)/shard_map/jit(_where)/select_n | solution.py:204
  21.1 0.3 copy.9
  21.4 0.0 collective-permute-done.2.passed_in
  21.4 0.0 copy-done.1
  21.4 0.0 copy-done.2
  21.5 10.1 %first_image.1 = (f32[512,128]{1,0:T(8,128)S(1)}, bf16[32,2048]{1,0:T(8,128)(2,1)S(1)}, f32[8,128]{1,0:T(8,128)S(1)}) custom-call(bf16[1024,192]{1,0:T(8,128)(2,1)S(1)} %bitcast.29, bf16[416,512]{1,0:T(8,128)(2,1)S(1)} %convert_element_type.24.coupling_in, bf16[3328,128]{1,0:T(8,128)(2,1)S(1)} %bitcast.31, bf16[1024,128]{1,0:T(8,128)(2,1)S(1)} %bitcast.34, ...), custom_call_target="tpu_custom_call" | custom-call | tf_op jit(solution)/shard_map/first_image/pallas_call | solution.py:231
  31.6 0.6 collective-permute-start.3
  32.1 1.0 %collective-permute-done.3.other_in = bf16[32,2048]{1,0:T(8,128)(2,1)S(1)} collective-permute-done((bf16[32,2048]{1,0:T(8,128)(2,1)S(1)}, bf16[32,2048]{1,0:T(8,128)(2,1)S(1)}, u32[]{:S(2)}, u32[]{:S(2)}) %collective-permute-start.3) | collective-permute-done | bytes 131104 | tf_op jit(solution)/shard_map/ppermute | solution.py:18
  33.1 3.6 %collective-permute-start.4 = (bf16[64,2048]{1,0:T(8,128)(2,1)S(1)}, bf16[64,2048]{1,0:T(8,128)(2,1)S(1)}, u32[]{:S(2)}, u32[]{:S(2)}) collective-permute-start(bf16[64,2048]{1,0:T(8,128)(2,1)S(1)} %pad_maximum_fusion), channel_id=1, source_target_pairs={{0,4},{4,0},{5,9},{8,12},{9,5},{12,8},{2,6},{6,2},{7,11},{10,14},{... | collective-permute-start | bytes 786440 | tf_op jit(solution)/shard_map/ppermute | solution.py:28
  36.7 4.7 %collective-permute-done.4.direct_in = bf16[64,2048]{1,0:T(8,128)(2,1)S(1)} collective-permute-done((bf16[64,2048]{1,0:T(8,128)(2,1)S(1)}, bf16[64,2048]{1,0:T(8,128)(2,1)S(1)}, u32[]{:S(2)}, u32[]{:S(2)}) %collective-permute-start.4) | collective-permute-done | bytes 262176 | tf_op jit(solution)/shard_map/ppermute | solution.py:28
  41.4 0.0 collective-permute-start.5
  41.4 0.7 constant_dynamic-slice_fusion
  42.1 0.5 collective-permute-start.11
  42.6 0.4 collective-permute-done.5.passed_in
  42.9 9.7 %second_image.1 = (f32[512,128]{1,0:T(8,128)S(1)}, f32[8,128]{1,0:T(8,128)S(1)}) custom-call(bf16[1024,192]{1,0:T(8,128)(2,1)S(1)} %bitcast.30, bf16[416,512]{1,0:T(8,128)(2,1)S(1)} %convert_element_type.24.coupling_in, bf16[3328,128]{1,0:T(8,128)(2,1)S(1)} %bitcast.32, bf16[32,2048]{1,0:T(8,128)(2,1)S(1)} %get-tuple-element.8.mine_in, ...), custom_call_target="tpu_custom_call" | custom-call | tf_op jit(solution)/shard_map/second_image/pallas_call | solution.py:261
  52.7 0.0 copy-start.3
  52.7 0.7 copy-done.3
  53.4 0.1 collective-permute-start.7
  53.5 1.0 %collective-permute-done.7 = f32[8,128]{1,0:T(8,128)S(1)} collective-permute-done((f32[8,128]{1,0:T(8,128)S(1)}, f32[8,128]{1,0:T(8,128)S(1)}, u32[]{:S(2)}, u32[]{:S(2)}) %collective-permute-start.7) | collective-permute-done | bytes 4128 | tf_op jit(solution)/shard_map/ppermute | solution.py:18
  54.6 1.5 %collective-permute-start.8 = (f32[8,128]{1,0:T(8,128)S(1)}, f32[8,128]{1,0:T(8,128)S(1)}, u32[]{:S(2)}, u32[]{:S(2)}) collective-permute-start(f32[8,128]{1,0:T(8,128)S(1)} %add.75), channel_id=1, source_target_pairs={{0,2},{2,0},{1,3},{3,1},{4,6},{6,4},{5,7},{7,5},{8,10},{10,8},{9,1... | collective-permute-start | bytes 12296 | tf_op jit(solution)/shard_map/ppermute | solution.py:282
  56.1 2.1 %collective-permute-done.8 = f32[8,128]{1,0:T(8,128)S(1)} collective-permute-done((f32[8,128]{1,0:T(8,128)S(1)}, f32[8,128]{1,0:T(8,128)S(1)}, u32[]{:S(2)}, u32[]{:S(2)}) %collective-permute-start.8) | collective-permute-done | bytes 4128 | tf_op jit(solution)/shard_map/ppermute | solution.py:282
  58.2 1.7 %collective-permute-start.9 = (f32[8,128]{1,0:T(8,128)S(1)}, f32[8,128]{1,0:T(8,128)S(1)}, u32[]{:S(2)}, u32[]{:S(2)}) collective-permute-start(f32[8,128]{1,0:T(8,128)S(1)} %add.76), channel_id=1, source_target_pairs={{0,4},{4,0},{8,12},{12,8},{1,5},{5,1},{9,13},{13,9},{2,6},{6,2},{1... | collective-permute-start | bytes 12296 | tf_op jit(solution)/shard_map/ppermute | solution.py:282
  59.8 0.0 collective-permute-done.11
  59.8 0.9 %dynamic-slice_select_fusion.1 = (f32[32,8,128]{2,1,0:T(8,128)S(1)}, f32[32,8,128]{2,1,0:T(8,128)S(1)}) fusion(f32[32,8,128]{2,1,0:T(8,128)} %collective-permute-done.11, f32[32,16,128]{2,1,0:T(8,128)S(1)} %bitcast.37, s32[]{:T(128)S(6)} %select_n.79, pred[]{:T(512)S(6)} %eq.20), kind=kLoop, calls=%fused_computation.27 | loop fusion | flops 65536 | bytes 524293 | tf_op jit(solution)/shard_map/jit(_where)/select_n | solution.py:291
  60.8 1.0 %collective-permute-done.9 = f32[8,128]{1,0:T(8,128)S(1)} collective-permute-done((f32[8,128]{1,0:T(8,128)S(1)}, f32[8,128]{1,0:T(8,128)S(1)}, u32[]{:S(2)}, u32[]{:S(2)}) %collective-permute-start.9) | collective-permute-done | bytes 4128 | tf_op jit(solution)/shard_map/ppermute | solution.py:282
  61.8 2.6 %collective-permute-start.10 = (f32[8,128]{1,0:T(8,128)S(1)}, f32[8,128]{1,0:T(8,128)S(1)}, u32[]{:S(2)}, u32[]{:S(2)}) collective-permute-start(f32[8,128]{1,0:T(8,128)S(1)} %add.77), channel_id=1, source_target_pairs={{0,8},{4,12},{8,0},{12,4},{1,9},{5,13},{9,1},{13,5},{2,10},{6,14},... | collective-permute-start | bytes 12296 | tf_op jit(solution)/shard_map/ppermute | solution.py:282
  64.4 0.9 %constant_dynamic-slice_fusion.1 = f32[32,8,128]{2,1,0:T(8,128)S(1)} fusion(f32[32,16,128]{2,1,0:T(8,128)} %bitcast.38, s32[]{:T(128)S(6)} %select_n.80), kind=kLoop, calls=%fused_computation.33 | loop fusion | bytes 262148 | tf_op jit(solution)/shard_map/dynamic_slice | solution.py:288
  65.3 0.1 collective-permute-start.6
  65.3 0.9 %collective-permute-done.10 = f32[8,128]{1,0:T(8,128)S(1)} collective-permute-done((f32[8,128]{1,0:T(8,128)S(1)}, f32[8,128]{1,0:T(8,128)S(1)}, u32[]{:S(2)}, u32[]{:S(2)}) %collective-permute-start.10) | collective-permute-done | bytes 4128 | tf_op jit(solution)/shard_map/ppermute | solution.py:282
  66.3 0.1 add_reduce_fusion
  66.4 0.7 fusion.17
  73.0 0.1 maximum_bitcast_fusion
  73.0 0.6 pad_maximum_fusion.2
  73.6 0.0 collective-permute-done.6
  73.6 0.9 %dynamic-slice_select_fusion.3 = (f32[32,8,128]{2,1,0:T(8,128)S(1)}, f32[32,8,128]{2,1,0:T(8,128)S(1)}) fusion(f32[32,8,128]{2,1,0:T(8,128)S(1)} %collective-permute-done.6, f32[32,16,128]{2,1,0:T(8,128)} %bitcast.39, s32[]{:T(128)S(6)} %select_n.79, pred[]{:T(512)S(6)} %eq.20), kind=kLoop, calls=%fused_computation.29 | loop fusion | flops 65536 | bytes 524293 | tf_op jit(solution)/shard_map/jit(_where)/select_n | solution.py:291
  74.6 0.8 %multiply_convert_fusion = (bf16[64,8,128]{2,1,0:T(8,128)(2,1)}, bf16[64,8,128]{2,1,0:T(8,128)(2,1)}) fusion(f32[32,8,128]{2,1,0:T(8,128)S(1)} %get-tuple-element.16, f32[32,8,128]{2,1,0:T(8,128)S(1)} %get-tuple-element.15, f32[]{:T(128)S(6)} %div.23, bf16[64,16,128]{2,1,0:T(8,128)(2,1)S(1)} %copy-done.2, s32[]{:T(128)S(6)} %select_n.79, f32[]{:T(128)S(6)} %div.21, ...), kind=kLoop, calls=%fused_computation.20 | loop fusion | flops 720896 | bytes 917520 | tf_op jit(solution)/shard_map/convert_element_type | solution.py:314
  (8 shorter events, 0.1 us)
Async XLA Ops:
  0.6 8.8 %copy-start = (f32[26,26,4,4]{1,3,2,0:T(4,128)S(1)}, f32[26,26,4,4]{1,3,2,0:T(4,128)}, u32[]{:S(2)}) copy-start(f32[26,26,4,4]{1,3,2,0:T(4,128)} %param.10) | copy-start | bytes 129796
  2.5 17.6 %collective-permute-start = (bf16[13,32,192]{2,1,0:T(8,128)(2,1)}, bf16[13,32,192]{2,1,0:T(8,128)(2,1)}, u32[]{:S(2)}, u32[]{:S(2)}) collective-permute-start(bf16[13,32,192]{2,1,0:T(8,128)(2,1)} %get-tuple-element.14), channel_id=1, source_target_pairs={{0,1},{1,0},{2,3},{3,2},{4,5},{5,4},{6,7},{7,6},{8,9},{9,8},{10,11... | collective-permute-start | bytes 479240 | tf_op jit(solution)/shard_map/ppermute | solution.py:18
  2.9 10.2 %collective-permute-start.1 = (bf16[1024,128]{1,0:T(8,128)(2,1)}, bf16[1024,128]{1,0:T(8,128)(2,1)S(1)}, u32[]{:S(2)}, u32[]{:S(2)}) collective-permute-start(bf16[1024,128]{1,0:T(8,128)(2,1)} %bitcast.33), channel_id=1, source_target_pairs={{0,4},{4,0},{5,9},{8,12},{9,5},{12,8},{2,6},{6,2},{7,11},{10,14},{... | collective-permute-start | bytes 786440 | tf_op jit(solution)/shard_map/ppermute | solution.py:28
  13.1 8.3 %collective-permute-start.2 = (bf16[1024,128]{1,0:T(8,128)(2,1)S(1)}, bf16[1024,128]{1,0:T(8,128)(2,1)S(1)}, u32[]{:S(2)}, u32[]{:S(2)}) collective-permute-start(bf16[1024,128]{1,0:T(8,128)(2,1)S(1)} %collective-permute-done.1.direct_in), channel_id=1, source_target_pairs={{0,1},{1,0},{2,3},{3,2},{4,5},{5,4},{6,7},{7,6},{8,9},{9,8},{10,11... | collective-permute-start | bytes 786440 | tf_op jit(solution)/shard_map/ppermute | solution.py:18
  17.3 4.2 %copy-start.1 = (bf16[26,128,128]{2,1,0:T(8,128)(2,1)S(1)}, bf16[26,128,128]{2,1,0:T(8,128)(2,1)}, u32[]{:S(2)}) copy-start(bf16[26,128,128]{2,1,0:T(8,128)(2,1)} %param.8) | copy-start | bytes 2555908
  17.3 4.2 %copy-start.2 = (bf16[64,16,128]{2,1,0:T(8,128)(2,1)S(1)}, bf16[64,16,128]{2,1,0:T(8,128)(2,1)}, u32[]{:S(2)}) copy-start(bf16[64,16,128]{2,1,0:T(8,128)(2,1)} %param.6) | copy-start | bytes 786436
  31.6 1.5 %collective-permute-start.3 = (bf16[32,2048]{1,0:T(8,128)(2,1)S(1)}, bf16[32,2048]{1,0:T(8,128)(2,1)S(1)}, u32[]{:S(2)}, u32[]{:S(2)}) collective-permute-start(bf16[32,2048]{1,0:T(8,128)(2,1)S(1)} %get-tuple-element.8.mine_in), channel_id=1, source_target_pairs={{0,1},{1,0},{2,3},{3,2},{4,5},{5,4},{6,7},{7,6},{8,9},{9,8},{10,11... | collective-permute-start | bytes 393224 | tf_op jit(solution)/shard_map/ppermute | solution.py:18
  33.1 8.3 %collective-permute-start.4 = (bf16[64,2048]{1,0:T(8,128)(2,1)S(1)}, bf16[64,2048]{1,0:T(8,128)(2,1)S(1)}, u32[]{:S(2)}, u32[]{:S(2)}) collective-permute-start(bf16[64,2048]{1,0:T(8,128)(2,1)S(1)} %pad_maximum_fusion), channel_id=1, source_target_pairs={{0,4},{4,0},{5,9},{8,12},{9,5},{12,8},{2,6},{6,2},{7,11},{10,14},{... | collective-permute-start | bytes 786440 | tf_op jit(solution)/shard_map/ppermute | solution.py:28
  41.4 1.5 %collective-permute-start.5 = (bf16[64,2048]{1,0:T(8,128)(2,1)S(1)}, bf16[64,2048]{1,0:T(8,128)(2,1)S(1)}, u32[]{:S(2)}, u32[]{:S(2)}) collective-permute-start(bf16[64,2048]{1,0:T(8,128)(2,1)S(1)} %collective-permute-done.4.direct_in), channel_id=1, source_target_pairs={{0,1},{1,0},{2,3},{3,2},{4,5},{5,4},{6,7},{7,6},{8,9},{9,8},{10,11... | collective-permute-start | bytes 786440 | tf_op jit(solution)/shard_map/ppermute | solution.py:18
  42.1 17.7 %collective-permute-start.11 = (f32[32,8,128]{2,1,0:T(8,128)}, f32[32,8,128]{2,1,0:T(8,128)}, u32[]{:S(2)}, u32[]{:S(2)}) collective-permute-start(f32[32,8,128]{2,1,0:T(8,128)} %constant_dynamic-slice_fusion), channel_id=1, source_target_pairs={{0,1},{1,0},{2,3},{3,2},{4,5},{5,4},{6,7},{7,6},{8,9},{9,8},{10,11... | collective-permute-start | bytes 393224 | tf_op jit(solution)/shard_map/ppermute | solution.py:18
  52.7 0.7 copy-start.3
  53.4 1.2 %collective-permute-start.7 = (f32[8,128]{1,0:T(8,128)S(1)}, f32[8,128]{1,0:T(8,128)S(1)}, u32[]{:S(2)}, u32[]{:S(2)}) collective-permute-start(f32[8,128]{1,0:T(8,128)S(1)} %get-tuple-element.12), channel_id=1, source_target_pairs={{0,1},{1,0},{2,3},{3,2},{4,5},{5,4},{6,7},{7,6},{8,9},{9,8},{10,11... | collective-permute-start | bytes 12296 | tf_op jit(solution)/shard_map/ppermute | solution.py:18
  54.6 3.6 %collective-permute-start.8 = (f32[8,128]{1,0:T(8,128)S(1)}, f32[8,128]{1,0:T(8,128)S(1)}, u32[]{:S(2)}, u32[]{:S(2)}) collective-permute-start(f32[8,128]{1,0:T(8,128)S(1)} %add.75), channel_id=1, source_target_pairs={{0,2},{2,0},{1,3},{3,1},{4,6},{6,4},{5,7},{7,5},{8,10},{10,8},{9,1... | collective-permute-start | bytes 12296 | tf_op jit(solution)/shard_map/ppermute | solution.py:282
  58.2 3.6 %collective-permute-start.9 = (f32[8,128]{1,0:T(8,128)S(1)}, f32[8,128]{1,0:T(8,128)S(1)}, u32[]{:S(2)}, u32[]{:S(2)}) collective-permute-start(f32[8,128]{1,0:T(8,128)S(1)} %add.76), channel_id=1, source_target_pairs={{0,4},{4,0},{8,12},{12,8},{1,5},{5,1},{9,13},{13,9},{2,6},{6,2},{1... | collective-permute-start | bytes 12296 | tf_op jit(solution)/shard_map/ppermute | solution.py:282
  61.8 4.5 %collective-permute-start.10 = (f32[8,128]{1,0:T(8,128)S(1)}, f32[8,128]{1,0:T(8,128)S(1)}, u32[]{:S(2)}, u32[]{:S(2)}) collective-permute-start(f32[8,128]{1,0:T(8,128)S(1)} %add.77), channel_id=1, source_target_pairs={{0,8},{4,12},{8,0},{12,4},{1,9},{5,13},{9,1},{13,5},{2,10},{6,14},... | collective-permute-start | bytes 12296 | tf_op jit(solution)/shard_map/ppermute | solution.py:282
  65.3 8.4 %collective-permute-start.6 = (f32[32,8,128]{2,1,0:T(8,128)S(1)}, f32[32,8,128]{2,1,0:T(8,128)S(1)}, u32[]{:S(2)}, u32[]{:S(2)}) collective-permute-start(f32[32,8,128]{2,1,0:T(8,128)S(1)} %constant_dynamic-slice_fusion.1), channel_id=1, source_target_pairs={{0,1},{1,0},{2,3},{3,2},{4,5},{5,4},{6,7},{7,6},{8,9},{9,8},{10,11... | collective-permute-start | bytes 393224 | tf_op jit(solution)/shard_map/ppermute | solution.py:18

commit v2 on v0

v2 whole, which is shorter than its diff:
```python
import jax
import jax.numpy as jnp
from jax import lax
from jax.experimental import pallas as pl
from jax.experimental.pallas import tpu as pltpu
from jax.sharding import PartitionSpec as P

EPSILON = 1e-06
SHRINK = 2.0**-12
GROW = 1.0 / SHRINK
SLOT = 32
LOCAL = 4
GROUP = 16
VMEM_LIMIT = 40 * 2**20
WHOLE = pl.BlockSpec(memory_space=pltpu.VMEM)


def swap_cores(x):
    return lax.ppermute(x, "mpo", [(0, 1), (1, 0)])


def swap_blocks(x):
    blocks = lax.axis_size("brow")
    pairs = []
    for i in range(blocks):
        for core, partner in ((0, i ^ 1), (1, i + 1 if i % 2 else i - 1)):
            if 0 <= partner < blocks:
                pairs.append((2 * i + core, 2 * partner + core))
    return lax.ppermute(x, ("brow", "mpo"), pairs)


def halo_places(rows):
    even = lax.rem(lax.axis_index("brow") + lax.axis_index("mpo"), 2) == 0
    direct = jnp.where(even, 2 * rows, 0)
    return pl.multiple_of(direct, rows), pl.multiple_of(2 * rows - direct, rows)


def states_apart(wide, rows, states, store):
    lanes = wide.shape[1]
    for state in range(states):
        piece = wide[pl.ds(state, rows, stride=states), :].astype(jnp.bfloat16)
        store(slice(state * lanes, (state + 1) * lanes), piece)


def prepare_kernel(
    env_mine, env_there, mask, left_mpo, right_mpo, vector,
    env, coupling, vector_rows,
    by_bond, wide, left_pad, right_pad, left_rows, right_rows, spread,
):
    core = lax.axis_index("mpo")
    share, rows, _ = env_mine.shape
    half = rows // 2
    here = pl.ds(pl.multiple_of(core * half, half), half)
    part = SLOT // 2
    band = mask.shape[1]
    by_bond[...] = jnp.zeros_like(by_bond)
    for low in range(0, band, 128):
        width = min(128, band - low)
        base = low // 128 * SLOT * half
        for group, source in enumerate((env_mine, env_there)):
            for bond in range(share):
                start = base + (group * part + bond) * half
                piece = source[bond, here, low : low + width].astype(jnp.float32)
                by_bond[start : start + half, 0:width] = piece
        for row in range(half):
            piece = by_bond[pl.ds(base + row, SLOT, stride=half), :][:, 0:width]
            kept = jnp.where(mask[row : row + 1, low : low + width] > 0.0, piece, 0.0)
            env[row * SLOT : (row + 1) * SLOT, low : low + width] = kept.astype(jnp.bfloat16)

    states = vector.shape[0] // rows
    wide[...] = vector[...].astype(jnp.float32)

    def store(columns, piece):
        vector_rows[:, columns] = piece

    states_apart(wide, rows, states, store)

    used, bonds = left_mpo.shape
    left_pad[...] = jnp.zeros_like(left_pad)
    right_pad[...] = jnp.zeros_like(right_pad)
    left_pad[0:used, 0:bonds] = left_mpo[...]
    right_pad[0:used, 0:bonds] = right_mpo[...]
    for state in range(states):
        for group, owner in enumerate((core, 1 - core)):
            start = state * SLOT + group * part
            left_rows[start : start + part, :] = left_pad[
                pl.ds(owner * (share * states) + state, part, stride=states), :
            ]
        across = right_pad[pl.ds(state, SLOT, stride=states), :]
        right_rows[state * SLOT : (state + 1) * SLOT, :] = jnp.transpose(across)[0:SLOT, :]
    joined = lax.dot_general(
        right_rows[...],
        left_rows[:, 0:SLOT],
        (((1,), (1,)), ((), ())),
        precision=lax.Precision.HIGHEST,
        preferred_element_type=jnp.float32,
    )
    width = LOCAL * SLOT
    for i in range(LOCAL):
        for j in range(LOCAL):
            for inner in range(LOCAL):
                start = inner * SLOT * states + i * LOCAL + j
                spread[pl.ds(start, SLOT, stride=states), :] = joined[
                    (j * LOCAL + inner) * SLOT : (j * LOCAL + inner + 1) * SLOT,
                    i * width : (i + 1) * width,
                ]
    for inner in range(LOCAL):
        start = inner * SLOT * states
        coupling[:, inner * width : (inner + 1) * width] = spread[
            start : start + used, :
        ].astype(jnp.bfloat16)


def apply_steps(env, coupling, right, extended, contracted, mixed):
    groups, depth, width = contracted.shape
    lanes = right.shape[1]
    group = width // lanes
    states = depth // SLOT
    bonds = mixed.shape[1] // lanes
    product = jnp.dot(env[...], extended[...], preferred_element_type=jnp.float32)
    product = product.astype(jnp.bfloat16)
    for state in range(states):
        place = state % LOCAL * LOCAL + state // LOCAL
        for row in range(groups * group):
            contracted[
                row // group,
                place * SLOT : (place + 1) * SLOT,
                row % group * lanes : (row % group + 1) * lanes,
            ] = product[row * SLOT : (row + 1) * SLOT, state * lanes : (state + 1) * lanes]

    @pl.loop(0, groups)
    def _(step):
        product = jnp.dot(coupling[...], contracted[step], preferred_element_type=jnp.float32)
        product = product.astype(jnp.bfloat16)
        for part in range(group):
            place = pl.ds(pl.multiple_of((group * step + part) * states, states), states)
            for bond in range(bonds):
                mixed[place, bond * lanes : (bond + 1) * lanes] = product[
                    bond * states : (bond + 1) * states, part * lanes : (part + 1) * lanes
                ]

    return SHRINK * jnp.dot(mixed[...], right[...], preferred_element_type=jnp.float32)


def column_sum(x):
    return jnp.sum(x, axis=0, keepdims=True)


def send_half(image, states):
    lanes = image.shape[1]
    pieces = image.reshape(image.shape[0] // states, states, lanes)
    low, high = pieces[:, : states // 2, :], pieces[:, states // 2 :, :]
    first = lax.axis_index("mpo") == 0
    return jnp.where(first, high, low), jnp.where(first, low, high)


def first_kernel(
    env, coupling, right, vector, vector_rows, direct_in, passed_in,
    image, image_rows, sent, kept, sums,
    wide, extended, contracted, mixed,
):
    rows = vector_rows.shape[0]
    states = vector.shape[0] // rows
    half = image.shape[0]
    extended[rows : 2 * rows, :] = vector_rows[...]
    for place, source in zip(halo_places(rows), (direct_in, passed_in)):
        wide[...] = source[...].astype(jnp.float32)

        def store(columns, piece, place=place):
            extended[pl.ds(place, rows), columns] = piece

        states_apart(wide, rows, states, store)
    out = apply_steps(env, coupling, right, extended, contracted, mixed)
    image[...] = out

    def store_rows(columns, piece):
        image_rows[:, columns] = piece

    states_apart(image, half // states, states, store_rows)
    sent[...], kept[...] = send_half(out, states)
    start = pl.multiple_of(lax.axis_index("mpo") * half, half)
    own = vector[pl.ds(start, half), :].astype(jnp.float32)
    lanes = out.shape[1]
    sums[...] = jnp.concatenate(
        [column_sum(own * own), column_sum(own * out), column_sum(out * out)]
        + [jnp.zeros((5, lanes), jnp.float32)],
        axis=0,
    )


def second_kernel(
    env, coupling, right, mine_in, other_in, direct_in, passed_in, first, vector, sums,
    sent, kept, totals,
    extended, contracted, mixed,
):
    rows = direct_in.shape[0]
    part = rows // 2
    half = first.shape[0]
    core = lax.axis_index("mpo")
    direct, passed = halo_places(rows)
    mine = pl.multiple_of(rows + core * part, part)
    other = pl.multiple_of(rows + (1 - core) * part, part)
    extended[pl.ds(mine, part), :] = mine_in[...]
    extended[pl.ds(other, part), :] = other_in[...]
    extended[pl.ds(direct, rows), :] = direct_in[...]
    extended[pl.ds(passed, rows), :] = passed_in[...]
    out = apply_steps(env, coupling, right, extended, contracted, mixed)
    sent[...], kept[...] = send_half(out, half // part)
    own = vector[pl.ds(pl.multiple_of(core * half, half), half), :].astype(jnp.float32)
    lanes = out.shape[1]
    columns = jnp.concatenate(
        [sums[0:3, :], column_sum(own * out), column_sum(first[...] * out)]
        + [jnp.zeros((3, lanes), jnp.float32)],
        axis=0,
    )
    lane = lax.broadcasted_iota(jnp.int32, columns.shape, 1)
    row = lax.broadcasted_iota(jnp.int32, columns.shape, 0)
    spread = jnp.where(lane == row, jnp.sum(columns, axis=1, keepdims=True), 0.0)
    totals[...] = jnp.broadcast_to(column_sum(spread)[None], totals.shape)


def final_kernel(
    entries, first_kept, first_got, second_kept, second_got, vector, gathered,
    image_two, basis_two, projected,
):
    half, half_states, lanes = first_kept.shape
    core = lax.axis_index("mpo")
    totals = column_sum(jnp.sum(gathered[...], axis=0))
    lane = lax.broadcasted_iota(jnp.int32, totals.shape, 1)

    def total(index):
        return jnp.sum(jnp.where(lane == index, totals, 0.0), axis=1, keepdims=True)

    s_aa, s_ay, s_yy, s_az, s_yz = (total(i) for i in range(5))
    scale_sq = s_aa / entries + EPSILON
    shrunk = s_ay / entries / scale_sq
    residual_sq = jnp.maximum(s_yy - 2.0 * shrunk * s_ay + shrunk * shrunk * s_aa, 0.0)
    residual_norm = jnp.sqrt(residual_sq / scale_sq / entries * (GROW * GROW) + EPSILON)
    factor = GROW / (jnp.sqrt(scale_sq) * residual_norm)
    final = (s_yz - shrunk * s_yy - shrunk * s_az + shrunk * shrunk * s_ay) / entries
    gamma = final * factor * factor * GROW
    r = lax.broadcasted_iota(jnp.int32, projected.shape, 0)
    c = lax.broadcasted_iota(jnp.int32, projected.shape, 1)
    diagonal = jnp.where(r == 0, shrunk * GROW, gamma)
    projected[...] = jnp.where(r == c, diagonal, residual_norm)

    size = half * half_states
    wide = vector[...].astype(jnp.float32).reshape(2 * half, 2 * half_states, lanes)
    own = jnp.where(core == 0, wide[:, :half_states, :], wide[:, half_states:, :])
    own = own.reshape(2 * size, lanes)
    ours = jnp.where(core == 0, own[:size, :], own[size:, :])
    theirs = jnp.where(core == 0, own[size:, :], own[:size, :])
    for index, y_ref, z_ref, a in (
        (core, first_kept, second_kept, ours),
        (1 - core, first_got, second_got, theirs),
    ):
        y = y_ref[...].reshape(size, lanes)
        z = z_ref[...].reshape(size, lanes)
        place = pl.ds(pl.multiple_of(index * size, size), size)
        basis_two[place, :] = ((y - shrunk * a) * factor).astype(jnp.bfloat16)
        image_two[place, :] = ((z - shrunk * y) * (factor * GROW)).astype(jnp.bfloat16)


def call(kernel, operands, outs, scratch, name):
    return pl.pallas_call(
        kernel,
        out_shape=tuple(jax.ShapeDtypeStruct(shape, dtype) for shape, dtype in outs),
        in_specs=[WHOLE] * len(operands),
        out_specs=(WHOLE,) * len(outs),
        scratch_shapes=[pltpu.VMEM(shape, dtype) for shape, dtype in scratch],
        compiler_params=pltpu.CompilerParams(vmem_limit_bytes=VMEM_LIMIT),
        name=name,
    )(*operands)


def per_device(amplitudes, left_env, right_env, mpo_left, mpo_right, sector_table):
    rows, states, columns = amplitudes.shape
    band = left_env.shape[2]
    bonds = mpo_left.shape[0]
    half = rows // 2
    half_states = states // 2
    size = half * states
    block = lax.axis_index("brow")
    core = lax.axis_index("mpo")
    axes = ("brow", "bcol", "mpo")
    peers = lax.axis_size(axes)
    entries = float(rows * lax.axis_size("brow") * states * columns * lax.axis_size("bcol"))
    f32, bf16 = jnp.float32, jnp.bfloat16
    flat = amplitudes.reshape(rows * states, columns)

    env_there = swap_cores(left_env)
    direct_one = swap_blocks(flat)
    passed_one = swap_cores(direct_one)

    outside = jnp.full((rows,), -1, dtype=jnp.int32)
    padded = jnp.concatenate([outside, sector_table, outside])
    own_labels = lax.dynamic_slice_in_dim(padded, (block + 1) * rows + core * half, half, 0)
    partner = lax.dynamic_slice_in_dim(padded, block * rows, 3 * rows, 0)
    mask = (own_labels[:, None] == partner[None, :]).astype(f32)
    left_rows = jnp.transpose(mpo_left, (0, 2, 3, 1)).reshape(bonds * states, bonds)
    right_rows = jnp.transpose(mpo_right, (0, 2, 3, 1)).reshape(bonds * states, bonds)
    env, coupling, vector_rows = call(
        prepare_kernel,
        (left_env, env_there, mask, left_rows, right_rows, flat),
        (
            ((half * SLOT, band), bf16),
            ((bonds * states, states * SLOT), bf16),
            ((rows, states * columns), bf16),
        ),
        (
            ((-(-band // 128) * SLOT * half, 128), f32),
            ((rows * states, columns), f32),
            ((SLOT * states, 128), f32),
            ((SLOT * states, 128), f32),
            ((states * SLOT, 128), f32),
            ((states * SLOT, SLOT), f32),
            ((states // LOCAL * SLOT * states, 128), f32),
        ),
        "operands",
    )
    right = right_env.reshape(bonds * columns, columns)

    work = (
        ((3 * rows, states * columns), bf16),
        ((half // GROUP, states * SLOT, GROUP * columns), bf16),
        ((size, bonds * columns), bf16),
    )
    half_shape = ((half, half_states, columns), f32)
    first, first_rows, first_sent, first_kept, sums = call(
        first_kernel,
        (env, coupling, right, flat, vector_rows, direct_one, passed_one),
        (
            ((size, columns), f32),
            ((half, states * columns), bf16),
            half_shape,
            half_shape,
            ((8, columns), f32),
        ),
        (((rows * states, columns), f32),) + work,
        "first_image",
    )

    other_rows = swap_cores(first_rows)
    mine_first = core == 0
    block_rows = jnp.concatenate(
        [jnp.where(mine_first, first_rows, other_rows), jnp.where(mine_first, other_rows, first_rows)],
        axis=0,
    )
    direct_two = swap_blocks(block_rows)
    first_got = swap_cores(first_sent)
    passed_two = swap_cores(direct_two)

    second_sent, second_kept, totals = call(
        second_kernel,
        (env, coupling, right, first_rows, other_rows, direct_two, passed_two, first, flat, sums),
        (half_shape, half_shape, ((peers, 1, columns), f32)),
        work,
        "second_image",
    )
    second_got = swap_cores(second_sent)
    gathered = lax.all_to_all(totals, axes, 0, 0)

    def finish(*refs):
        final_kernel(entries, *refs)

    image_two, basis_two, projected = call(
        finish,
        (first_kept, first_got, second_kept, second_got, flat, gathered),
        (
            ((rows * half_states, columns), bf16),
            ((rows * half_states, columns), bf16),
            ((2, 2), f32),
        ),
        (),
        "outputs",
    )
    shape = (rows, half_states, columns)
    return (image_two.reshape(shape), basis_two.reshape(shape), projected)


def solution(mesh):
    return jax.shard_map(
        per_device,
        mesh=mesh,
        in_specs=(
            P(("groups", "brow"), None, "bcol"),
            P(("groups", "mpo"), "brow", None),
            P("groups", "bcol", None),
            P(),
            P(),
            P("groups"),
        ),
        out_specs=(
            P(("groups", "brow"), "mpo", "bcol"),
            P(("groups", "brow"), "mpo", "bcol"),
            P("groups", None),
        ),
        check_vma=False,
    )
```

time: 339 us -> 52.8 us (0.16)
  blocking collectives: 123 us -> 0 us
  matrix products: 95.5 us -> 0 us
  local copies, waits for them, and re-layouts: 50.9 us -> 3.98 us
  between operations: 17 us -> 0.75 us
  waiting for transfers between devices: 32.6 us -> 17.1 us
  Pallas kernels: 0 us -> 13.8 us
  other arithmetic: 12.5 us -> 0.19 us
  starting transfers between devices: 6.14 us -> 16.5 us
    psum x4 -> x0, blocking collectives: 123 us -> none  [the longest x1 34.5 us: per_device(): lax.psum(jnp.sum(basis_two_mine.astype(jnp.float32) * image_two), ('brow'...]
    dot_general x29 -> x0, matrix products: 95.5 us -> none  [the longest x26 88.8 us: add_pair(): jnp.einsum('vasb,vbc->asc', mixed_rows, env_pair, preferred_element_type=...]
    dynamic_slice x55 -> x2, local copies, waits for them, and re-layouts: 42.3 us -> 0.15 us  [the longest x1 0.08 us: per_device(): lax.dynamic_slice_in_dim(padded, (block + 1) * rows + core * half, half, 0)]
    psum x1 -> x0, waiting for transfers between devices: 18.5 us -> none  [per_device(): image_whole = lax.psum(partial_one, 'mpo')]
    pallas_call x0 -> x4, Pallas kernels: none -> 13.8 us  [call(): pl.pallas_call(kernel, out_shape=tuple((jax.ShapeDtypeStruct(shape, dtype...]
    reduce_sum x4 -> x0, other arithmetic: 7.39 us -> none  [the longest x1 2.39 us: per_device(): jnp.sum(basis_two_mine.astype(jnp.float32) * image_two)]
    all_to_all x0 -> x1, starting transfers between devices: none -> 6.36 us  [per_device(): gathered = lax.all_to_all(totals, axes, 0, 0)]
    all_to_all x0 -> x1, waiting for transfers between devices: none -> 6.32 us  [per_device(): gathered = lax.all_to_all(totals, axes, 0, 0)]
  transfers between devices with their start and end apart: 6 -> 9, of which waited for: 4 -> 5; matrix products, arithmetic and copies ran while one was open for 2% -> 1% of each run, Pallas kernels for 0% -> 15%
where the time goes in v2:
time: 52.8 us; the launch traced here: 52.4 us
  waiting for transfers between devices  17.1 us (32%)
  starting transfers between devices  16.5 us (31%)
  Pallas kernels  13.8 us (26%)
  local copies, waits for them, and re-layouts  3.98 us (8%)
  between operations  0.75 us (1%)
    pallas_call x4, Pallas kernels, call(): pl.pallas_call(kernel, out_shape=tuple((jax.ShapeDtypeStruct(shape, dtype...  13.8 us
    ppermute x2, starting transfers between devices, swap_blocks(): return lax.ppermute(x, ('brow', 'mpo'), pairs)  8.86 us
    ppermute x2, waiting for transfers between devices, swap_blocks(): return lax.ppermute(x, ('brow', 'mpo'), pairs)  8.8 us
    all_to_all x1, starting transfers between devices, per_device(): gathered = lax.all_to_all(totals, axes, 0, 0)  6.36 us
    all_to_all x1, waiting for transfers between devices, per_device(): gathered = lax.all_to_all(totals, axes, 0, 0)  6.32 us
    unnamed x14, local copies, waits for them, and re-layouts  3.83 us
    ppermute x6, waiting for transfers between devices, swap_cores(): return lax.ppermute(x, 'mpo', [(0, 1), (1, 0)])  2.02 us
    ppermute x6, starting transfers between devices, swap_cores(): return lax.ppermute(x, 'mpo', [(0, 1), (1, 0)])  1.27 us
  transfers between devices with their start and end apart: 9, of which 5 were waited for; matrix products, arithmetic and copies ran while one was open for 1% of the time, Pallas kernels for 15%

profile of v2, /device:TPU:0, one launch (start us, length us, event | category | flops | bytes accessed | tf_op | source)
XLA Modules:
  0.0 52.4 jit_solution(5887536883275512749)
XLA Ops:
  0.6 0.0 copy-start.6
  0.6 4.9 %collective-permute-start.1 = (bf16[1024,128]{1,0:T(8,128)(2,1)}, bf16[1024,128]{1,0:T(8,128)(2,1)S(1)}, u32[]{:S(2)}, u32[]{:S(2)}) collective-permute-start(bf16[1024,128]{1,0:T(8,128)(2,1)} %bitcast.10), channel_id=1, source_target_pairs={{0,4},{4,0},{5,9},{8,12},{9,5},{12,8},{2,6},{6,2},{7,11},{10,14},{... | collective-permute-start | bytes 786440 | tf_op jit(solution)/shard_map/ppermute | solution.py:29
  5.6 0.1 collective-permute-start
  5.7 4.5 %collective-permute-done.1.direct_in = bf16[1024,128]{1,0:T(8,128)(2,1)S(1)} collective-permute-done((bf16[1024,128]{1,0:T(8,128)(2,1)}, bf16[1024,128]{1,0:T(8,128)(2,1)S(1)}, u32[]{:S(2)}, u32[]{:S(2)}) %collective-permute-start.1) | collective-permute-done | bytes 262176 | tf_op jit(solution)/shard_map/ppermute | solution.py:29
  10.1 0.0 collective-permute-start.2
  10.1 0.0 copy-done.6
  10.1 0.1 pad_add_fusion
  10.2 0.1 dynamic_slice.6
  10.3 0.1 dynamic_slice.7
  10.4 0.1 compare_convert_fusion.mask
  10.4 0.0 collective-permute-done.env_there
  10.4 0.0 copy-start
  10.5 0.9 %copy-done = bf16[64,16,128]{2,1,0:T(8,128)(2,1)S(1)} copy-done((bf16[64,16,128]{2,1,0:T(8,128)(2,1)S(1)}, bf16[64,16,128]{2,1,0:T(8,128)(2,1)}, u32[]{:S(2)}) %copy-start) | copy-done | bytes 262168
  11.4 0.0 copy-start.3
  11.4 1.0 %copy-done.3 = bf16[13,64,192]{2,1,0:T(8,128)(2,1)S(1)} copy-done((bf16[13,64,192]{2,1,0:T(8,128)(2,1)S(1)}, bf16[13,64,192]{2,1,0:T(8,128)(2,1)}, u32[]{:S(2)}) %copy-start.3) | copy-done | bytes 319512
  12.4 0.0 copy-start.4
  12.4 0.9 %copy-done.4 = f32[26,26,4,4]{1,3,2,0:T(4,128)S(1)} copy-done((f32[26,26,4,4]{1,3,2,0:T(4,128)S(1)}, f32[26,26,4,4]{1,3,2,0:T(4,128)}, u32[]{:S(2)}) %copy-start.4) | copy-done | bytes 43288
  13.3 0.0 copy-start.5
  13.3 0.9 %copy-done.5 = f32[26,26,4,4]{1,3,2,0:T(4,128)S(1)} copy-done((f32[26,26,4,4]{1,3,2,0:T(4,128)S(1)}, f32[26,26,4,4]{1,3,2,0:T(4,128)}, u32[]{:S(2)}) %copy-start.5) | copy-done | bytes 43288
  14.3 0.0 copy-start.1
  14.3 0.0 copy-start.2
  14.3 2.3 %operands.1 = (bf16[1024,192]{1,0:T(8,128)(2,1)S(1)}, bf16[416,512]{1,0:T(8,128)(2,1)S(1)}, bf16[64,2048]{1,0:T(8,128)(2,1)S(1)}) custom-call(bf16[13,64,192]{2,1,0:T(8,128)(2,1)S(1)} %copy-done.3, bf16[13,64,192]{2,1,0:T(8,128)(2,1)S(1)} %collective-permute-done.env_there, f32[32,192]{1,0:T(8,128)S(1)} %compare_convert_fusion.mask, f32[416,26]{1,0:T(8,128)S(1)} %bitcast.17, ...), custom_call_target="tpu_custom_call" | custom-call | tf_op jit(solution)/shard_map/operands/pallas_call | solution.py:265
  16.6 0.0 collective-permute-done.2.passed_in
  16.6 0.0 copy-done.1
  16.6 0.0 copy-done.2
  16.6 5.2 %first_image.1 = (f32[512,128]{1,0:T(8,128)S(1)}, bf16[32,2048]{1,0:T(8,128)(2,1)S(1)}, f32[32,8,128]{2,1,0:T(8,128)S(1)}, f32[32,8,128]{2,1,0:T(8,128)S(1)}, f32[8,128]{1,0:T(8,128)S(1)}) custom-call(bf16[1024,192]{1,0:T(8,128)(2,1)S(1)} %get-tuple-element.17.env, bf16[416,512]{1,0:T(8,128)(2,1)S(1)} %get-tuple-element.18.coupling, ...), custom_call_target="tpu_custom_call" | custom-call | tf_op jit(solution)/shard_map/first_image/pallas_call | solution.py:265
  21.8 0.6 %collective-permute-start.4 = (bf16[32,2048]{1,0:T(8,128)(2,1)S(1)}, bf16[32,2048]{1,0:T(8,128)(2,1)S(1)}, u32[]{:S(2)}, u32[]{:S(2)}) collective-permute-start(bf16[32,2048]{1,0:T(8,128)(2,1)S(1)} %get-tuple-element.22.mine_in), channel_id=1, source_target_pairs={{0,1},{1,0},{2,3},{3,2},{4,5},{5,4},{6,7},{7,6},{8,9},{9,8},{10,11... | collective-permute-start | bytes 393224 | tf_op jit(solution)/shard_map/ppermute | solution.py:19
  22.4 1.0 %collective-permute-done.4.other_in = bf16[32,2048]{1,0:T(8,128)(2,1)S(1)} collective-permute-done((bf16[32,2048]{1,0:T(8,128)(2,1)S(1)}, bf16[32,2048]{1,0:T(8,128)(2,1)S(1)}, u32[]{:S(2)}, u32[]{:S(2)}) %collective-permute-start.4) | collective-permute-done | bytes 131104 | tf_op jit(solution)/shard_map/ppermute | solution.py:19
  23.4 3.9 %collective-permute-start.5 = (bf16[64,2048]{1,0:T(8,128)(2,1)S(1)}, bf16[64,2048]{1,0:T(8,128)(2,1)S(1)}, u32[]{:S(2)}, u32[]{:S(2)}) collective-permute-start(bf16[64,2048]{1,0:T(8,128)(2,1)S(1)} %pad_maximum_fusion), channel_id=1, source_target_pairs={{0,4},{4,0},{5,9},{8,12},{9,5},{12,8},{2,6},{6,2},{7,11},{10,14},{... | collective-permute-start | bytes 786440 | tf_op jit(solution)/shard_map/ppermute | solution.py:29
  27.4 4.3 %collective-permute-done.5.direct_in = bf16[64,2048]{1,0:T(8,128)(2,1)S(1)} collective-permute-done((bf16[64,2048]{1,0:T(8,128)(2,1)S(1)}, bf16[64,2048]{1,0:T(8,128)(2,1)S(1)}, u32[]{:S(2)}, u32[]{:S(2)}) %collective-permute-start.5) | collective-permute-done | bytes 262176 | tf_op jit(solution)/shard_map/ppermute | solution.py:29
  31.7 0.0 collective-permute-start.6
  31.7 0.5 collective-permute-start.3
  32.2 1.0 %collective-permute-done.6.passed_in = bf16[64,2048]{1,0:T(8,128)(2,1)S(1)} collective-permute-done((bf16[64,2048]{1,0:T(8,128)(2,1)S(1)}, bf16[64,2048]{1,0:T(8,128)(2,1)S(1)}, u32[]{:S(2)}, u32[]{:S(2)}) %collective-permute-start.6) | collective-permute-done | bytes 262176 | tf_op jit(solution)/shard_map/ppermute | solution.py:19
  33.2 5.5 %second_image.1 = (f32[32,8,128]{2,1,0:T(8,128)S(1)}, f32[32,8,128]{2,1,0:T(8,128)S(1)}, f32[16,1,128]{2,1,0:T(1,128)}) custom-call(bf16[1024,192]{1,0:T(8,128)(2,1)S(1)} %get-tuple-element.17.env, bf16[416,512]{1,0:T(8,128)(2,1)S(1)} %get-tuple-element.18.coupling, bf16[3328,128]{1,0:T(8,128)(2,1)S(1)} %bitcast.16, ...), custom_call_target="tpu_custom_call" | custom-call | tf_op jit(solution)/shard_map/second_image/pallas_call | solution.py:265
  38.7 0.1 collective-permute-start.7
  38.8 6.4 %all-to-all-start = ((f32[16,1,128]{2,1,0:T(1,128)}), f32[16,1,128]{2,1,0:T(1,128)S(1)}, u32[]{:S(2)}, u32[]{:S(2)}) async-start(f32[16,1,128]{2,1,0:T(1,128)} %get-tuple-element.27), calls=%async_computation | async-start | bytes 16384 | tf_op jit(solution)/shard_map/all_to_all | solution.py:361
  45.2 0.0 collective-permute-done.3.refs_1_
  45.2 6.3 %all-to-all-done.refs_5_ = f32[16,1,128]{2,1,0:T(1,128)S(1)} async-done(((f32[16,1,128]{2,1,0:T(1,128)}), f32[16,1,128]{2,1,0:T(1,128)S(1)}, u32[]{:S(2)}, u32[]{:S(2)}) %all-to-all-start) | async-done | bytes 8224 | tf_op jit(solution)/shard_map/all_to_all | solution.py:361
  51.5 0.0 collective-permute-done.7.refs_3_
  51.5 0.9 %outputs.1 = (bf16[512,128]{1,0:T(8,128)(2,1)}, bf16[512,128]{1,0:T(8,128)(2,1)}, f32[2,2]{1,0:T(2,128)}) custom-call(f32[32,8,128]{2,1,0:T(8,128)S(1)} %get-tuple-element.20.refs_0_, f32[32,8,128]{2,1,0:T(8,128)S(1)} %collective-permute-done.3.refs_1_, f32[32,8,128]{2,1,0:T(8,128)S(1)} %get-tuple-element.25.refs_2_, ...), custom_call_target="tpu_custom_call" | custom-call | tf_op jit(solution)/shard_map/outputs/pallas_call | solution.py:265
  (3 shorter events, 0.0 us)
Async XLA Ops:
  0.6 9.5 %copy-start.6 = (s32[256]{0:T(256)S(1)}, s32[256]{0:T(256)}, u32[]{:S(2)}) copy-start(s32[256]{0:T(256)} %param.11) | copy-start | bytes 3076
  0.6 9.5 %collective-permute-start.1 = (bf16[1024,128]{1,0:T(8,128)(2,1)}, bf16[1024,128]{1,0:T(8,128)(2,1)S(1)}, u32[]{:S(2)}, u32[]{:S(2)}) collective-permute-start(bf16[1024,128]{1,0:T(8,128)(2,1)} %bitcast.10), channel_id=1, source_target_pairs={{0,4},{4,0},{5,9},{8,12},{9,5},{12,8},{2,6},{6,2},{7,11},{10,14},{... | collective-permute-start | bytes 786440 | tf_op jit(solution)/shard_map/ppermute | solution.py:29
  5.6 4.9 %collective-permute-start = (bf16[13,64,192]{2,1,0:T(8,128)(2,1)}, bf16[13,64,192]{2,1,0:T(8,128)(2,1)S(1)}, u32[]{:S(2)}, u32[]{:S(2)}) collective-permute-start(bf16[13,64,192]{2,1,0:T(8,128)(2,1)} %env_mine.1), channel_id=1, source_target_pairs={{0,1},{1,0},{2,3},{3,2},{4,5},{5,4},{6,7},{7,6},{8,9},{9,8},{10,11... | collective-permute-start | bytes 958472 | tf_op jit(solution)/shard_map/ppermute | solution.py:19
  10.1 6.5 %collective-permute-start.2 = (bf16[1024,128]{1,0:T(8,128)(2,1)S(1)}, bf16[1024,128]{1,0:T(8,128)(2,1)S(1)}, u32[]{:S(2)}, u32[]{:S(2)}) collective-permute-start(bf16[1024,128]{1,0:T(8,128)(2,1)S(1)} %collective-permute-done.1.direct_in), channel_id=1, source_target_pairs={{0,1},{1,0},{2,3},{3,2},{4,5},{5,4},{6,7},{7,6},{8,9},{9,8},{10,11... | collective-permute-start | bytes 786440 | tf_op jit(solution)/shard_map/ppermute | solution.py:19
  10.4 1.0 %copy-start = (bf16[64,16,128]{2,1,0:T(8,128)(2,1)S(1)}, bf16[64,16,128]{2,1,0:T(8,128)(2,1)}, u32[]{:S(2)}) copy-start(bf16[64,16,128]{2,1,0:T(8,128)(2,1)} %param.6) | copy-start | bytes 786436
  11.4 1.0 %copy-start.3 = (bf16[13,64,192]{2,1,0:T(8,128)(2,1)S(1)}, bf16[13,64,192]{2,1,0:T(8,128)(2,1)}, u32[]{:S(2)}) copy-start(bf16[13,64,192]{2,1,0:T(8,128)(2,1)} %env_mine.1) | copy-start | bytes 958468
  12.4 0.9 %copy-start.4 = (f32[26,26,4,4]{1,3,2,0:T(4,128)S(1)}, f32[26,26,4,4]{1,3,2,0:T(4,128)}, u32[]{:S(2)}) copy-start(f32[26,26,4,4]{1,3,2,0:T(4,128)} %param.9) | copy-start | bytes 129796
  13.3 0.9 %copy-start.5 = (f32[26,26,4,4]{1,3,2,0:T(4,128)S(1)}, f32[26,26,4,4]{1,3,2,0:T(4,128)}, u32[]{:S(2)}) copy-start(f32[26,26,4,4]{1,3,2,0:T(4,128)} %param.10) | copy-start | bytes 129796
  14.3 2.3 %copy-start.1 = (bf16[64,16,128]{2,1,0:T(8,128)(2,1)S(1)}, bf16[64,16,128]{2,1,0:T(8,128)(2,1)}, u32[]{:S(2)}) copy-start(bf16[64,16,128]{2,1,0:T(8,128)(2,1)} %param.6) | copy-start | bytes 786436
  14.3 2.3 %copy-start.2 = (bf16[26,128,128]{2,1,0:T(8,128)(2,1)S(1)}, bf16[26,128,128]{2,1,0:T(8,128)(2,1)}, u32[]{:S(2)}) copy-start(bf16[26,128,128]{2,1,0:T(8,128)(2,1)} %param.8) | copy-start | bytes 2555908
  21.8 1.6 %collective-permute-start.4 = (bf16[32,2048]{1,0:T(8,128)(2,1)S(1)}, bf16[32,2048]{1,0:T(8,128)(2,1)S(1)}, u32[]{:S(2)}, u32[]{:S(2)}) collective-permute-start(bf16[32,2048]{1,0:T(8,128)(2,1)S(1)} %get-tuple-element.22.mine_in), channel_id=1, source_target_pairs={{0,1},{1,0},{2,3},{3,2},{4,5},{5,4},{6,7},{7,6},{8,9},{9,8},{10,11... | collective-permute-start | bytes 393224 | tf_op jit(solution)/shard_map/ppermute | solution.py:19
  23.4 8.3 %collective-permute-start.5 = (bf16[64,2048]{1,0:T(8,128)(2,1)S(1)}, bf16[64,2048]{1,0:T(8,128)(2,1)S(1)}, u32[]{:S(2)}, u32[]{:S(2)}) collective-permute-start(bf16[64,2048]{1,0:T(8,128)(2,1)S(1)} %pad_maximum_fusion), channel_id=1, source_target_pairs={{0,4},{4,0},{5,9},{8,12},{9,5},{12,8},{2,6},{6,2},{7,11},{10,14},{... | collective-permute-start | bytes 786440 | tf_op jit(solution)/shard_map/ppermute | solution.py:29
  31.7 1.5 %collective-permute-start.6 = (bf16[64,2048]{1,0:T(8,128)(2,1)S(1)}, bf16[64,2048]{1,0:T(8,128)(2,1)S(1)}, u32[]{:S(2)}, u32[]{:S(2)}) collective-permute-start(bf16[64,2048]{1,0:T(8,128)(2,1)S(1)} %collective-permute-done.5.direct_in), channel_id=1, source_target_pairs={{0,1},{1,0},{2,3},{3,2},{4,5},{5,4},{6,7},{7,6},{8,9},{9,8},{10,11... | collective-permute-start | bytes 786440 | tf_op jit(solution)/shard_map/ppermute | solution.py:19
  31.7 13.5 %collective-permute-start.3 = (f32[32,8,128]{2,1,0:T(8,128)S(1)}, f32[32,8,128]{2,1,0:T(8,128)S(1)}, u32[]{:S(2)}, u32[]{:S(2)}) collective-permute-start(f32[32,8,128]{2,1,0:T(8,128)S(1)} %get-tuple-element.21), channel_id=1, source_target_pairs={{0,1},{1,0},{2,3},{3,2},{4,5},{5,4},{6,7},{7,6},{8,9},{9,8},{10,11... | collective-permute-start | bytes 393224 | tf_op jit(solution)/shard_map/ppermute | solution.py:19
  38.7 12.8 %collective-permute-start.7 = (f32[32,8,128]{2,1,0:T(8,128)S(1)}, f32[32,8,128]{2,1,0:T(8,128)S(1)}, u32[]{:S(2)}, u32[]{:S(2)}) collective-permute-start(f32[32,8,128]{2,1,0:T(8,128)S(1)} %get-tuple-element.26), channel_id=1, source_target_pairs={{0,1},{1,0},{2,3},{3,2},{4,5},{5,4},{6,7},{7,6},{8,9},{9,8},{10,11... | collective-permute-start | bytes 393224 | tf_op jit(solution)/shard_map/ppermute | solution.py:19
  38.8 12.7 %all-to-all-start = ((f32[16,1,128]{2,1,0:T(1,128)}), f32[16,1,128]{2,1,0:T(1,128)S(1)}, u32[]{:S(2)}, u32[]{:S(2)}) async-start(f32[16,1,128]{2,1,0:T(1,128)} %get-tuple-element.27), calls=%async_computation | async-start | bytes 16384 | tf_op jit(solution)/shard_map/all_to_all | solution.py:361

commit v3 on v2

--- a/solution.py
+++ b/solution.py
@@ -43,15 +43,51 @@
 
 
 def prepare_kernel(
-    env_mine, env_there, mask, left_mpo, right_mpo, vector,
-    env, coupling, vector_rows,
-    by_bond, wide, left_pad, right_pad, left_rows, right_rows, spread,
+    env_mine, env_there, mask, both_mpo,
+    env, coupling,
+    by_bond, left_pad, right_pad, left_rows, right_rows, spread,
 ):
     core = lax.axis_index("mpo")
     share, rows, _ = env_mine.shape
     half = rows // 2
     here = pl.ds(pl.multiple_of(core * half, half), half)
     part = SLOT // 2
+    used, bonds = both_mpo.shape[0] // 2, both_mpo.shape[1]
+    states = used // bonds
+    left_pad[...] = jnp.zeros_like(left_pad)
+    right_pad[...] = jnp.zeros_like(right_pad)
+    left_pad[0:used, 0:bonds] = both_mpo[0:used, :]
+    right_pad[0:used, 0:bonds] = both_mpo[used : 2 * used, :]
+    for state in range(states):
+        for group, owner in enumerate((core, 1 - core)):
+            start = state * SLOT + group * part
+            left_rows[start : start + part, :] = left_pad[
+                pl.ds(owner * (share * states) + state, part, stride=states), :
+            ]
+        across = right_pad[pl.ds(state, SLOT, stride=states), :]
+        right_rows[state * SLOT : (state + 1) * SLOT, :] = jnp.transpose(across)[0:SLOT, :]
+    joined = lax.dot_general(
+        right_rows[...],
+        left_rows[:, 0:SLOT],
+        (((1,), (1,)), ((), ())),
+        precision=lax.Precision.HIGHEST,
+        preferred_element_type=jnp.float32,
+    )
+    width = LOCAL * SLOT
+    for i in range(LOCAL):
+        for j in range(LOCAL):
+            for inner in range(LOCAL):
+                start = inner * SLOT * states + i * LOCAL + j
+                spread[pl.ds(start, SLOT, stride=states), :] = joined[
+                    (j * LOCAL + inner) * SLOT : (j * LOCAL + inner + 1) * SLOT,
+                    i * width : (i + 1) * width,
+                ]
+    for inner in range(LOCAL):
+        start = inner * SLOT * states
+        coupling[:, inner * width : (inner + 1) * width] = spread[
+            start : start + used, :
+        ].astype(jnp.bfloat16)
+
     band = mask.shape[1]
     by_bond[...] = jnp.zeros_like(by_bond)
     for low in range(0, band, 128):
@@ -66,49 +102,6 @@
             piece = by_bond[pl.ds(base + row, SLOT, stride=half), :][:, 0:width]
             kept = jnp.where(mask[row : row + 1, low : low + width] > 0.0, piece, 0.0)
             env[row * SLOT : (row + 1) * SLOT, low : low + width] = kept.astype(jnp.bfloat16)
-
-    states = vector.shape[0] // rows
-    wide[...] = vector[...].astype(jnp.float32)
-
-    def store(columns, piece):
-        vector_rows[:, columns] = piece
-
-    states_apart(wide, rows, states, store)
-
-    used, bonds = left_mpo.shape
-    left_pad[...] = jnp.zeros_like(left_pad)
-    right_pad[...] = jnp.zeros_like(right_pad)
-    left_pad[0:used, 0:bonds] = left_mpo[...]
-    right_pad[0:used, 0:bonds] = right_mpo[...]
-    for state in range(states):
-        for group, owner in enumerate((core, 1 - core)):
-            start = state * SLOT + group * part
-            left_rows[start : start + part, :] = left_pad[
-                pl.ds(owner * (share * states) + state, part, stride=states), :
-            ]
-        across = right_pad[pl.ds(state, SLOT, stride=states), :]
-        right_rows[state * SLOT : (state + 1) * SLOT, :] = jnp.transpose(across)[0:SLOT, :]
-    joined = lax.dot_general(
-        right_rows[...],
-        left_rows[:, 0:SLOT],
-        (((1,), (1,)), ((), ())),
-        precision=lax.Precision.HIGHEST,
-        preferred_element_type=jnp.float32,
-    )
-    width = LOCAL * SLOT
-    for i in range(LOCAL):
-        for j in range(LOCAL):
-            for inner in range(LOCAL):
-                start = inner * SLOT * states + i * LOCAL + j
-                spread[pl.ds(start, SLOT, stride=states), :] = joined[
-                    (j * LOCAL + inner) * SLOT : (j * LOCAL + inner + 1) * SLOT,
-                    i * width : (i + 1) * width,
-                ]
-    for inner in range(LOCAL):
-        start = inner * SLOT * states
-        coupling[:, inner * width : (inner + 1) * width] = spread[
-            start : start + used, :
-        ].astype(jnp.bfloat16)
 
 
 def apply_steps(env, coupling, right, extended, contracted, mixed):
@@ -155,15 +148,14 @@
 
 
 def first_kernel(
-    env, coupling, right, vector, vector_rows, direct_in, passed_in,
+    env, coupling, right, vector, direct_in, passed_in,
     image, image_rows, sent, kept, sums,
     wide, extended, contracted, mixed,
 ):
-    rows = vector_rows.shape[0]
+    rows = extended.shape[0] // 3
     states = vector.shape[0] // rows
     half = image.shape[0]
-    extended[rows : 2 * rows, :] = vector_rows[...]
-    for place, source in zip(halo_places(rows), (direct_in, passed_in)):
+    for place, source in zip((rows,) + halo_places(rows), (vector, direct_in, passed_in)):
         wide[...] = source[...].astype(jnp.float32)
 
         def store(columns, piece, place=place):
@@ -261,13 +253,14 @@
         image_two[place, :] = ((z - shrunk * y) * (factor * GROW)).astype(jnp.bfloat16)
 
 
-def call(kernel, operands, outs, scratch, name):
+def call(kernel, operands, outs, scratch, name, cost=None):
     return pl.pallas_call(
         kernel,
         out_shape=tuple(jax.ShapeDtypeStruct(shape, dtype) for shape, dtype in outs),
         in_specs=[WHOLE] * len(operands),
         out_specs=(WHOLE,) * len(outs),
         scratch_shapes=[pltpu.VMEM(shape, dtype) for shape, dtype in scratch],
+        cost_estimate=cost,
         compiler_params=pltpu.CompilerParams(vmem_limit_bytes=VMEM_LIMIT),
         name=name,
     )(*operands)
@@ -290,26 +283,23 @@
 
     env_there = swap_cores(left_env)
     direct_one = swap_blocks(flat)
-    passed_one = swap_cores(direct_one)
 
     outside = jnp.full((rows,), -1, dtype=jnp.int32)
     padded = jnp.concatenate([outside, sector_table, outside])
     own_labels = lax.dynamic_slice_in_dim(padded, (block + 1) * rows + core * half, half, 0)
     partner = lax.dynamic_slice_in_dim(padded, block * rows, 3 * rows, 0)
     mask = (own_labels[:, None] == partner[None, :]).astype(f32)
-    left_rows = jnp.transpose(mpo_left, (0, 2, 3, 1)).reshape(bonds * states, bonds)
-    right_rows = jnp.transpose(mpo_right, (0, 2, 3, 1)).reshape(bonds * states, bonds)
-    env, coupling, vector_rows = call(
+    both = jnp.concatenate([mpo_left, mpo_right], axis=0)
+    both = jnp.transpose(both, (0, 2, 3, 1)).reshape(2 * bonds * states, bonds)
+    env, coupling = call(
         prepare_kernel,
-        (left_env, env_there, mask, left_rows, right_rows, flat),
+        (left_env, env_there, mask, both),
         (
             ((half * SLOT, band), bf16),
             ((bonds * states, states * SLOT), bf16),
-            ((rows, states * columns), bf16),
         ),
         (
             ((-(-band // 128) * SLOT * half, 128), f32),
-            ((rows * states, columns), f32),
             ((SLOT * states, 128), f32),
             ((SLOT * states, 128), f32),
             ((states * SLOT, 128), f32),
@@ -317,7 +307,10 @@
             ((states // LOCAL * SLOT * states, 128), f32),
         ),
         "operands",
-    )
+        cost=pl.CostEstimate(flops=4 * 10**9, bytes_accessed=2**23, transcendentals=0),
+    )
+    direct_one, env, coupling = lax.optimization_barrier((direct_one, env, coupling))
+    passed_one = swap_cores(direct_one)
     right = right_env.reshape(bonds * columns, columns)
 
     work = (
@@ -328,7 +321,7 @@
     half_shape = ((half, half_states, columns), f32)
     first, first_rows, first_sent, first_kept, sums = call(
         first_kernel,
-        (env, coupling, right, flat, vector_rows, direct_one, passed_one),
+        (env, coupling, right, flat, direct_one, passed_one),
         (
             ((size, columns), f32),
             ((half, states * columns), bf16),

time: 52.8 us -> 47.8 us (0.905)
  local copies, waits for them, and re-layouts: 3.98 us -> 0.83 us
  waiting for transfers between devices: 17.1 us -> 14 us
  other arithmetic: 0.19 us -> 1.39 us
    ppermute x2, waiting for transfers between devices: 8.8 us -> 4.54 us  [swap_blocks(): return lax.ppermute(x, ('brow', 'mpo'), pairs)]
    unnamed x14 -> x8, local copies, waits for them, and re-layouts: 3.83 us -> 0.68 us
    concatenate x0 -> x1, other arithmetic: none -> 1.2 us  [per_device(): both = jnp.concatenate([mpo_left, mpo_right], axis=0)]
    ppermute x6, waiting for transfers between devices: 2.02 us -> 3.18 us  [swap_cores(): return lax.ppermute(x, 'mpo', [(0, 1), (1, 0)])]
  transfers between devices with their start and end apart: 9 -> 9, of which waited for: 5 -> 6; matrix products, arithmetic and copies ran while one was open for 1% -> 3% of each run, Pallas kernels for 15% -> 16%
where the time goes in v3:
time: 47.8 us; the launch traced here: 47.6 us
  starting transfers between devices  16.6 us (35%)
  waiting for transfers between devices  14 us (29%)
  Pallas kernels  13.9 us (29%)
  other arithmetic  1.39 us (3%)
  local copies, waits for them, and re-layouts  0.83 us (2%)
  between operations  0.76 us (2%)
    pallas_call x4, Pallas kernels, call(): pl.pallas_call(kernel, out_shape=tuple((jax.ShapeDtypeStruct(shape, dtype...  13.9 us
    ppermute x2, starting transfers between devices, swap_blocks(): return lax.ppermute(x, ('brow', 'mpo'), pairs)  8.77 us
    all_to_all x1, waiting for transfers between devices, per_device(): gathered = lax.all_to_all(totals, axes, 0, 0)  6.32 us
    all_to_all x1, starting transfers between devices, per_device(): gathered = lax.all_to_all(totals, axes, 0, 0)  6.27 us
    ppermute x2, waiting for transfers between devices, swap_blocks(): return lax.ppermute(x, ('brow', 'mpo'), pairs)  4.54 us
    ppermute x6, waiting for transfers between devices, swap_cores(): return lax.ppermute(x, 'mpo', [(0, 1), (1, 0)])  3.18 us
    ppermute x6, starting transfers between devices, swap_cores(): return lax.ppermute(x, 'mpo', [(0, 1), (1, 0)])  1.59 us
    concatenate x1, other arithmetic, per_device(): both = jnp.concatenate([mpo_left, mpo_right], axis=0)  1.2 us
  transfers between devices with their start and end apart: 9, of which 6 were waited for; matrix products, arithmetic and copies ran while one was open for 3% of the time, Pallas kernels for 16%

profile of v3, /device:TPU:0, one launch (start us, length us, event | category | flops | bytes accessed | tf_op | source)
XLA Modules:
  0.0 47.6 jit_solution(2610179907257755068)
XLA Ops:
  0.6 4.9 %collective-permute-start = (bf16[1024,128]{1,0:T(8,128)(2,1)}, bf16[1024,128]{1,0:T(8,128)(2,1)S(1)}, u32[]{:S(2)}, u32[]{:S(2)}) collective-permute-start(bf16[1024,128]{1,0:T(8,128)(2,1)} %bitcast.9), channel_id=1, source_target_pairs={{0,4},{4,0},{5,9},{8,12},{9,5},{12,8},{2,6},{6,2},{7,11},{10,14},{... | collective-permute-start | bytes 786440 | tf_op jit(solution)/shard_map/ppermute | solution.py:29
  5.6 0.1 collective-permute-start.1
  5.7 0.0 copy-start.3
  5.7 0.7 %copy-done.3 = s32[256]{0:T(256)S(1)} copy-done((s32[256]{0:T(256)S(1)}, s32[256]{0:T(256)}, u32[]{:S(2)}) %copy-start.3) | copy-done | bytes 1048
  6.3 0.1 pad_add_fusion
  6.4 0.1 dynamic_slice.6
  6.5 0.1 dynamic_slice.7
  6.6 0.0 copy-start.2
  6.6 1.2 %pad_maximum_fusion = f32[52,26,4,4]{1,3,2,0:T(4,128)S(1)} fusion(f32[26,26,4,4]{1,3,2,0:T(4,128)} %param.10, f32[26,26,4,4]{1,3,2,0:T(4,128)} %param.9), kind=kLoop, calls=%fused_computation | loop fusion | flops 21632 | bytes 173056 | tf_op jit(solution)/shard_map/concatenate | solution.py:292
  7.8 0.1 compare_convert_fusion.mask
  7.8 0.0 collective-permute-done.1.env_there
  7.9 0.0 copy-done.2
  7.9 0.0 copy-start
  7.9 0.0 copy-start.1
  7.9 2.1 %operands.1 = (bf16[1024,192]{1,0:T(8,128)(2,1)S(1)}, bf16[416,512]{1,0:T(8,128)(2,1)S(1)}) custom-call(bf16[13,64,192]{2,1,0:T(8,128)(2,1)S(1)} %copy-done.2, bf16[13,64,192]{2,1,0:T(8,128)(2,1)S(1)} %collective-permute-done.1.env_there, f32[32,192]{1,0:T(8,128)S(1)} %compare_convert_fusion.mask, f32[832,26]{1,0:T(8,128)S(1)} %bitcast.13), custom_call_target="tpu_custom_call" | custom-call | flops 4000000000 | bytes 8388608 | tf_op jit(solution)/shard_map/operands/pallas_call | solution.py:257
  10.0 0.1 collective-permute-done.direct_in
  10.1 0.4 collective-permute-start.2
  10.6 1.2 %collective-permute-done.2.passed_in = bf16[1024,128]{1,0:T(8,128)(2,1)S(1)} collective-permute-done((bf16[1024,128]{1,0:T(8,128)(2,1)S(1)}, bf16[1024,128]{1,0:T(8,128)(2,1)S(1)}, u32[]{:S(2)}, u32[]{:S(2)}) %collective-permute-start.2) | collective-permute-done | bytes 262176 | tf_op jit(solution)/shard_map/ppermute | solution.py:19
  11.7 0.0 copy-done
  11.7 0.0 copy-done.1
  11.7 5.5 %first_image.1 = (f32[512,128]{1,0:T(8,128)S(1)}, bf16[32,2048]{1,0:T(8,128)(2,1)S(1)}, f32[32,8,128]{2,1,0:T(8,128)S(1)}, f32[32,8,128]{2,1,0:T(8,128)S(1)}, f32[8,128]{1,0:T(8,128)S(1)}) custom-call(bf16[1024,192]{1,0:T(8,128)(2,1)S(1)} %get-tuple-element.21.env, bf16[416,512]{1,0:T(8,128)(2,1)S(1)} %get-tuple-element.22.coupling, ...), custom_call_target="tpu_custom_call" | custom-call | tf_op jit(solution)/shard_map/first_image/pallas_call | solution.py:257
  17.2 0.4 collective-permute-start.4
  17.6 1.0 %collective-permute-done.4.other_in = bf16[32,2048]{1,0:T(8,128)(2,1)S(1)} collective-permute-done((bf16[32,2048]{1,0:T(8,128)(2,1)S(1)}, bf16[32,2048]{1,0:T(8,128)(2,1)S(1)}, u32[]{:S(2)}, u32[]{:S(2)}) %collective-permute-start.4) | collective-permute-done | bytes 131104 | tf_op jit(solution)/shard_map/ppermute | solution.py:19
  18.7 3.8 %collective-permute-start.5 = (bf16[64,2048]{1,0:T(8,128)(2,1)S(1)}, bf16[64,2048]{1,0:T(8,128)(2,1)S(1)}, u32[]{:S(2)}, u32[]{:S(2)}) collective-permute-start(bf16[64,2048]{1,0:T(8,128)(2,1)S(1)} %pad_maximum_fusion.1), channel_id=1, source_target_pairs={{0,4},{4,0},{5,9},{8,12},{9,5},{12,8},{2,6},{6,2},{7,11},{10,14},{... | collective-permute-start | bytes 786440 | tf_op jit(solution)/shard_map/ppermute | solution.py:29
  22.5 4.4 %collective-permute-done.5.direct_in = bf16[64,2048]{1,0:T(8,128)(2,1)S(1)} collective-permute-done((bf16[64,2048]{1,0:T(8,128)(2,1)S(1)}, bf16[64,2048]{1,0:T(8,128)(2,1)S(1)}, u32[]{:S(2)}, u32[]{:S(2)}) %collective-permute-start.5) | collective-permute-done | bytes 262176 | tf_op jit(solution)/shard_map/ppermute | solution.py:29
  27.0 0.0 collective-permute-start.6
  27.0 0.5 %collective-permute-start.3 = (f32[32,8,128]{2,1,0:T(8,128)S(1)}, f32[32,8,128]{2,1,0:T(8,128)S(1)}, u32[]{:S(2)}, u32[]{:S(2)}) collective-permute-start(f32[32,8,128]{2,1,0:T(8,128)S(1)} %get-tuple-element.25), channel_id=1, source_target_pairs={{0,1},{1,0},{2,3},{3,2},{4,5},{5,4},{6,7},{7,6},{8,9},{9,8},{10,11... | collective-permute-start | bytes 393224 | tf_op jit(solution)/shard_map/ppermute | solution.py:19
  27.5 1.0 %collective-permute-done.6.passed_in = bf16[64,2048]{1,0:T(8,128)(2,1)S(1)} collective-permute-done((bf16[64,2048]{1,0:T(8,128)(2,1)S(1)}, bf16[64,2048]{1,0:T(8,128)(2,1)S(1)}, u32[]{:S(2)}, u32[]{:S(2)}) %collective-permute-start.6) | collective-permute-done | bytes 262176 | tf_op jit(solution)/shard_map/ppermute | solution.py:19
  28.5 5.5 %second_image.1 = (f32[32,8,128]{2,1,0:T(8,128)S(1)}, f32[32,8,128]{2,1,0:T(8,128)S(1)}, f32[16,1,128]{2,1,0:T(1,128)}) custom-call(bf16[1024,192]{1,0:T(8,128)(2,1)S(1)} %get-tuple-element.21.env, bf16[416,512]{1,0:T(8,128)(2,1)S(1)} %get-tuple-element.22.coupling, bf16[3328,128]{1,0:T(8,128)(2,1)S(1)} %bitcast.8, ...), custom_call_target="tpu_custom_call" | custom-call | tf_op jit(solution)/shard_map/second_image/pallas_call | solution.py:257
  33.9 0.1 collective-permute-start.7
  34.1 6.3 %all-to-all-start = ((f32[16,1,128]{2,1,0:T(1,128)}), f32[16,1,128]{2,1,0:T(1,128)S(1)}, u32[]{:S(2)}, u32[]{:S(2)}) async-start(f32[16,1,128]{2,1,0:T(1,128)} %get-tuple-element.31), calls=%async_computation | async-start | bytes 16384 | tf_op jit(solution)/shard_map/all_to_all | solution.py:354
  40.4 0.0 collective-permute-done.3.refs_1_
  40.4 6.3 %all-to-all-done.refs_5_ = f32[16,1,128]{2,1,0:T(1,128)S(1)} async-done(((f32[16,1,128]{2,1,0:T(1,128)}), f32[16,1,128]{2,1,0:T(1,128)S(1)}, u32[]{:S(2)}, u32[]{:S(2)}) %all-to-all-start) | async-done | bytes 8224 | tf_op jit(solution)/shard_map/all_to_all | solution.py:354
  46.7 0.0 collective-permute-done.7.refs_3_
  46.7 0.9 %outputs.1 = (bf16[512,128]{1,0:T(8,128)(2,1)}, bf16[512,128]{1,0:T(8,128)(2,1)}, f32[2,2]{1,0:T(2,128)}) custom-call(f32[32,8,128]{2,1,0:T(8,128)S(1)} %get-tuple-element.24.refs_0_, f32[32,8,128]{2,1,0:T(8,128)S(1)} %collective-permute-done.3.refs_1_, f32[32,8,128]{2,1,0:T(8,128)S(1)} %get-tuple-element.29.refs_2_, ...), custom_call_target="tpu_custom_call" | custom-call | tf_op jit(solution)/shard_map/outputs/pallas_call | solution.py:257
  (3 shorter events, 0.0 us)
Async XLA Ops:
  0.6 9.5 %collective-permute-start = (bf16[1024,128]{1,0:T(8,128)(2,1)}, bf16[1024,128]{1,0:T(8,128)(2,1)S(1)}, u32[]{:S(2)}, u32[]{:S(2)}) collective-permute-start(bf16[1024,128]{1,0:T(8,128)(2,1)} %bitcast.9), channel_id=1, source_target_pairs={{0,4},{4,0},{5,9},{8,12},{9,5},{12,8},{2,6},{6,2},{7,11},{10,14},{... | collective-permute-start | bytes 786440 | tf_op jit(solution)/shard_map/ppermute | solution.py:29
  5.6 2.3 %collective-permute-start.1 = (bf16[13,64,192]{2,1,0:T(8,128)(2,1)}, bf16[13,64,192]{2,1,0:T(8,128)(2,1)S(1)}, u32[]{:S(2)}, u32[]{:S(2)}) collective-permute-start(bf16[13,64,192]{2,1,0:T(8,128)(2,1)} %env_mine.1), channel_id=1, source_target_pairs={{0,1},{1,0},{2,3},{3,2},{4,5},{5,4},{6,7},{7,6},{8,9},{9,8},{10,11... | collective-permute-start | bytes 958472 | tf_op jit(solution)/shard_map/ppermute | solution.py:19
  5.7 0.7 %copy-start.3 = (s32[256]{0:T(256)S(1)}, s32[256]{0:T(256)}, u32[]{:S(2)}) copy-start(s32[256]{0:T(256)} %param.11) | copy-start | bytes 3076
  6.6 1.3 %copy-start.2 = (bf16[13,64,192]{2,1,0:T(8,128)(2,1)S(1)}, bf16[13,64,192]{2,1,0:T(8,128)(2,1)}, u32[]{:S(2)}) copy-start(bf16[13,64,192]{2,1,0:T(8,128)(2,1)} %env_mine.1) | copy-start | bytes 958468
  7.9 3.9 %copy-start = (bf16[26,128,128]{2,1,0:T(8,128)(2,1)S(1)}, bf16[26,128,128]{2,1,0:T(8,128)(2,1)}, u32[]{:S(2)}) copy-start(bf16[26,128,128]{2,1,0:T(8,128)(2,1)} %param.8) | copy-start | bytes 2555908
  7.9 3.9 %copy-start.1 = (bf16[64,16,128]{2,1,0:T(8,128)(2,1)S(1)}, bf16[64,16,128]{2,1,0:T(8,128)(2,1)}, u32[]{:S(2)}) copy-start(bf16[64,16,128]{2,1,0:T(8,128)(2,1)} %param.6) | copy-start | bytes 786436
  10.1 1.6 %collective-permute-start.2 = (bf16[1024,128]{1,0:T(8,128)(2,1)S(1)}, bf16[1024,128]{1,0:T(8,128)(2,1)S(1)}, u32[]{:S(2)}, u32[]{:S(2)}) collective-permute-start(bf16[1024,128]{1,0:T(8,128)(2,1)S(1)} %collective-permute-done.direct_in), channel_id=1, source_target_pairs={{0,1},{1,0},{2,3},{3,2},{4,5},{5,4},{6,7},{7,6},{8,9},{9,8},{10,11... | collective-permute-start | bytes 786440 | tf_op jit(solution)/shard_map/ppermute | solution.py:19
  17.2 1.4 %collective-permute-start.4 = (bf16[32,2048]{1,0:T(8,128)(2,1)S(1)}, bf16[32,2048]{1,0:T(8,128)(2,1)S(1)}, u32[]{:S(2)}, u32[]{:S(2)}) collective-permute-start(bf16[32,2048]{1,0:T(8,128)(2,1)S(1)} %get-tuple-element.26.mine_in), channel_id=1, source_target_pairs={{0,1},{1,0},{2,3},{3,2},{4,5},{5,4},{6,7},{7,6},{8,9},{9,8},{10,11... | collective-permute-start | bytes 393224 | tf_op jit(solution)/shard_map/ppermute | solution.py:19
  18.7 8.3 %collective-permute-start.5 = (bf16[64,2048]{1,0:T(8,128)(2,1)S(1)}, bf16[64,2048]{1,0:T(8,128)(2,1)S(1)}, u32[]{:S(2)}, u32[]{:S(2)}) collective-permute-start(bf16[64,2048]{1,0:T(8,128)(2,1)S(1)} %pad_maximum_fusion.1), channel_id=1, source_target_pairs={{0,4},{4,0},{5,9},{8,12},{9,5},{12,8},{2,6},{6,2},{7,11},{10,14},{... | collective-permute-start | bytes 786440 | tf_op jit(solution)/shard_map/ppermute | solution.py:29
  27.0 1.5 %collective-permute-start.6 = (bf16[64,2048]{1,0:T(8,128)(2,1)S(1)}, bf16[64,2048]{1,0:T(8,128)(2,1)S(1)}, u32[]{:S(2)}, u32[]{:S(2)}) collective-permute-start(bf16[64,2048]{1,0:T(8,128)(2,1)S(1)} %collective-permute-done.5.direct_in), channel_id=1, source_target_pairs={{0,1},{1,0},{2,3},{3,2},{4,5},{5,4},{6,7},{7,6},{8,9},{9,8},{10,11... | collective-permute-start | bytes 786440 | tf_op jit(solution)/shard_map/ppermute | solution.py:19
  27.0 13.4 %collective-permute-start.3 = (f32[32,8,128]{2,1,0:T(8,128)S(1)}, f32[32,8,128]{2,1,0:T(8,128)S(1)}, u32[]{:S(2)}, u32[]{:S(2)}) collective-permute-start(f32[32,8,128]{2,1,0:T(8,128)S(1)} %get-tuple-element.25), channel_id=1, source_target_pairs={{0,1},{1,0},{2,3},{3,2},{4,5},{5,4},{6,7},{7,6},{8,9},{9,8},{10,11... | collective-permute-start | bytes 393224 | tf_op jit(solution)/shard_map/ppermute | solution.py:19
  33.9 12.8 %collective-permute-start.7 = (f32[32,8,128]{2,1,0:T(8,128)S(1)}, f32[32,8,128]{2,1,0:T(8,128)S(1)}, u32[]{:S(2)}, u32[]{:S(2)}) collective-permute-start(f32[32,8,128]{2,1,0:T(8,128)S(1)} %get-tuple-element.30), channel_id=1, source_target_pairs={{0,1},{1,0},{2,3},{3,2},{4,5},{5,4},{6,7},{7,6},{8,9},{9,8},{10,11... | collective-permute-start | bytes 393224 | tf_op jit(solution)/shard_map/ppermute | solution.py:19
  34.1 12.6 %all-to-all-start = ((f32[16,1,128]{2,1,0:T(1,128)}), f32[16,1,128]{2,1,0:T(1,128)S(1)}, u32[]{:S(2)}, u32[]{:S(2)}) async-start(f32[16,1,128]{2,1,0:T(1,128)} %get-tuple-element.31), calls=%async_computation | async-start | bytes 16384 | tf_op jit(solution)/shard_map/all_to_all | solution.py:354

commit v4 on v3

--- a/solution.py
+++ b/solution.py
@@ -10,7 +10,7 @@
 GROW = 1.0 / SHRINK
 SLOT = 32
 LOCAL = 4
-GROUP = 16
+GROUP = 8
 VMEM_LIMIT = 40 * 2**20
 WHOLE = pl.BlockSpec(memory_space=pltpu.VMEM)
 
@@ -104,7 +104,7 @@
             env[row * SLOT : (row + 1) * SLOT, low : low + width] = kept.astype(jnp.bfloat16)
 
 
-def apply_steps(env, coupling, right, extended, contracted, mixed):
+def apply_steps(env, coupling, right, extended, contracted, mixed, image):
     groups, depth, width = contracted.shape
     lanes = right.shape[1]
     group = width // lanes
@@ -121,35 +121,41 @@
                 row % group * lanes : (row % group + 1) * lanes,
             ] = product[row * SLOT : (row + 1) * SLOT, state * lanes : (state + 1) * lanes]
 
-    @pl.loop(0, groups)
-    def _(step):
+    def mix(step):
         product = jnp.dot(coupling[...], contracted[step], preferred_element_type=jnp.float32)
         product = product.astype(jnp.bfloat16)
         for part in range(group):
-            place = pl.ds(pl.multiple_of((group * step + part) * states, states), states)
+            start = (group * step + part) * states
             for bond in range(bonds):
-                mixed[place, bond * lanes : (bond + 1) * lanes] = product[
+                mixed[start : start + states, bond * lanes : (bond + 1) * lanes] = product[
                     bond * states : (bond + 1) * states, part * lanes : (part + 1) * lanes
                 ]
 
-    return SHRINK * jnp.dot(mixed[...], right[...], preferred_element_type=jnp.float32)
+    def finish(step):
+        place = slice(group * step * states, group * (step + 1) * states)
+        image[place, :] = SHRINK * jnp.dot(
+            mixed[place, :], right[...], preferred_element_type=jnp.float32
+        )
+
+    mix(0)
+    for step in range(groups):
+        if step + 1 < groups:
+            mix(step + 1)
+        finish(step)
 
 
 def column_sum(x):
     return jnp.sum(x, axis=0, keepdims=True)
 
 
-def send_half(image, states):
-    lanes = image.shape[1]
-    pieces = image.reshape(image.shape[0] // states, states, lanes)
-    low, high = pieces[:, : states // 2, :], pieces[:, states // 2 :, :]
-    first = lax.axis_index("mpo") == 0
-    return jnp.where(first, high, low), jnp.where(first, low, high)
+def state_half(image, states, index):
+    pieces = image.reshape(image.shape[0] // states, states, image.shape[1])
+    return jnp.where(index == 0, pieces[:, : states // 2, :], pieces[:, states // 2 :, :])
 
 
 def first_kernel(
     env, coupling, right, vector, direct_in, passed_in,
-    image, image_rows, sent, kept, sums,
+    image, image_rows, sums,
     wide, extended, contracted, mixed,
 ):
     rows = extended.shape[0] // 3
@@ -162,14 +168,13 @@
             extended[pl.ds(place, rows), columns] = piece
 
         states_apart(wide, rows, states, store)
-    out = apply_steps(env, coupling, right, extended, contracted, mixed)
-    image[...] = out
+    apply_steps(env, coupling, right, extended, contracted, mixed, image)
+    out = image[...]
 
     def store_rows(columns, piece):
         image_rows[:, columns] = piece
 
     states_apart(image, half // states, states, store_rows)
-    sent[...], kept[...] = send_half(out, states)
     start = pl.multiple_of(lax.axis_index("mpo") * half, half)
     own = vector[pl.ds(start, half), :].astype(jnp.float32)
     lanes = out.shape[1]
@@ -182,7 +187,7 @@
 
 def second_kernel(
     env, coupling, right, mine_in, other_in, direct_in, passed_in, first, vector, sums,
-    sent, kept, totals,
+    image, sent, totals,
     extended, contracted, mixed,
 ):
     rows = direct_in.shape[0]
@@ -196,8 +201,11 @@
     extended[pl.ds(other, part), :] = other_in[...]
     extended[pl.ds(direct, rows), :] = direct_in[...]
     extended[pl.ds(passed, rows), :] = passed_in[...]
-    out = apply_steps(env, coupling, right, extended, contracted, mixed)
-    sent[...], kept[...] = send_half(out, half // part)
+    apply_steps(env, coupling, right, extended, contracted, mixed, image)
+    out = image[...]
+    states = half // part
+    sent[0:part] = state_half(first[...], states, 1 - core)
+    sent[part : 2 * part] = state_half(out, states, 1 - core)
     own = vector[pl.ds(pl.multiple_of(core * half, half), half), :].astype(jnp.float32)
     lanes = out.shape[1]
     columns = jnp.concatenate(
@@ -205,25 +213,20 @@
         + [jnp.zeros((3, lanes), jnp.float32)],
         axis=0,
     )
-    lane = lax.broadcasted_iota(jnp.int32, columns.shape, 1)
-    row = lax.broadcasted_iota(jnp.int32, columns.shape, 0)
-    spread = jnp.where(lane == row, jnp.sum(columns, axis=1, keepdims=True), 0.0)
-    totals[...] = jnp.broadcast_to(column_sum(spread)[None], totals.shape)
+    totals[...] = jnp.broadcast_to(columns[None], totals.shape)
 
 
 def final_kernel(
-    entries, first_kept, first_got, second_kept, second_got, vector, gathered,
+    entries, first, second, got, vector, gathered,
     image_two, basis_two, projected,
 ):
-    half, half_states, lanes = first_kept.shape
+    half = got.shape[0] // 2
+    half_states = got.shape[1]
+    states = 2 * half_states
+    lanes = first.shape[1]
     core = lax.axis_index("mpo")
-    totals = column_sum(jnp.sum(gathered[...], axis=0))
-    lane = lax.broadcasted_iota(jnp.int32, totals.shape, 1)
-
-    def total(index):
-        return jnp.sum(jnp.where(lane == index, totals, 0.0), axis=1, keepdims=True)
-
-    s_aa, s_ay, s_yy, s_az, s_yz = (total(i) for i in range(5))
+    totals = jnp.sum(jnp.sum(gathered[...], axis=0), axis=1, keepdims=True)
+    s_aa, s_ay, s_yy, s_az, s_yz = (totals[i : i + 1, :] for i in range(5))
     scale_sq = s_aa / entries + EPSILON
     shrunk = s_ay / entries / scale_sq
     residual_sq = jnp.maximum(s_yy - 2.0 * shrunk * s_ay + shrunk * shrunk * s_aa, 0.0)
@@ -237,17 +240,16 @@
     projected[...] = jnp.where(r == c, diagonal, residual_norm)
 
     size = half * half_states
-    wide = vector[...].astype(jnp.float32).reshape(2 * half, 2 * half_states, lanes)
-    own = jnp.where(core == 0, wide[:, :half_states, :], wide[:, half_states:, :])
-    own = own.reshape(2 * size, lanes)
+    own = state_half(vector[...].astype(jnp.float32), states, core).reshape(2 * size, lanes)
     ours = jnp.where(core == 0, own[:size, :], own[size:, :])
     theirs = jnp.where(core == 0, own[size:, :], own[:size, :])
-    for index, y_ref, z_ref, a in (
-        (core, first_kept, second_kept, ours),
-        (1 - core, first_got, second_got, theirs),
+    mine = [state_half(image[...], states, core) for image in (first, second)]
+    for index, (y, z), a in (
+        (core, mine, ours),
+        (1 - core, (got[0:half], got[half : 2 * half]), theirs),
     ):
-        y = y_ref[...].reshape(size, lanes)
-        z = z_ref[...].reshape(size, lanes)
+        y = y.reshape(size, lanes)
+        z = z.reshape(size, lanes)
         place = pl.ds(pl.multiple_of(index * size, size), size)
         basis_two[place, :] = ((y - shrunk * a) * factor).astype(jnp.bfloat16)
         image_two[place, :] = ((z - shrunk * y) * (factor * GROW)).astype(jnp.bfloat16)
@@ -318,15 +320,12 @@
         ((half // GROUP, states * SLOT, GROUP * columns), bf16),
         ((size, bonds * columns), bf16),
     )
-    half_shape = ((half, half_states, columns), f32)
-    first, first_rows, first_sent, first_kept, sums = call(
+    first, first_rows, sums = call(
         first_kernel,
         (env, coupling, right, flat, direct_one, passed_one),
         (
             ((size, columns), f32),
             ((half, states * columns), bf16),
-            half_shape,
-            half_shape,
             ((8, columns), f32),
         ),
         (((rows * states, columns), f32),) + work,
@@ -340,17 +339,20 @@
         axis=0,
     )
     direct_two = swap_blocks(block_rows)
-    first_got = swap_cores(first_sent)
     passed_two = swap_cores(direct_two)
 
-    second_sent, second_kept, totals = call(
+    second, sent, totals = call(
         second_kernel,
         (env, coupling, right, first_rows, other_rows, direct_two, passed_two, first, flat, sums),
-        (half_shape, half_shape, ((peers, 1, columns), f32)),
+        (
+            ((size, columns), f32),
+            ((2 * half, half_states, columns), f32),
+            ((peers, 8, columns), f32),
+        ),
         work,
         "second_image",
     )
-    second_got = swap_cores(second_sent)
+    got = swap_cores(sent)
     gathered = lax.all_to_all(totals, axes, 0, 0)
 
     def finish(*refs):
@@ -358,7 +360,7 @@
 
     image_two, basis_two, projected = call(
         finish,
-        (first_kept, first_got, second_kept, second_got, flat, gathered),
+        (first, second, got, flat, gathered),
         (
             ((rows * half_states, columns), bf16),
             ((rows * half_states, columns), bf16),

time: 47.8 us -> 46.4 us (0.971)
  blocking collectives: 0 us -> 13 us
  starting transfers between devices: 16.6 us -> 9.92 us
  waiting for transfers between devices: 14 us -> 8.22 us
  Pallas kernels: 13.9 us -> 12.1 us
    all_to_all x0 -> x1, blocking collectives: none -> 13 us  [per_device(): gathered = lax.all_to_all(totals, axes, 0, 0)]
    all_to_all x1 -> x0, waiting for transfers between devices: 6.32 us -> none  [per_device(): gathered = lax.all_to_all(totals, axes, 0, 0)]
    all_to_all x1 -> x0, starting transfers between devices: 6.27 us -> none  [per_device(): gathered = lax.all_to_all(totals, axes, 0, 0)]
    pallas_call x4, Pallas kernels: 13.9 us -> 12.1 us  [call(): pl.pallas_call(kernel, out_shape=tuple((jax.ShapeDtypeStruct(shape, dtype...]
    ppermute x6 -> x5, waiting for transfers between devices: 3.18 us -> 3.69 us  [swap_cores(): return lax.ppermute(x, 'mpo', [(0, 1), (1, 0)])]
    ppermute x6 -> x5, starting transfers between devices: 1.59 us -> 1.14 us  [swap_cores(): return lax.ppermute(x, 'mpo', [(0, 1), (1, 0)])]
  transfers between devices with their start and end apart: 9 -> 7, of which waited for: 6 -> 5; matrix products, arithmetic and copies ran while one was open for 3% -> 3% of each run, Pallas kernels for 16% -> 5%
where the time goes in v4:
time: 46.4 us; the launch traced here: 46.2 us
  blocking collectives  13 us (28%)
  Pallas kernels  12.1 us (26%)
  starting transfers between devices  9.92 us (21%)
  waiting for transfers between devices  8.22 us (18%)
  other arithmetic  1.39 us (3%)
  local copies, waits for them, and re-layouts  0.83 us (2%)
  between operations  0.75 us (2%)
    all_to_all x1, blocking collectives, per_device(): gathered = lax.all_to_all(totals, axes, 0, 0)  13 us
    pallas_call x4, Pallas kernels, call(): pl.pallas_call(kernel, out_shape=tuple((jax.ShapeDtypeStruct(shape, dtype...  12.1 us
    ppermute x2, starting transfers between devices, swap_blocks(): return lax.ppermute(x, ('brow', 'mpo'), pairs)  8.78 us
    ppermute x2, waiting for transfers between devices, swap_blocks(): return lax.ppermute(x, ('brow', 'mpo'), pairs)  4.54 us
    ppermute x5, waiting for transfers between devices, swap_cores(): return lax.ppermute(x, 'mpo', [(0, 1), (1, 0)])  3.69 us
    concatenate x1, other arithmetic, per_device(): both = jnp.concatenate([mpo_left, mpo_right], axis=0)  1.2 us
    ppermute x5, starting transfers between devices, swap_cores(): return lax.ppermute(x, 'mpo', [(0, 1), (1, 0)])  1.14 us
  transfers between devices with their start and end apart: 7, of which 5 were waited for; matrix products, arithmetic and copies ran while one was open for 3% of the time, Pallas kernels for 5%

profile of v4, /device:TPU:0, one launch (start us, length us, event | category | flops | bytes accessed | tf_op | source)
XLA Modules:
  0.0 46.2 jit_solution(7395844567158007663)
XLA Ops:
  0.6 4.9 %collective-permute-start = (bf16[1024,128]{1,0:T(8,128)(2,1)}, bf16[1024,128]{1,0:T(8,128)(2,1)S(1)}, u32[]{:S(2)}, u32[]{:S(2)}) collective-permute-start(bf16[1024,128]{1,0:T(8,128)(2,1)} %bitcast.9), channel_id=1, source_target_pairs={{0,4},{4,0},{5,9},{8,12},{9,5},{12,8},{2,6},{6,2},{7,11},{10,14},{... | collective-permute-start | bytes 786440 | tf_op jit(solution)/shard_map/ppermute | solution.py:29
  5.6 0.1 collective-permute-start.1
  5.7 0.0 copy-start.3
  5.7 0.7 %copy-done.3 = s32[256]{0:T(256)S(1)} copy-done((s32[256]{0:T(256)S(1)}, s32[256]{0:T(256)}, u32[]{:S(2)}) %copy-start.3) | copy-done | bytes 1048
  6.3 0.1 pad_add_fusion
  6.4 0.1 dynamic_slice.6
  6.5 0.1 dynamic_slice.7
  6.6 0.0 copy-start.2
  6.6 1.2 %pad_maximum_fusion = f32[52,26,4,4]{1,3,2,0:T(4,128)S(1)} fusion(f32[26,26,4,4]{1,3,2,0:T(4,128)} %param.10, f32[26,26,4,4]{1,3,2,0:T(4,128)} %param.9), kind=kLoop, calls=%fused_computation | loop fusion | flops 21632 | bytes 173056 | tf_op jit(solution)/shard_map/concatenate | solution.py:294
  7.8 0.1 compare_convert_fusion.mask
  7.8 0.0 collective-permute-done.1.env_there
  7.9 0.0 copy-done.2
  7.9 0.0 copy-start
  7.9 0.0 copy-start.1
  7.9 2.1 %operands.1 = (bf16[1024,192]{1,0:T(8,128)(2,1)S(1)}, bf16[416,512]{1,0:T(8,128)(2,1)S(1)}) custom-call(bf16[13,64,192]{2,1,0:T(8,128)(2,1)S(1)} %copy-done.2, bf16[13,64,192]{2,1,0:T(8,128)(2,1)S(1)} %collective-permute-done.1.env_there, f32[32,192]{1,0:T(8,128)S(1)} %compare_convert_fusion.mask, f32[832,26]{1,0:T(8,128)S(1)} %bitcast.13), custom_call_target="tpu_custom_call" | custom-call | flops 4000000000 | bytes 8388608 | tf_op jit(solution)/shard_map/operands/pallas_call | solution.py:259
  10.0 0.1 collective-permute-done.direct_in
  10.1 0.4 collective-permute-start.2
  10.6 1.2 %collective-permute-done.2.passed_in = bf16[1024,128]{1,0:T(8,128)(2,1)S(1)} collective-permute-done((bf16[1024,128]{1,0:T(8,128)(2,1)S(1)}, bf16[1024,128]{1,0:T(8,128)(2,1)S(1)}, u32[]{:S(2)}, u32[]{:S(2)}) %collective-permute-start.2) | collective-permute-done | bytes 262176 | tf_op jit(solution)/shard_map/ppermute | solution.py:19
  11.7 0.0 copy-done
  11.7 0.0 copy-done.1
  11.7 4.8 %first_image.1 = (f32[512,128]{1,0:T(8,128)S(1)}, bf16[32,2048]{1,0:T(8,128)(2,1)S(1)}, f32[8,128]{1,0:T(8,128)S(1)}) custom-call(bf16[1024,192]{1,0:T(8,128)(2,1)S(1)} %get-tuple-element.19.env, bf16[416,512]{1,0:T(8,128)(2,1)S(1)} %get-tuple-element.20.coupling, bf16[3328,128]{1,0:T(8,128)(2,1)S(1)} %bitcast.7, bf16[1024,128]{1,0:T(8,128)(2,1)S(1)} %bitcast.10, ...), custom_call_target="tpu_custom_call" | custom-call | tf_op jit(solution)/shard_map/first_image/pallas_call | solution.py:259
  16.5 0.4 collective-permute-start.3
  17.0 1.0 %collective-permute-done.3.other_in = bf16[32,2048]{1,0:T(8,128)(2,1)S(1)} collective-permute-done((bf16[32,2048]{1,0:T(8,128)(2,1)S(1)}, bf16[32,2048]{1,0:T(8,128)(2,1)S(1)}, u32[]{:S(2)}, u32[]{:S(2)}) %collective-permute-start.3) | collective-permute-done | bytes 131104 | tf_op jit(solution)/shard_map/ppermute | solution.py:19
  18.0 3.8 %collective-permute-start.4 = (bf16[64,2048]{1,0:T(8,128)(2,1)S(1)}, bf16[64,2048]{1,0:T(8,128)(2,1)S(1)}, u32[]{:S(2)}, u32[]{:S(2)}) collective-permute-start(bf16[64,2048]{1,0:T(8,128)(2,1)S(1)} %pad_maximum_fusion.1), channel_id=1, source_target_pairs={{0,4},{4,0},{5,9},{8,12},{9,5},{12,8},{2,6},{6,2},{7,11},{10,14},{... | collective-permute-start | bytes 786440 | tf_op jit(solution)/shard_map/ppermute | solution.py:29
  21.9 4.4 %collective-permute-done.4.direct_in = bf16[64,2048]{1,0:T(8,128)(2,1)S(1)} collective-permute-done((bf16[64,2048]{1,0:T(8,128)(2,1)S(1)}, bf16[64,2048]{1,0:T(8,128)(2,1)S(1)}, u32[]{:S(2)}, u32[]{:S(2)}) %collective-permute-start.4) | collective-permute-done | bytes 262176 | tf_op jit(solution)/shard_map/ppermute | solution.py:29
  26.3 0.0 collective-permute-start.5
  26.3 1.5 %collective-permute-done.5.passed_in = bf16[64,2048]{1,0:T(8,128)(2,1)S(1)} collective-permute-done((bf16[64,2048]{1,0:T(8,128)(2,1)S(1)}, bf16[64,2048]{1,0:T(8,128)(2,1)S(1)}, u32[]{:S(2)}, u32[]{:S(2)}) %collective-permute-start.5) | collective-permute-done | bytes 262176 | tf_op jit(solution)/shard_map/ppermute | solution.py:19
  27.8 4.2 %second_image.1 = (f32[512,128]{1,0:T(8,128)S(1)}, f32[64,8,128]{2,1,0:T(8,128)S(1)}, f32[16,8,128]{2,1,0:T(8,128)S(1)}) custom-call(bf16[1024,192]{1,0:T(8,128)(2,1)S(1)} %get-tuple-element.19.env, bf16[416,512]{1,0:T(8,128)(2,1)S(1)} %get-tuple-element.20.coupling, bf16[3328,128]{1,0:T(8,128)(2,1)S(1)} %bitcast.8, ...), custom_call_target="tpu_custom_call" | custom-call | tf_op jit(solution)/shard_map/second_image/pallas_call | solution.py:259
  32.0 0.2 collective-permute-start.6
  32.2 13.0 %all_to_all.5.refs_4_ = f32[16,8,128]{2,1,0:T(8,128)S(1)} all-to-all(f32[16,8,128]{2,1,0:T(8,128)S(1)} %get-tuple-element.27), channel_id=1, replica_groups=mesh['groups'=2,'brow'=4,'bcol'=2,'mpo'=2] {'brow','bcol','mpo'}, dimensions={0} | all-to-all | bytes 131072 | tf_op jit(solution)/shard_map/all_to_all | solution.py:356
  45.2 0.0 collective-permute-done.6.refs_2_
  45.2 1.0 %outputs.1 = (bf16[512,128]{1,0:T(8,128)(2,1)}, bf16[512,128]{1,0:T(8,128)(2,1)}, f32[2,2]{1,0:T(2,128)}) custom-call(f32[512,128]{1,0:T(8,128)S(1)} %get-tuple-element.22.first.refs_0_, f32[512,128]{1,0:T(8,128)S(1)} %get-tuple-element.25.refs_1_, f32[64,8,128]{2,1,0:T(8,128)S(1)} %collective-permute-done.6.refs_2_, bf16[1024,128]{1,0:T(8,128)(2,1)S(1)} %bitcast.12, ...), custom_call_target="tpu_custom_call" | custom-call | tf_op jit(solution)/shard_map/outputs/pallas_call | solution.py:259
  (3 shorter events, 0.0 us)
Async XLA Ops:
  0.6 9.5 %collective-permute-start = (bf16[1024,128]{1,0:T(8,128)(2,1)}, bf16[1024,128]{1,0:T(8,128)(2,1)S(1)}, u32[]{:S(2)}, u32[]{:S(2)}) collective-permute-start(bf16[1024,128]{1,0:T(8,128)(2,1)} %bitcast.9), channel_id=1, source_target_pairs={{0,4},{4,0},{5,9},{8,12},{9,5},{12,8},{2,6},{6,2},{7,11},{10,14},{... | collective-permute-start | bytes 786440 | tf_op jit(solution)/shard_map/ppermute | solution.py:29
  5.6 2.3 %collective-permute-start.1 = (bf16[13,64,192]{2,1,0:T(8,128)(2,1)}, bf16[13,64,192]{2,1,0:T(8,128)(2,1)S(1)}, u32[]{:S(2)}, u32[]{:S(2)}) collective-permute-start(bf16[13,64,192]{2,1,0:T(8,128)(2,1)} %env_mine.1), channel_id=1, source_target_pairs={{0,1},{1,0},{2,3},{3,2},{4,5},{5,4},{6,7},{7,6},{8,9},{9,8},{10,11... | collective-permute-start | bytes 958472 | tf_op jit(solution)/shard_map/ppermute | solution.py:19
  5.7 0.7 %copy-start.3 = (s32[256]{0:T(256)S(1)}, s32[256]{0:T(256)}, u32[]{:S(2)}) copy-start(s32[256]{0:T(256)} %param.11) | copy-start | bytes 3076
  6.6 1.3 %copy-start.2 = (bf16[13,64,192]{2,1,0:T(8,128)(2,1)S(1)}, bf16[13,64,192]{2,1,0:T(8,128)(2,1)}, u32[]{:S(2)}) copy-start(bf16[13,64,192]{2,1,0:T(8,128)(2,1)} %env_mine.1) | copy-start | bytes 958468
  7.9 3.9 %copy-start = (bf16[26,128,128]{2,1,0:T(8,128)(2,1)S(1)}, bf16[26,128,128]{2,1,0:T(8,128)(2,1)}, u32[]{:S(2)}) copy-start(bf16[26,128,128]{2,1,0:T(8,128)(2,1)} %param.8) | copy-start | bytes 2555908
  7.9 3.9 %copy-start.1 = (bf16[64,16,128]{2,1,0:T(8,128)(2,1)S(1)}, bf16[64,16,128]{2,1,0:T(8,128)(2,1)}, u32[]{:S(2)}) copy-start(bf16[64,16,128]{2,1,0:T(8,128)(2,1)} %param.6) | copy-start | bytes 786436
  10.1 1.6 %collective-permute-start.2 = (bf16[1024,128]{1,0:T(8,128)(2,1)S(1)}, bf16[1024,128]{1,0:T(8,128)(2,1)S(1)}, u32[]{:S(2)}, u32[]{:S(2)}) collective-permute-start(bf16[1024,128]{1,0:T(8,128)(2,1)S(1)} %collective-permute-done.direct_in), channel_id=1, source_target_pairs={{0,1},{1,0},{2,3},{3,2},{4,5},{5,4},{6,7},{7,6},{8,9},{9,8},{10,11... | collective-permute-start | bytes 786440 | tf_op jit(solution)/shard_map/ppermute | solution.py:19
  16.5 1.4 %collective-permute-start.3 = (bf16[32,2048]{1,0:T(8,128)(2,1)S(1)}, bf16[32,2048]{1,0:T(8,128)(2,1)S(1)}, u32[]{:S(2)}, u32[]{:S(2)}) collective-permute-start(bf16[32,2048]{1,0:T(8,128)(2,1)S(1)} %get-tuple-element.23.mine_in), channel_id=1, source_target_pairs={{0,1},{1,0},{2,3},{3,2},{4,5},{5,4},{6,7},{7,6},{8,9},{9,8},{10,11... | collective-permute-start | bytes 393224 | tf_op jit(solution)/shard_map/ppermute | solution.py:19
  18.0 8.3 %collective-permute-start.4 = (bf16[64,2048]{1,0:T(8,128)(2,1)S(1)}, bf16[64,2048]{1,0:T(8,128)(2,1)S(1)}, u32[]{:S(2)}, u32[]{:S(2)}) collective-permute-start(bf16[64,2048]{1,0:T(8,128)(2,1)S(1)} %pad_maximum_fusion.1), channel_id=1, source_target_pairs={{0,4},{4,0},{5,9},{8,12},{9,5},{12,8},{2,6},{6,2},{7,11},{10,14},{... | collective-permute-start | bytes 786440 | tf_op jit(solution)/shard_map/ppermute | solution.py:29
  26.3 1.5 %collective-permute-start.5 = (bf16[64,2048]{1,0:T(8,128)(2,1)S(1)}, bf16[64,2048]{1,0:T(8,128)(2,1)S(1)}, u32[]{:S(2)}, u32[]{:S(2)}) collective-permute-start(bf16[64,2048]{1,0:T(8,128)(2,1)S(1)} %collective-permute-done.4.direct_in), channel_id=1, source_target_pairs={{0,1},{1,0},{2,3},{3,2},{4,5},{5,4},{6,7},{7,6},{8,9},{9,8},{10,11... | collective-permute-start | bytes 786440 | tf_op jit(solution)/shard_map/ppermute | solution.py:19
  32.0 13.2 %collective-permute-start.6 = (f32[64,8,128]{2,1,0:T(8,128)S(1)}, f32[64,8,128]{2,1,0:T(8,128)S(1)}, u32[]{:S(2)}, u32[]{:S(2)}) collective-permute-start(f32[64,8,128]{2,1,0:T(8,128)S(1)} %get-tuple-element.26), channel_id=1, source_target_pairs={{0,1},{1,0},{2,3},{3,2},{4,5},{5,4},{6,7},{7,6},{8,9},{9,8},{10,11... | collective-permute-start | bytes 786440 | tf_op jit(solution)/shard_map/ppermute | solution.py:19

commit v5 on v4

--- a/solution.py
+++ b/solution.py
@@ -19,13 +19,20 @@
     return lax.ppermute(x, "mpo", [(0, 1), (1, 0)])
 
 
+def neighbours(blocks, odd):
+    pairs = []
+    for i in range(blocks):
+        partner = (i + 1 if i % 2 else i - 1) if odd else i ^ 1
+        if 0 <= partner < blocks:
+            pairs.append((i, partner))
+    return pairs
+
+
 def swap_blocks(x):
     blocks = lax.axis_size("brow")
-    pairs = []
-    for i in range(blocks):
-        for core, partner in ((0, i ^ 1), (1, i + 1 if i % 2 else i - 1)):
-            if 0 <= partner < blocks:
-                pairs.append((2 * i + core, 2 * partner + core))
+    pairs = [
+        (2 * i + core, 2 * j + core) for core in range(2) for i, j in neighbours(blocks, core == 1)
+    ]
     return lax.ppermute(x, ("brow", "mpo"), pairs)
 
 
@@ -186,21 +193,22 @@
 
 
 def second_kernel(
-    env, coupling, right, mine_in, other_in, direct_in, passed_in, first, vector, sums,
+    env, coupling, right, own_here, own_there, even_here, even_there, odd_here, odd_there,
+    first, vector, sums,
     image, sent, totals,
     extended, contracted, mixed,
 ):
-    rows = direct_in.shape[0]
-    part = rows // 2
+    part = own_here.shape[0]
+    rows = 2 * part
     half = first.shape[0]
     core = lax.axis_index("mpo")
-    direct, passed = halo_places(rows)
-    mine = pl.multiple_of(rows + core * part, part)
-    other = pl.multiple_of(rows + (1 - core) * part, part)
-    extended[pl.ds(mine, part), :] = mine_in[...]
-    extended[pl.ds(other, part), :] = other_in[...]
-    extended[pl.ds(direct, rows), :] = direct_in[...]
-    extended[pl.ds(passed, rows), :] = passed_in[...]
+    even = lax.rem(lax.axis_index("brow"), 2) == 0
+    above, below = jnp.where(even, 2 * rows, 0), jnp.where(even, 0, 2 * rows)
+    for base, here, there in (
+        (rows, own_here, own_there), (above, even_here, even_there), (below, odd_here, odd_there)
+    ):
+        extended[pl.ds(pl.multiple_of(base + core * part, part), part), :] = here[...]
+        extended[pl.ds(pl.multiple_of(base + (1 - core) * part, part), part), :] = there[...]
     apply_steps(env, coupling, right, extended, contracted, mixed, image)
     out = image[...]
     states = half // part
@@ -213,7 +221,10 @@
         + [jnp.zeros((3, lanes), jnp.float32)],
         axis=0,
     )
-    totals[...] = jnp.broadcast_to(columns[None], totals.shape)
+    lane = lax.broadcasted_iota(jnp.int32, columns.shape, 1)
+    row = lax.broadcasted_iota(jnp.int32, columns.shape, 0)
+    spread = jnp.where(lane == row, jnp.sum(columns, axis=1, keepdims=True), 0.0)
+    totals[...] = jnp.broadcast_to(column_sum(spread)[None], totals.shape)
 
 
 def final_kernel(
@@ -225,8 +236,11 @@
     states = 2 * half_states
     lanes = first.shape[1]
     core = lax.axis_index("mpo")
-    totals = jnp.sum(jnp.sum(gathered[...], axis=0), axis=1, keepdims=True)
-    s_aa, s_ay, s_yy, s_az, s_yz = (totals[i : i + 1, :] for i in range(5))
+    totals = jnp.sum(gathered[...], axis=0)
+    lane = lax.broadcasted_iota(jnp.int32, totals.shape, 1)
+    s_aa, s_ay, s_yy, s_az, s_yz = (
+        jnp.sum(jnp.where(lane == i, totals, 0.0), axis=1, keepdims=True) for i in range(5)
+    )
     scale_sq = s_aa / entries + EPSILON
     shrunk = s_ay / entries / scale_sq
     residual_sq = jnp.maximum(s_yy - 2.0 * shrunk * s_ay + shrunk * shrunk * s_aa, 0.0)
@@ -332,22 +346,19 @@
         "first_image",
     )
 
-    other_rows = swap_cores(first_rows)
-    mine_first = core == 0
-    block_rows = jnp.concatenate(
-        [jnp.where(mine_first, first_rows, other_rows), jnp.where(mine_first, other_rows, first_rows)],
-        axis=0,
-    )
-    direct_two = swap_blocks(block_rows)
-    passed_two = swap_cores(direct_two)
+    blocks = lax.axis_size("brow")
+    even_rows = lax.ppermute(first_rows, "brow", neighbours(blocks, False))
+    odd_rows = lax.ppermute(first_rows, "brow", neighbours(blocks, True))
+    pieces = [(x, swap_cores(x)) for x in (first_rows, even_rows, odd_rows)]
+    pieces = [x for pair in pieces for x in pair]
 
     second, sent, totals = call(
         second_kernel,
-        (env, coupling, right, first_rows, other_rows, direct_two, passed_two, first, flat, sums),
+        (env, coupling, right, *pieces, first, flat, sums),
         (
             ((size, columns), f32),
             ((2 * half, half_states, columns), f32),
-            ((peers, 8, columns), f32),
+            ((peers, 1, columns), f32),
         ),
         work,
         "second_image",

time: 46.4 us -> 43 us (0.927)
  blocking collectives: 13 us -> 10.3 us
  waiting for transfers between devices: 8.22 us -> 5.63 us
  starting transfers between devices: 9.92 us -> 11.6 us
    ppermute x0 -> x2, starting transfers between devices: none -> 5.49 us  [the longest x1 4.83 us: per_device(): even_rows = lax.ppermute(first_rows, 'brow', neighbours(blocks, False))]
    ppermute x2 -> x1, waiting for transfers between devices: 4.54 us -> 0.12 us  [swap_blocks(): return lax.ppermute(x, ('brow', 'mpo'), pairs)]
    ppermute x2 -> x1, starting transfers between devices: 8.78 us -> 4.93 us  [swap_blocks(): return lax.ppermute(x, ('brow', 'mpo'), pairs)]
    ppermute x0 -> x2, waiting for transfers between devices: none -> 3 us  [the longest x1 3 us: per_device(): even_rows = lax.ppermute(first_rows, 'brow', neighbours(blocks, False))]
    all_to_all x1, blocking collectives: 13 us -> 10.3 us  [per_device(): gathered = lax.all_to_all(totals, axes, 0, 0)]
    ppermute x5 -> x6, waiting for transfers between devices: 3.69 us -> 2.51 us  [swap_cores(): return lax.ppermute(x, 'mpo', [(0, 1), (1, 0)])]
    ppermute x5 -> x6, starting transfers between devices: 1.14 us -> 1.21 us  [swap_cores(): return lax.ppermute(x, 'mpo', [(0, 1), (1, 0)])]
  transfers between devices with their start and end apart: 7 -> 9, of which waited for: 5 -> 4; matrix products, arithmetic and copies ran while one was open for 3% -> 4% of each run, Pallas kernels for 5% -> 5%
where the time goes in v5:
time: 43 us; the launch traced here: 42.8 us
  Pallas kernels  12.4 us (29%)
  starting transfers between devices  11.6 us (27%)
  blocking collectives  10.3 us (24%)
  waiting for transfers between devices  5.63 us (13%)
  other arithmetic  1.35 us (3%)
  local copies, waits for them, and re-layouts  0.83 us (2%)
  between operations  0.73 us (2%)
    pallas_call x4, Pallas kernels, call(): pl.pallas_call(kernel, out_shape=tuple((jax.ShapeDtypeStruct(shape, dtype...  12.4 us
    all_to_all x1, blocking collectives, per_device(): gathered = lax.all_to_all(totals, axes, 0, 0)  10.3 us
    ppermute x1, starting transfers between devices, swap_blocks(): return lax.ppermute(x, ('brow', 'mpo'), pairs)  4.93 us
    ppermute x1, starting transfers between devices, per_device(): even_rows = lax.ppermute(first_rows, 'brow', neighbours(blocks, False))  4.83 us
    ppermute x1, waiting for transfers between devices, per_device(): even_rows = lax.ppermute(first_rows, 'brow', neighbours(blocks, False))  3 us
    ppermute x6, waiting for transfers between devices, swap_cores(): return lax.ppermute(x, 'mpo', [(0, 1), (1, 0)])  2.51 us
    ppermute x6, starting transfers between devices, swap_cores(): return lax.ppermute(x, 'mpo', [(0, 1), (1, 0)])  1.21 us
    concatenate x1, other arithmetic, per_device(): both = jnp.concatenate([mpo_left, mpo_right], axis=0)  1.2 us
  transfers between devices with their start and end apart: 9, of which 4 were waited for; matrix products, arithmetic and copies ran while one was open for 4% of the time, Pallas kernels for 5%

profile of v5, /device:TPU:0, one launch (start us, length us, event | category | flops | bytes accessed | tf_op | source)
XLA Modules:
  0.0 42.8 jit_solution(16711481979900224648)
XLA Ops:
  0.6 4.9 %collective-permute-start = (bf16[1024,128]{1,0:T(8,128)(2,1)}, bf16[1024,128]{1,0:T(8,128)(2,1)S(1)}, u32[]{:S(2)}, u32[]{:S(2)}) collective-permute-start(bf16[1024,128]{1,0:T(8,128)(2,1)} %bitcast.9), channel_id=1, source_target_pairs={{0,4},{4,0},{8,12},{12,8},{5,9},{9,5},{2,6},{6,2},{10,14},{14,10},... | collective-permute-start | bytes 786440 | tf_op jit(solution)/shard_map/ppermute | solution.py:36
  5.6 0.1 collective-permute-start.1
  5.7 0.0 copy-start.3
  5.7 0.7 %copy-done.3 = s32[256]{0:T(256)S(1)} copy-done((s32[256]{0:T(256)S(1)}, s32[256]{0:T(256)}, u32[]{:S(2)}) %copy-start.3) | copy-done | bytes 1048
  6.3 0.1 pad_add_fusion
  6.4 0.1 dynamic_slice.6
  6.5 0.1 dynamic_slice.7
  6.6 0.0 copy-start.2
  6.6 1.2 %pad_maximum_fusion = f32[52,26,4,4]{1,3,2,0:T(4,128)S(1)} fusion(f32[26,26,4,4]{1,3,2,0:T(4,128)} %param.10, f32[26,26,4,4]{1,3,2,0:T(4,128)} %param.9), kind=kLoop, calls=%fused_computation | loop fusion | flops 21632 | bytes 173056 | tf_op jit(solution)/shard_map/concatenate | solution.py:308
  7.8 0.1 compare_convert_fusion.mask
  7.8 0.0 collective-permute-done.1.env_there
  7.9 0.0 copy-done.2
  7.9 0.0 copy-start
  7.9 0.0 copy-start.1
  7.9 2.1 %operands.1 = (bf16[1024,192]{1,0:T(8,128)(2,1)S(1)}, bf16[416,512]{1,0:T(8,128)(2,1)S(1)}) custom-call(bf16[13,64,192]{2,1,0:T(8,128)(2,1)S(1)} %copy-done.2, bf16[13,64,192]{2,1,0:T(8,128)(2,1)S(1)} %collective-permute-done.1.env_there, f32[32,192]{1,0:T(8,128)S(1)} %compare_convert_fusion.mask, f32[832,26]{1,0:T(8,128)S(1)} %bitcast.13), custom_call_target="tpu_custom_call" | custom-call | flops 4000000000 | bytes 8388608 | tf_op jit(solution)/shard_map/operands/pallas_call | solution.py:273
  10.0 0.1 collective-permute-done.direct_in
  10.1 0.4 %collective-permute-start.2 = (bf16[1024,128]{1,0:T(8,128)(2,1)S(1)}, bf16[1024,128]{1,0:T(8,128)(2,1)S(1)}, u32[]{:S(2)}, u32[]{:S(2)}) collective-permute-start(bf16[1024,128]{1,0:T(8,128)(2,1)S(1)} %collective-permute-done.direct_in), channel_id=1, source_target_pairs={{0,1},{1,0},{2,3},{3,2},{4,5},{5,4},{6,7},{7,6},{8,9},{9,8},{10,11... | collective-permute-start | bytes 786440 | tf_op jit(solution)/shard_map/ppermute | solution.py:19
  10.6 1.2 %collective-permute-done.2.passed_in = bf16[1024,128]{1,0:T(8,128)(2,1)S(1)} collective-permute-done((bf16[1024,128]{1,0:T(8,128)(2,1)S(1)}, bf16[1024,128]{1,0:T(8,128)(2,1)S(1)}, u32[]{:S(2)}, u32[]{:S(2)}) %collective-permute-start.2) | collective-permute-done | bytes 262176 | tf_op jit(solution)/shard_map/ppermute | solution.py:19
  11.7 0.0 copy-done
  11.7 0.0 copy-done.1
  11.7 5.0 %first_image.1 = (f32[512,128]{1,0:T(8,128)S(1)}, bf16[32,2048]{1,0:T(8,128)(2,1)S(1)}, f32[8,128]{1,0:T(8,128)S(1)}) custom-call(bf16[1024,192]{1,0:T(8,128)(2,1)S(1)} %get-tuple-element.19.env, bf16[416,512]{1,0:T(8,128)(2,1)S(1)} %get-tuple-element.20.coupling, bf16[3328,128]{1,0:T(8,128)(2,1)S(1)} %bitcast.7, bf16[1024,128]{1,0:T(8,128)(2,1)S(1)} %bitcast.10, ...), custom_call_target="tpu_custom_call" | custom-call | tf_op jit(solution)/shard_map/first_image/pallas_call | solution.py:273
  16.7 0.7 %collective-permute-start.6 = (bf16[32,2048]{1,0:T(8,128)(2,1)S(1)}, bf16[32,2048]{1,0:T(8,128)(2,1)S(1)}, u32[]{:S(2)}, u32[]{:S(2)}) collective-permute-start(bf16[32,2048]{1,0:T(8,128)(2,1)S(1)} %get-tuple-element.23.own_here), channel_id=1, source_target_pairs={{4,8},{8,4},{5,9},{9,5},{6,10},{10,6},{7,11},{11,7},{20,24},{24,20... | collective-permute-start | bytes 393224 | tf_op jit(solution)/shard_map/ppermute | solution.py:351
  17.4 4.8 %collective-permute-start.4 = (bf16[32,2048]{1,0:T(8,128)(2,1)S(1)}, bf16[32,2048]{1,0:T(8,128)(2,1)S(1)}, u32[]{:S(2)}, u32[]{:S(2)}) collective-permute-start(bf16[32,2048]{1,0:T(8,128)(2,1)S(1)} %get-tuple-element.23.own_here), channel_id=1, source_target_pairs={{0,4},{4,0},{8,12},{12,8},{1,5},{5,1},{9,13},{13,9},{2,6},{6,2},{1... | collective-permute-start | bytes 393224 | tf_op jit(solution)/shard_map/ppermute | solution.py:350
  22.2 0.0 collective-permute-start.3
  22.2 0.0 collective-permute-done.6.odd_here
  22.2 0.5 %collective-permute-start.7 = (bf16[32,2048]{1,0:T(8,128)(2,1)S(1)}, bf16[32,2048]{1,0:T(8,128)(2,1)S(1)}, u32[]{:S(2)}, u32[]{:S(2)}) collective-permute-start(bf16[32,2048]{1,0:T(8,128)(2,1)S(1)} %collective-permute-done.6.odd_here), channel_id=1, source_target_pairs={{0,1},{1,0},{2,3},{3,2},{4,5},{5,4},{6,7},{7,6},{8,9},{9,8},{10,11... | collective-permute-start | bytes 393224 | tf_op jit(solution)/shard_map/ppermute | solution.py:19
  22.7 3.0 %collective-permute-done.4.even_here = bf16[32,2048]{1,0:T(8,128)(2,1)S(1)} collective-permute-done((bf16[32,2048]{1,0:T(8,128)(2,1)S(1)}, bf16[32,2048]{1,0:T(8,128)(2,1)S(1)}, u32[]{:S(2)}, u32[]{:S(2)}) %collective-permute-start.4) | collective-permute-done | bytes 131104 | tf_op jit(solution)/shard_map/ppermute | solution.py:350
  25.7 0.0 collective-permute-start.5
  25.7 0.0 collective-permute-done.3.own_there
  25.7 0.0 collective-permute-done.7.odd_there
  25.7 1.3 %collective-permute-done.5.even_there = bf16[32,2048]{1,0:T(8,128)(2,1)S(1)} collective-permute-done((bf16[32,2048]{1,0:T(8,128)(2,1)S(1)}, bf16[32,2048]{1,0:T(8,128)(2,1)S(1)}, u32[]{:S(2)}, u32[]{:S(2)}) %collective-permute-start.5) | collective-permute-done | bytes 131104 | tf_op jit(solution)/shard_map/ppermute | solution.py:19
  27.1 4.4 %second_image.1 = (f32[512,128]{1,0:T(8,128)S(1)}, f32[64,8,128]{2,1,0:T(8,128)S(1)}, f32[16,1,128]{2,1,0:T(1,128)S(1)}) custom-call(bf16[1024,192]{1,0:T(8,128)(2,1)S(1)} %get-tuple-element.19.env, bf16[416,512]{1,0:T(8,128)(2,1)S(1)} %get-tuple-element.20.coupling, bf16[3328,128]{1,0:T(8,128)(2,1)S(1)} %bitcast.8, ...), custom_call_target="tpu_custom_call" | custom-call | tf_op jit(solution)/shard_map/second_image/pallas_call | solution.py:273
  31.5 0.2 collective-permute-start.8
  31.7 10.3 %all_to_all.5.refs_4_ = f32[16,1,128]{2,1,0:T(1,128)S(1)} all-to-all(f32[16,1,128]{2,1,0:T(1,128)S(1)} %get-tuple-element.27), channel_id=1, replica_groups=mesh['groups'=2,'brow'=4,'bcol'=2,'mpo'=2] {'brow','bcol','mpo'}, dimensions={0} | all-to-all | bytes 16384 | tf_op jit(solution)/shard_map/all_to_all | solution.py:367
  41.9 0.0 collective-permute-done.8.refs_2_
  41.9 0.9 %outputs.1 = (bf16[512,128]{1,0:T(8,128)(2,1)}, bf16[512,128]{1,0:T(8,128)(2,1)}, f32[2,2]{1,0:T(2,128)}) custom-call(f32[512,128]{1,0:T(8,128)S(1)} %get-tuple-element.22.first.refs_0_, f32[512,128]{1,0:T(8,128)S(1)} %get-tuple-element.25.refs_1_, f32[64,8,128]{2,1,0:T(8,128)S(1)} %collective-permute-done.8.refs_2_, bf16[1024,128]{1,0:T(8,128)(2,1)S(1)} %bitcast.12, ...), custom_call_target="tpu_custom_call" | custom-call | tf_op jit(solution)/shard_map/outputs/pallas_call | solution.py:273
  (1 shorter events, 0.0 us)
Async XLA Ops:
  0.6 9.5 %collective-permute-start = (bf16[1024,128]{1,0:T(8,128)(2,1)}, bf16[1024,128]{1,0:T(8,128)(2,1)S(1)}, u32[]{:S(2)}, u32[]{:S(2)}) collective-permute-start(bf16[1024,128]{1,0:T(8,128)(2,1)} %bitcast.9), channel_id=1, source_target_pairs={{0,4},{4,0},{8,12},{12,8},{5,9},{9,5},{2,6},{6,2},{10,14},{14,10},... | collective-permute-start | bytes 786440 | tf_op jit(solution)/shard_map/ppermute | solution.py:36
  5.6 2.3 %collective-permute-start.1 = (bf16[13,64,192]{2,1,0:T(8,128)(2,1)}, bf16[13,64,192]{2,1,0:T(8,128)(2,1)S(1)}, u32[]{:S(2)}, u32[]{:S(2)}) collective-permute-start(bf16[13,64,192]{2,1,0:T(8,128)(2,1)} %env_mine.1), channel_id=1, source_target_pairs={{0,1},{1,0},{2,3},{3,2},{4,5},{5,4},{6,7},{7,6},{8,9},{9,8},{10,11... | collective-permute-start | bytes 958472 | tf_op jit(solution)/shard_map/ppermute | solution.py:19
  5.7 0.7 %copy-start.3 = (s32[256]{0:T(256)S(1)}, s32[256]{0:T(256)}, u32[]{:S(2)}) copy-start(s32[256]{0:T(256)} %param.11) | copy-start | bytes 3076
  6.6 1.3 %copy-start.2 = (bf16[13,64,192]{2,1,0:T(8,128)(2,1)S(1)}, bf16[13,64,192]{2,1,0:T(8,128)(2,1)}, u32[]{:S(2)}) copy-start(bf16[13,64,192]{2,1,0:T(8,128)(2,1)} %env_mine.1) | copy-start | bytes 958468
  7.9 3.9 %copy-start = (bf16[26,128,128]{2,1,0:T(8,128)(2,1)S(1)}, bf16[26,128,128]{2,1,0:T(8,128)(2,1)}, u32[]{:S(2)}) copy-start(bf16[26,128,128]{2,1,0:T(8,128)(2,1)} %param.8) | copy-start | bytes 2555908
  7.9 3.9 %copy-start.1 = (bf16[64,16,128]{2,1,0:T(8,128)(2,1)S(1)}, bf16[64,16,128]{2,1,0:T(8,128)(2,1)}, u32[]{:S(2)}) copy-start(bf16[64,16,128]{2,1,0:T(8,128)(2,1)} %param.6) | copy-start | bytes 786436
  10.1 1.6 %collective-permute-start.2 = (bf16[1024,128]{1,0:T(8,128)(2,1)S(1)}, bf16[1024,128]{1,0:T(8,128)(2,1)S(1)}, u32[]{:S(2)}, u32[]{:S(2)}) collective-permute-start(bf16[1024,128]{1,0:T(8,128)(2,1)S(1)} %collective-permute-done.direct_in), channel_id=1, source_target_pairs={{0,1},{1,0},{2,3},{3,2},{4,5},{5,4},{6,7},{7,6},{8,9},{9,8},{10,11... | collective-permute-start | bytes 786440 | tf_op jit(solution)/shard_map/ppermute | solution.py:19
  16.7 5.5 %collective-permute-start.6 = (bf16[32,2048]{1,0:T(8,128)(2,1)S(1)}, bf16[32,2048]{1,0:T(8,128)(2,1)S(1)}, u32[]{:S(2)}, u32[]{:S(2)}) collective-permute-start(bf16[32,2048]{1,0:T(8,128)(2,1)S(1)} %get-tuple-element.23.own_here), channel_id=1, source_target_pairs={{4,8},{8,4},{5,9},{9,5},{6,10},{10,6},{7,11},{11,7},{20,24},{24,20... | collective-permute-start | bytes 393224 | tf_op jit(solution)/shard_map/ppermute | solution.py:351
  17.4 8.3 %collective-permute-start.4 = (bf16[32,2048]{1,0:T(8,128)(2,1)S(1)}, bf16[32,2048]{1,0:T(8,128)(2,1)S(1)}, u32[]{:S(2)}, u32[]{:S(2)}) collective-permute-start(bf16[32,2048]{1,0:T(8,128)(2,1)S(1)} %get-tuple-element.23.own_here), channel_id=1, source_target_pairs={{0,4},{4,0},{8,12},{12,8},{1,5},{5,1},{9,13},{13,9},{2,6},{6,2},{1... | collective-permute-start | bytes 393224 | tf_op jit(solution)/shard_map/ppermute | solution.py:350
  22.2 3.5 %collective-permute-start.3 = (bf16[32,2048]{1,0:T(8,128)(2,1)S(1)}, bf16[32,2048]{1,0:T(8,128)(2,1)S(1)}, u32[]{:S(2)}, u32[]{:S(2)}) collective-permute-start(bf16[32,2048]{1,0:T(8,128)(2,1)S(1)} %get-tuple-element.23.own_here), channel_id=1, source_target_pairs={{0,1},{1,0},{2,3},{3,2},{4,5},{5,4},{6,7},{7,6},{8,9},{9,8},{10,11... | collective-permute-start | bytes 393224 | tf_op jit(solution)/shard_map/ppermute | solution.py:19
  22.2 3.5 %collective-permute-start.7 = (bf16[32,2048]{1,0:T(8,128)(2,1)S(1)}, bf16[32,2048]{1,0:T(8,128)(2,1)S(1)}, u32[]{:S(2)}, u32[]{:S(2)}) collective-permute-start(bf16[32,2048]{1,0:T(8,128)(2,1)S(1)} %collective-permute-done.6.odd_here), channel_id=1, source_target_pairs={{0,1},{1,0},{2,3},{3,2},{4,5},{5,4},{6,7},{7,6},{8,9},{9,8},{10,11... | collective-permute-start | bytes 393224 | tf_op jit(solution)/shard_map/ppermute | solution.py:19
  25.7 1.3 %collective-permute-start.5 = (bf16[32,2048]{1,0:T(8,128)(2,1)S(1)}, bf16[32,2048]{1,0:T(8,128)(2,1)S(1)}, u32[]{:S(2)}, u32[]{:S(2)}) collective-permute-start(bf16[32,2048]{1,0:T(8,128)(2,1)S(1)} %collective-permute-done.4.even_here), channel_id=1, source_target_pairs={{0,1},{1,0},{2,3},{3,2},{4,5},{5,4},{6,7},{7,6},{8,9},{9,8},{10,11... | collective-permute-start | bytes 393224 | tf_op jit(solution)/shard_map/ppermute | solution.py:19
  31.5 10.4 %collective-permute-start.8 = (f32[64,8,128]{2,1,0:T(8,128)S(1)}, f32[64,8,128]{2,1,0:T(8,128)S(1)}, u32[]{:S(2)}, u32[]{:S(2)}) collective-permute-start(f32[64,8,128]{2,1,0:T(8,128)S(1)} %get-tuple-element.26), channel_id=1, source_target_pairs={{0,1},{1,0},{2,3},{3,2},{4,5},{5,4},{6,7},{7,6},{8,9},{9,8},{10,11... | collective-permute-start | bytes 786440 | tf_op jit(solution)/shard_map/ppermute | solution.py:19

commit v6 on v5

--- a/solution.py
+++ b/solution.py
@@ -12,6 +12,7 @@
 LOCAL = 4
 GROUP = 8
 VMEM_LIMIT = 40 * 2**20
+SHORT = pl.CostEstimate(flops=10**9, bytes_accessed=2**21, transcendentals=0)
 WHOLE = pl.BlockSpec(memory_space=pltpu.VMEM)
 
 
@@ -160,31 +161,48 @@
     return jnp.where(index == 0, pieces[:, : states // 2, :], pieces[:, states // 2 :, :])
 
 
+def lay_kernel(vector, direct, vector_rows, direct_rows, wide):
+    rows, width = vector_rows.shape
+    states = width // vector.shape[1]
+    for source, target in ((vector, vector_rows), (direct, direct_rows)):
+        wide[...] = source[...].astype(jnp.float32)
+
+        def store(columns, piece, target=target):
+            target[:, columns] = piece
+
+        states_apart(wide, rows, states, store)
+
+
 def first_kernel(
-    env, coupling, right, vector, direct_in, passed_in,
-    image, image_rows, sums,
+    env, coupling, right, vector_rows, direct_rows, passed_in,
+    image, image_rows,
     wide, extended, contracted, mixed,
 ):
-    rows = extended.shape[0] // 3
-    states = vector.shape[0] // rows
+    rows = vector_rows.shape[0]
+    states = passed_in.shape[0] // rows
     half = image.shape[0]
-    for place, source in zip((rows,) + halo_places(rows), (vector, direct_in, passed_in)):
-        wide[...] = source[...].astype(jnp.float32)
-
-        def store(columns, piece, place=place):
-            extended[pl.ds(place, rows), columns] = piece
-
-        states_apart(wide, rows, states, store)
+    direct, passed = halo_places(rows)
+    extended[rows : 2 * rows, :] = vector_rows[...]
+    extended[pl.ds(direct, rows), :] = direct_rows[...]
+    wide[...] = passed_in[...].astype(jnp.float32)
+
+    def store(columns, piece):
+        extended[pl.ds(passed, rows), columns] = piece
+
+    states_apart(wide, rows, states, store)
     apply_steps(env, coupling, right, extended, contracted, mixed, image)
-    out = image[...]
 
     def store_rows(columns, piece):
         image_rows[:, columns] = piece
 
     states_apart(image, half // states, states, store_rows)
+
+
+def sums_kernel(image, vector, sums):
+    half, lanes = image.shape
     start = pl.multiple_of(lax.axis_index("mpo") * half, half)
     own = vector[pl.ds(start, half), :].astype(jnp.float32)
-    lanes = out.shape[1]
+    out = image[...]
     sums[...] = jnp.concatenate(
         [column_sum(own * own), column_sum(own * out), column_sum(out * out)]
         + [jnp.zeros((5, lanes), jnp.float32)],
@@ -334,17 +352,19 @@
         ((half // GROUP, states * SLOT, GROUP * columns), bf16),
         ((size, bonds * columns), bf16),
     )
-    first, first_rows, sums = call(
+    laid = ((rows, states * columns), bf16)
+    wide = ((rows * states, columns), f32)
+    vector_rows, direct_rows = call(
+        lay_kernel, (flat, direct_one), (laid, laid), (wide,), "rows", cost=SHORT
+    )
+    first, first_rows = call(
         first_kernel,
-        (env, coupling, right, flat, direct_one, passed_one),
-        (
-            ((size, columns), f32),
-            ((half, states * columns), bf16),
-            ((8, columns), f32),
-        ),
-        (((rows * states, columns), f32),) + work,
+        (env, coupling, right, vector_rows, direct_rows, passed_one),
+        (((size, columns), f32), ((half, states * columns), bf16)),
+        (wide,) + work,
         "first_image",
     )
+    (sums,) = call(sums_kernel, (first, flat), (((8, columns), f32),), (), "sums", cost=SHORT)
 
     blocks = lax.axis_size("brow")
     even_rows = lax.ppermute(first_rows, "brow", neighbours(blocks, False))

time: 43 us -> 42.4 us (0.986)
  waiting for transfers between devices: 5.63 us -> 5.12 us
    ppermute x6, waiting for transfers between devices: 2.51 us -> 1.97 us  [swap_cores(): return lax.ppermute(x, 'mpo', [(0, 1), (1, 0)])]
    pallas_call x4 -> x6, Pallas kernels: 12.4 us -> 12.2 us  [call(): pl.pallas_call(kernel, out_shape=tuple((jax.ShapeDtypeStruct(shape, dtype...]
  transfers between devices with their start and end apart: 9 -> 9, of which waited for: 4 -> 4; matrix products, arithmetic and copies ran while one was open for 4% -> 4% of each run, Pallas kernels for 5% -> 6%
where the time goes in v6:
time: 42.4 us; the launch traced here: 42.1 us
  Pallas kernels  12.2 us (29%)
  starting transfers between devices  11.6 us (27%)
  blocking collectives  10.2 us (24%)
  waiting for transfers between devices  5.12 us (12%)
  other arithmetic  1.35 us (3%)
  local copies, waits for them, and re-layouts  0.83 us (2%)
  between operations  0.74 us (2%)
    pallas_call x6, Pallas kernels, call(): pl.pallas_call(kernel, out_shape=tuple((jax.ShapeDtypeStruct(shape, dtype...  12.2 us
    all_to_all x1, blocking collectives, per_device(): gathered = lax.all_to_all(totals, axes, 0, 0)  10.2 us
    ppermute x1, starting transfers between devices, swap_blocks(): return lax.ppermute(x, ('brow', 'mpo'), pairs)  4.93 us
    ppermute x1, starting transfers between devices, per_device(): even_rows = lax.ppermute(first_rows, 'brow', neighbours(blocks, False))  4.83 us
    ppermute x1, waiting for transfers between devices, per_device(): even_rows = lax.ppermute(first_rows, 'brow', neighbours(blocks, False))  3 us
    ppermute x6, waiting for transfers between devices, swap_cores(): return lax.ppermute(x, 'mpo', [(0, 1), (1, 0)])  1.97 us
    ppermute x6, starting transfers between devices, swap_cores(): return lax.ppermute(x, 'mpo', [(0, 1), (1, 0)])  1.22 us
    concatenate x1, other arithmetic, per_device(): both = jnp.concatenate([mpo_left, mpo_right], axis=0)  1.2 us
  transfers between devices with their start and end apart: 9, of which 4 were waited for; matrix products, arithmetic and copies ran while one was open for 4% of the time, Pallas kernels for 6%

profile of v6, /device:TPU:0, one launch (start us, length us, event | category | flops | bytes accessed | tf_op | source)
XLA Modules:
  0.0 42.1 jit_solution(1840646951119518464)
XLA Ops:
  0.6 4.9 %collective-permute-start = (bf16[1024,128]{1,0:T(8,128)(2,1)}, bf16[1024,128]{1,0:T(8,128)(2,1)S(1)}, u32[]{:S(2)}, u32[]{:S(2)}) collective-permute-start(bf16[1024,128]{1,0:T(8,128)(2,1)} %bitcast.9), channel_id=1, source_target_pairs={{0,4},{4,0},{8,12},{12,8},{5,9},{9,5},{2,6},{6,2},{10,14},{14,10},... | collective-permute-start | bytes 786440 | tf_op jit(solution)/shard_map/ppermute | solution.py:37
  5.6 0.1 collective-permute-start.1
  5.7 0.0 copy-start.3
  5.7 0.7 %copy-done.3 = s32[256]{0:T(256)S(1)} copy-done((s32[256]{0:T(256)S(1)}, s32[256]{0:T(256)}, u32[]{:S(2)}) %copy-start.3) | copy-done | bytes 1048
  6.3 0.1 pad_add_fusion
  6.4 0.1 dynamic_slice.6
  6.5 0.1 dynamic_slice.7
  6.6 0.0 copy-start.2
  6.6 1.2 %pad_maximum_fusion = f32[52,26,4,4]{1,3,2,0:T(4,128)S(1)} fusion(f32[26,26,4,4]{1,3,2,0:T(4,128)} %param.10, f32[26,26,4,4]{1,3,2,0:T(4,128)} %param.9), kind=kLoop, calls=%fused_computation | loop fusion | flops 21632 | bytes 173056 | tf_op jit(solution)/shard_map/concatenate | solution.py:326
  7.8 0.1 compare_convert_fusion.mask
  7.8 0.0 collective-permute-done.1.env_there
  7.9 0.0 copy-done.2
  7.9 0.0 copy-start.1
  7.9 2.1 %operands.1 = (bf16[1024,192]{1,0:T(8,128)(2,1)S(1)}, bf16[416,512]{1,0:T(8,128)(2,1)S(1)}) custom-call(bf16[13,64,192]{2,1,0:T(8,128)(2,1)S(1)} %copy-done.2, bf16[13,64,192]{2,1,0:T(8,128)(2,1)S(1)} %collective-permute-done.1.env_there, f32[32,192]{1,0:T(8,128)S(1)} %compare_convert_fusion.mask, f32[832,26]{1,0:T(8,128)S(1)} %bitcast.14), custom_call_target="tpu_custom_call" | custom-call | flops 4000000000 | bytes 8388608 | tf_op jit(solution)/shard_map/operands/pallas_call | solution.py:291
  10.0 0.1 collective-permute-done.direct
  10.1 0.0 copy-start
  10.1 0.4 %collective-permute-start.2 = (bf16[1024,128]{1,0:T(8,128)(2,1)S(1)}, bf16[1024,128]{1,0:T(8,128)(2,1)S(1)}, u32[]{:S(2)}, u32[]{:S(2)}) collective-permute-start(bf16[1024,128]{1,0:T(8,128)(2,1)S(1)} %collective-permute-done.direct), channel_id=1, source_target_pairs={{0,1},{1,0},{2,3},{3,2},{4,5},{5,4},{6,7},{7,6},{8,9},{9,8},{10,11... | collective-permute-start | bytes 786440 | tf_op jit(solution)/shard_map/ppermute | solution.py:20
  10.6 0.0 copy-done.1
  10.6 0.4 rows.1
  11.0 0.7 %collective-permute-done.2.passed_in = bf16[1024,128]{1,0:T(8,128)(2,1)S(1)} collective-permute-done((bf16[1024,128]{1,0:T(8,128)(2,1)S(1)}, bf16[1024,128]{1,0:T(8,128)(2,1)S(1)}, u32[]{:S(2)}, u32[]{:S(2)}) %collective-permute-start.2) | collective-permute-done | bytes 262176 | tf_op jit(solution)/shard_map/ppermute | solution.py:20
  11.7 0.0 copy-done
  11.7 4.4 %first_image.1 = (f32[512,128]{1,0:T(8,128)S(1)}, bf16[32,2048]{1,0:T(8,128)(2,1)S(1)}) custom-call(bf16[1024,192]{1,0:T(8,128)(2,1)S(1)} %get-tuple-element.20.env, bf16[416,512]{1,0:T(8,128)(2,1)S(1)} %get-tuple-element.21.coupling, bf16[3328,128]{1,0:T(8,128)(2,1)S(1)} %bitcast.7, bf16[64,2048]{1,0:T(8,128)(2,1)S(1)} %get-tuple-element.23.vector_rows, ...), custom_call_target="tpu_custom_call" | custom-call | tf_op jit(solution)/shard_map/first_image/pallas_call | solution.py:291
  16.1 0.7 %collective-permute-start.6 = (bf16[32,2048]{1,0:T(8,128)(2,1)S(1)}, bf16[32,2048]{1,0:T(8,128)(2,1)S(1)}, u32[]{:S(2)}, u32[]{:S(2)}) collective-permute-start(bf16[32,2048]{1,0:T(8,128)(2,1)S(1)} %get-tuple-element.26.own_here), channel_id=1, source_target_pairs={{4,8},{8,4},{5,9},{9,5},{6,10},{10,6},{7,11},{11,7},{20,24},{24,20... | collective-permute-start | bytes 393224 | tf_op jit(solution)/shard_map/ppermute | solution.py:371
  16.8 4.8 %collective-permute-start.4 = (bf16[32,2048]{1,0:T(8,128)(2,1)S(1)}, bf16[32,2048]{1,0:T(8,128)(2,1)S(1)}, u32[]{:S(2)}, u32[]{:S(2)}) collective-permute-start(bf16[32,2048]{1,0:T(8,128)(2,1)S(1)} %get-tuple-element.26.own_here), channel_id=1, source_target_pairs={{0,4},{4,0},{8,12},{12,8},{1,5},{5,1},{9,13},{13,9},{2,6},{6,2},{1... | collective-permute-start | bytes 393224 | tf_op jit(solution)/shard_map/ppermute | solution.py:370
  21.6 0.0 collective-permute-start.3
  21.6 0.0 collective-permute-done.6.odd_here
  21.6 0.5 %collective-permute-start.7 = (bf16[32,2048]{1,0:T(8,128)(2,1)S(1)}, bf16[32,2048]{1,0:T(8,128)(2,1)S(1)}, u32[]{:S(2)}, u32[]{:S(2)}) collective-permute-start(bf16[32,2048]{1,0:T(8,128)(2,1)S(1)} %collective-permute-done.6.odd_here), channel_id=1, source_target_pairs={{0,1},{1,0},{2,3},{3,2},{4,5},{5,4},{6,7},{7,6},{8,9},{9,8},{10,11... | collective-permute-start | bytes 393224 | tf_op jit(solution)/shard_map/ppermute | solution.py:20
  22.1 3.0 %collective-permute-done.4.even_here = bf16[32,2048]{1,0:T(8,128)(2,1)S(1)} collective-permute-done((bf16[32,2048]{1,0:T(8,128)(2,1)S(1)}, bf16[32,2048]{1,0:T(8,128)(2,1)S(1)}, u32[]{:S(2)}, u32[]{:S(2)}) %collective-permute-start.4) | collective-permute-done | bytes 131104 | tf_op jit(solution)/shard_map/ppermute | solution.py:370
  25.1 0.0 collective-permute-start.5
  25.1 0.1 sums.1
  25.2 0.0 collective-permute-done.3.own_there
  25.2 0.0 collective-permute-done.7.odd_there
  25.2 1.2 %collective-permute-done.5.even_there = bf16[32,2048]{1,0:T(8,128)(2,1)S(1)} collective-permute-done((bf16[32,2048]{1,0:T(8,128)(2,1)S(1)}, bf16[32,2048]{1,0:T(8,128)(2,1)S(1)}, u32[]{:S(2)}, u32[]{:S(2)}) %collective-permute-start.5) | collective-permute-done | bytes 131104 | tf_op jit(solution)/shard_map/ppermute | solution.py:20
  26.5 4.4 %second_image.1 = (f32[512,128]{1,0:T(8,128)S(1)}, f32[64,8,128]{2,1,0:T(8,128)S(1)}, f32[16,1,128]{2,1,0:T(1,128)S(1)}) custom-call(bf16[1024,192]{1,0:T(8,128)(2,1)S(1)} %get-tuple-element.20.env, bf16[416,512]{1,0:T(8,128)(2,1)S(1)} %get-tuple-element.21.coupling, bf16[3328,128]{1,0:T(8,128)(2,1)S(1)} %bitcast.8, ...), custom_call_target="tpu_custom_call" | custom-call | tf_op jit(solution)/shard_map/second_image/pallas_call | solution.py:291
  30.8 0.2 collective-permute-start.8
  31.0 10.2 %all_to_all.5.refs_4_ = f32[16,1,128]{2,1,0:T(1,128)S(1)} all-to-all(f32[16,1,128]{2,1,0:T(1,128)S(1)} %get-tuple-element.29), channel_id=1, replica_groups=mesh['groups'=2,'brow'=4,'bcol'=2,'mpo'=2] {'brow','bcol','mpo'}, dimensions={0} | all-to-all | bytes 16384 | tf_op jit(solution)/shard_map/all_to_all | solution.py:387
  41.3 0.0 collective-permute-done.8.refs_2_
  41.3 0.9 %outputs.1 = (bf16[512,128]{1,0:T(8,128)(2,1)}, bf16[512,128]{1,0:T(8,128)(2,1)}, f32[2,2]{1,0:T(2,128)}) custom-call(f32[512,128]{1,0:T(8,128)S(1)} %get-tuple-element.25.image.first.refs_0_, f32[512,128]{1,0:T(8,128)S(1)} %get-tuple-element.27.refs_1_, f32[64,8,128]{2,1,0:T(8,128)S(1)} %collective-permute-done.8.refs_2_, bf16[1024,128]{1,0:T(8,128)(2,1)S(1)} %bitcast.13, ...), custom_call_target="tpu_custom_call" | custom-call | tf_op jit(solution)/shard_map/outputs/pallas_call | solution.py:291
  (1 shorter events, 0.0 us)
Async XLA Ops:
  0.6 9.5 %collective-permute-start = (bf16[1024,128]{1,0:T(8,128)(2,1)}, bf16[1024,128]{1,0:T(8,128)(2,1)S(1)}, u32[]{:S(2)}, u32[]{:S(2)}) collective-permute-start(bf16[1024,128]{1,0:T(8,128)(2,1)} %bitcast.9), channel_id=1, source_target_pairs={{0,4},{4,0},{8,12},{12,8},{5,9},{9,5},{2,6},{6,2},{10,14},{14,10},... | collective-permute-start | bytes 786440 | tf_op jit(solution)/shard_map/ppermute | solution.py:37
  5.6 2.3 %collective-permute-start.1 = (bf16[13,64,192]{2,1,0:T(8,128)(2,1)}, bf16[13,64,192]{2,1,0:T(8,128)(2,1)S(1)}, u32[]{:S(2)}, u32[]{:S(2)}) collective-permute-start(bf16[13,64,192]{2,1,0:T(8,128)(2,1)} %env_mine.1), channel_id=1, source_target_pairs={{0,1},{1,0},{2,3},{3,2},{4,5},{5,4},{6,7},{7,6},{8,9},{9,8},{10,11... | collective-permute-start | bytes 958472 | tf_op jit(solution)/shard_map/ppermute | solution.py:20
  5.7 0.7 %copy-start.3 = (s32[256]{0:T(256)S(1)}, s32[256]{0:T(256)}, u32[]{:S(2)}) copy-start(s32[256]{0:T(256)} %param.11) | copy-start | bytes 3076
  6.6 1.3 %copy-start.2 = (bf16[13,64,192]{2,1,0:T(8,128)(2,1)S(1)}, bf16[13,64,192]{2,1,0:T(8,128)(2,1)}, u32[]{:S(2)}) copy-start(bf16[13,64,192]{2,1,0:T(8,128)(2,1)} %env_mine.1) | copy-start | bytes 958468
  7.9 2.7 %copy-start.1 = (bf16[64,16,128]{2,1,0:T(8,128)(2,1)S(1)}, bf16[64,16,128]{2,1,0:T(8,128)(2,1)}, u32[]{:S(2)}) copy-start(bf16[64,16,128]{2,1,0:T(8,128)(2,1)} %param.6) | copy-start | bytes 786436
  10.1 1.6 %copy-start = (bf16[26,128,128]{2,1,0:T(8,128)(2,1)S(1)}, bf16[26,128,128]{2,1,0:T(8,128)(2,1)}, u32[]{:S(2)}) copy-start(bf16[26,128,128]{2,1,0:T(8,128)(2,1)} %param.8) | copy-start | bytes 2555908
  10.1 1.6 %collective-permute-start.2 = (bf16[1024,128]{1,0:T(8,128)(2,1)S(1)}, bf16[1024,128]{1,0:T(8,128)(2,1)S(1)}, u32[]{:S(2)}, u32[]{:S(2)}) collective-permute-start(bf16[1024,128]{1,0:T(8,128)(2,1)S(1)} %collective-permute-done.direct), channel_id=1, source_target_pairs={{0,1},{1,0},{2,3},{3,2},{4,5},{5,4},{6,7},{7,6},{8,9},{9,8},{10,11... | collective-permute-start | bytes 786440 | tf_op jit(solution)/shard_map/ppermute | solution.py:20
  16.1 5.5 %collective-permute-start.6 = (bf16[32,2048]{1,0:T(8,128)(2,1)S(1)}, bf16[32,2048]{1,0:T(8,128)(2,1)S(1)}, u32[]{:S(2)}, u32[]{:S(2)}) collective-permute-start(bf16[32,2048]{1,0:T(8,128)(2,1)S(1)} %get-tuple-element.26.own_here), channel_id=1, source_target_pairs={{4,8},{8,4},{5,9},{9,5},{6,10},{10,6},{7,11},{11,7},{20,24},{24,20... | collective-permute-start | bytes 393224 | tf_op jit(solution)/shard_map/ppermute | solution.py:371
  16.8 8.3 %collective-permute-start.4 = (bf16[32,2048]{1,0:T(8,128)(2,1)S(1)}, bf16[32,2048]{1,0:T(8,128)(2,1)S(1)}, u32[]{:S(2)}, u32[]{:S(2)}) collective-permute-start(bf16[32,2048]{1,0:T(8,128)(2,1)S(1)} %get-tuple-element.26.own_here), channel_id=1, source_target_pairs={{0,4},{4,0},{8,12},{12,8},{1,5},{5,1},{9,13},{13,9},{2,6},{6,2},{1... | collective-permute-start | bytes 393224 | tf_op jit(solution)/shard_map/ppermute | solution.py:370
  21.6 3.6 %collective-permute-start.3 = (bf16[32,2048]{1,0:T(8,128)(2,1)S(1)}, bf16[32,2048]{1,0:T(8,128)(2,1)S(1)}, u32[]{:S(2)}, u32[]{:S(2)}) collective-permute-start(bf16[32,2048]{1,0:T(8,128)(2,1)S(1)} %get-tuple-element.26.own_here), channel_id=1, source_target_pairs={{0,1},{1,0},{2,3},{3,2},{4,5},{5,4},{6,7},{7,6},{8,9},{9,8},{10,11... | collective-permute-start | bytes 393224 | tf_op jit(solution)/shard_map/ppermute | solution.py:20
  21.6 3.6 %collective-permute-start.7 = (bf16[32,2048]{1,0:T(8,128)(2,1)S(1)}, bf16[32,2048]{1,0:T(8,128)(2,1)S(1)}, u32[]{:S(2)}, u32[]{:S(2)}) collective-permute-start(bf16[32,2048]{1,0:T(8,128)(2,1)S(1)} %collective-permute-done.6.odd_here), channel_id=1, source_target_pairs={{0,1},{1,0},{2,3},{3,2},{4,5},{5,4},{6,7},{7,6},{8,9},{9,8},{10,11... | collective-permute-start | bytes 393224 | tf_op jit(solution)/shard_map/ppermute | solution.py:20
  25.1 1.3 %collective-permute-start.5 = (bf16[32,2048]{1,0:T(8,128)(2,1)S(1)}, bf16[32,2048]{1,0:T(8,128)(2,1)S(1)}, u32[]{:S(2)}, u32[]{:S(2)}) collective-permute-start(bf16[32,2048]{1,0:T(8,128)(2,1)S(1)} %collective-permute-done.4.even_here), channel_id=1, source_target_pairs={{0,1},{1,0},{2,3},{3,2},{4,5},{5,4},{6,7},{7,6},{8,9},{9,8},{10,11... | collective-permute-start | bytes 393224 | tf_op jit(solution)/shard_map/ppermute | solution.py:20
  30.8 10.4 %collective-permute-start.8 = (f32[64,8,128]{2,1,0:T(8,128)S(1)}, f32[64,8,128]{2,1,0:T(8,128)S(1)}, u32[]{:S(2)}, u32[]{:S(2)}) collective-permute-start(f32[64,8,128]{2,1,0:T(8,128)S(1)} %get-tuple-element.28), channel_id=1, source_target_pairs={{0,1},{1,0},{2,3},{3,2},{4,5},{5,4},{6,7},{7,6},{8,9},{9,8},{10,11... | collective-permute-start | bytes 786440 | tf_op jit(solution)/shard_map/ppermute | solution.py:20

commit v7 on v6

--- a/solution.py
+++ b/solution.py
@@ -20,21 +20,26 @@
     return lax.ppermute(x, "mpo", [(0, 1), (1, 0)])
 
 
-def neighbours(blocks, odd):
+def partner_of(block, slab, odd):
+    blocks, slabs = lax.axis_size("brow"), lax.axis_size("bcol")
+    other = (block + 1 if block % 2 else block - 1) if odd else block ^ 1
+    if 0 <= other < blocks:
+        return other, slab
+    return block, slab ^ 1 if slab ^ 1 < slabs else slab
+
+
+def place_of(block, slab, core):
+    return (block * lax.axis_size("bcol") + slab) * 2 + core
+
+
+def trade(x, odd):
     pairs = []
-    for i in range(blocks):
-        partner = (i + 1 if i % 2 else i - 1) if odd else i ^ 1
-        if 0 <= partner < blocks:
-            pairs.append((i, partner))
-    return pairs
-
-
-def swap_blocks(x):
-    blocks = lax.axis_size("brow")
-    pairs = [
-        (2 * i + core, 2 * j + core) for core in range(2) for i, j in neighbours(blocks, core == 1)
-    ]
-    return lax.ppermute(x, ("brow", "mpo"), pairs)
+    for block in range(lax.axis_size("brow")):
+        for slab in range(lax.axis_size("bcol")):
+            for core in range(2):
+                other = partner_of(block, slab, odd[core])
+                pairs.append((place_of(block, slab, core), place_of(*other, core)))
+    return lax.ppermute(x, ("brow", "bcol", "mpo"), pairs)
 
 
 def halo_places(rows):
@@ -316,7 +321,7 @@
     flat = amplitudes.reshape(rows * states, columns)
 
     env_there = swap_cores(left_env)
-    direct_one = swap_blocks(flat)
+    direct_one = trade(flat, (False, True))
 
     outside = jnp.full((rows,), -1, dtype=jnp.int32)
     padded = jnp.concatenate([outside, sector_table, outside])
@@ -366,9 +371,8 @@
     )
     (sums,) = call(sums_kernel, (first, flat), (((8, columns), f32),), (), "sums", cost=SHORT)
 
-    blocks = lax.axis_size("brow")
-    even_rows = lax.ppermute(first_rows, "brow", neighbours(blocks, False))
-    odd_rows = lax.ppermute(first_rows, "brow", neighbours(blocks, True))
+    even_rows = trade(first_rows, (False, False))
+    odd_rows = trade(first_rows, (True, True))
     pieces = [(x, swap_cores(x)) for x in (first_rows, even_rows, odd_rows)]
     pieces = [x for pair in pieces for x in pair]
 

time: 42.4 us -> 39.7 us (0.936)
  starting transfers between devices: 11.6 us -> 7.3 us
  blocking collectives: 10.2 us -> 11.2 us
  waiting for transfers between devices: 5.12 us -> 5.82 us
    ppermute x3, starting transfers between devices: 10.4 us -> 6.75 us  [trade(): return lax.ppermute(x, ('brow', 'bcol', 'mpo'), pairs)]
    all_to_all x1, blocking collectives: 10.2 us -> 11.2 us  [per_device(): gathered = lax.all_to_all(totals, axes, 0, 0)]
    ppermute x3, waiting for transfers between devices: 3.14 us -> 3.83 us  [trade(): return lax.ppermute(x, ('brow', 'bcol', 'mpo'), pairs)]
    ppermute x6, starting transfers between devices: 1.22 us -> 0.55 us  [swap_cores(): return lax.ppermute(x, 'mpo', [(0, 1), (1, 0)])]
  transfers between devices with their start and end apart: 9 -> 9, of which waited for: 4 -> 5; matrix products, arithmetic and copies ran while one was open for 4% -> 4% of each run, Pallas kernels for 6% -> 7%
where the time goes in v7:
time: 39.7 us; the launch traced here: 39.5 us
  Pallas kernels  12.2 us (31%)
  blocking collectives  11.2 us (28%)
  starting transfers between devices  7.3 us (18%)
  waiting for transfers between devices  5.82 us (15%)
  other arithmetic  1.35 us (3%)
  local copies, waits for them, and re-layouts  0.84 us (2%)
  between operations  0.7 us (2%)
    pallas_call x6, Pallas kernels, call(): pl.pallas_call(kernel, out_shape=tuple((jax.ShapeDtypeStruct(shape, dtype...  12.2 us
    all_to_all x1, blocking collectives, per_device(): gathered = lax.all_to_all(totals, axes, 0, 0)  11.2 us
    ppermute x3, starting transfers between devices, trade(): return lax.ppermute(x, ('brow', 'bcol', 'mpo'), pairs)  6.75 us
    ppermute x3, waiting for transfers between devices, trade(): return lax.ppermute(x, ('brow', 'bcol', 'mpo'), pairs)  3.83 us
    ppermute x6, waiting for transfers between devices, swap_cores(): return lax.ppermute(x, 'mpo', [(0, 1), (1, 0)])  1.99 us
    concatenate x1, other arithmetic, per_device(): both = jnp.concatenate([mpo_left, mpo_right], axis=0)  1.2 us
  transfers between devices with their start and end apart: 9, of which 5 were waited for; matrix products, arithmetic and copies ran while one was open for 4% of the time, Pallas kernels for 7%

profile of v7, /device:TPU:0, one launch (start us, length us, event | category | flops | bytes accessed | tf_op | source)
XLA Modules:
  0.0 39.5 jit_solution(17922410559045978954)
XLA Ops:
  0.6 3.1 %collective-permute-start = (bf16[1024,128]{1,0:T(8,128)(2,1)}, bf16[1024,128]{1,0:T(8,128)(2,1)S(1)}, u32[]{:S(2)}, u32[]{:S(2)}) collective-permute-start(bf16[1024,128]{1,0:T(8,128)(2,1)} %bitcast.9), channel_id=1, source_target_pairs={{0,4},{1,3},{2,6},{3,1},{4,0},{5,9},{6,2},{7,11},{8,12},{9,5},{10,... | collective-permute-start | bytes 786440 | tf_op jit(solution)/shard_map/ppermute | solution.py:42
  3.7 0.0 collective-permute-start.1
  3.7 0.0 copy-start.3
  3.7 0.7 %copy-done.3 = s32[256]{0:T(256)S(1)} copy-done((s32[256]{0:T(256)S(1)}, s32[256]{0:T(256)}, u32[]{:S(2)}) %copy-start.3) | copy-done | bytes 1048
  4.4 0.1 pad_add_fusion
  4.5 0.1 dynamic_slice.6
  4.6 0.1 dynamic_slice.7
  4.6 0.0 copy-start.2
  4.6 1.2 %pad_maximum_fusion = f32[52,26,4,4]{1,3,2,0:T(4,128)S(1)} fusion(f32[26,26,4,4]{1,3,2,0:T(4,128)} %param.10, f32[26,26,4,4]{1,3,2,0:T(4,128)} %param.9), kind=kLoop, calls=%fused_computation | loop fusion | flops 21632 | bytes 173056 | tf_op jit(solution)/shard_map/concatenate | solution.py:331
  5.8 0.1 compare_convert_fusion.mask
  5.9 0.0 collective-permute-done.1.env_there
  5.9 0.0 copy-done.2
  5.9 0.0 copy-start.1
  5.9 2.1 %operands.1 = (bf16[1024,192]{1,0:T(8,128)(2,1)S(1)}, bf16[416,512]{1,0:T(8,128)(2,1)S(1)}) custom-call(bf16[13,64,192]{2,1,0:T(8,128)(2,1)S(1)} %copy-done.2, bf16[13,64,192]{2,1,0:T(8,128)(2,1)S(1)} %collective-permute-done.1.env_there, f32[32,192]{1,0:T(8,128)S(1)} %compare_convert_fusion.mask, f32[832,26]{1,0:T(8,128)S(1)} %bitcast.14), custom_call_target="tpu_custom_call" | custom-call | flops 4000000000 | bytes 8388608 | tf_op jit(solution)/shard_map/operands/pallas_call | solution.py:296
  8.0 0.2 collective-permute-done.direct
  8.3 0.0 copy-start
  8.3 0.4 collective-permute-start.2
  8.6 0.0 copy-done.1
  8.6 0.4 %rows.1 = (bf16[64,2048]{1,0:T(8,128)(2,1)S(1)}, bf16[64,2048]{1,0:T(8,128)(2,1)S(1)}) custom-call(bf16[1024,128]{1,0:T(8,128)(2,1)S(1)} %bitcast.10, bf16[1024,128]{1,0:T(8,128)(2,1)S(1)} %collective-permute-done.direct), custom_call_target="tpu_custom_call" | custom-call | flops 1000000000 | bytes 2097152 | tf_op jit(solution)/shard_map/rows/pallas_call | solution.py:296
  9.1 0.8 %collective-permute-done.2.passed_in = bf16[1024,128]{1,0:T(8,128)(2,1)S(1)} collective-permute-done((bf16[1024,128]{1,0:T(8,128)(2,1)S(1)}, bf16[1024,128]{1,0:T(8,128)(2,1)S(1)}, u32[]{:S(2)}, u32[]{:S(2)}) %collective-permute-start.2) | collective-permute-done | bytes 262176 | tf_op jit(solution)/shard_map/ppermute | solution.py:20
  9.8 0.0 copy-done
  9.8 4.4 %first_image.1 = (f32[512,128]{1,0:T(8,128)S(1)}, bf16[32,2048]{1,0:T(8,128)(2,1)S(1)}) custom-call(bf16[1024,192]{1,0:T(8,128)(2,1)S(1)} %get-tuple-element.20.env, bf16[416,512]{1,0:T(8,128)(2,1)S(1)} %get-tuple-element.21.coupling, bf16[3328,128]{1,0:T(8,128)(2,1)S(1)} %bitcast.7, bf16[64,2048]{1,0:T(8,128)(2,1)S(1)} %get-tuple-element.23.vector_rows, ...), custom_call_target="tpu_custom_call" | custom-call | tf_op jit(solution)/shard_map/first_image/pallas_call | solution.py:296
  14.2 2.0 %collective-permute-start.6 = (bf16[32,2048]{1,0:T(8,128)(2,1)S(1)}, bf16[32,2048]{1,0:T(8,128)(2,1)S(1)}, u32[]{:S(2)}, u32[]{:S(2)}) collective-permute-start(bf16[32,2048]{1,0:T(8,128)(2,1)S(1)} %get-tuple-element.26.own_here), channel_id=1, source_target_pairs={{0,2},{1,3},{2,0},{3,1},{4,8},{5,9},{6,10},{7,11},{8,4},{9,5},{10,... | collective-permute-start | bytes 393224 | tf_op jit(solution)/shard_map/ppermute | solution.py:42
  16.2 1.7 %collective-permute-start.4 = (bf16[32,2048]{1,0:T(8,128)(2,1)S(1)}, bf16[32,2048]{1,0:T(8,128)(2,1)S(1)}, u32[]{:S(2)}, u32[]{:S(2)}) collective-permute-start(bf16[32,2048]{1,0:T(8,128)(2,1)S(1)} %get-tuple-element.26.own_here), channel_id=1, source_target_pairs={{0,4},{1,5},{2,6},{3,7},{4,0},{5,1},{6,2},{7,3},{8,12},{9,13},{10,... | collective-permute-start | bytes 393224 | tf_op jit(solution)/shard_map/ppermute | solution.py:42
  17.9 0.0 collective-permute-start.3
  17.9 2.2 %collective-permute-done.6.odd_here = bf16[32,2048]{1,0:T(8,128)(2,1)S(1)} collective-permute-done((bf16[32,2048]{1,0:T(8,128)(2,1)S(1)}, bf16[32,2048]{1,0:T(8,128)(2,1)S(1)}, u32[]{:S(2)}, u32[]{:S(2)}) %collective-permute-start.6) | collective-permute-done | bytes 131104 | tf_op jit(solution)/shard_map/ppermute | solution.py:42
  20.0 0.0 collective-permute-start.7
  20.0 1.4 %collective-permute-done.4.even_here = bf16[32,2048]{1,0:T(8,128)(2,1)S(1)} collective-permute-done((bf16[32,2048]{1,0:T(8,128)(2,1)S(1)}, bf16[32,2048]{1,0:T(8,128)(2,1)S(1)}, u32[]{:S(2)}, u32[]{:S(2)}) %collective-permute-start.4) | collective-permute-done | bytes 131104 | tf_op jit(solution)/shard_map/ppermute | solution.py:42
  21.4 0.0 collective-permute-start.5
  21.5 0.1 sums.1
  21.6 0.0 collective-permute-done.3.own_there
  21.6 0.0 collective-permute-done.7.odd_there
  21.6 1.2 %collective-permute-done.5.even_there = bf16[32,2048]{1,0:T(8,128)(2,1)S(1)} collective-permute-done((bf16[32,2048]{1,0:T(8,128)(2,1)S(1)}, bf16[32,2048]{1,0:T(8,128)(2,1)S(1)}, u32[]{:S(2)}, u32[]{:S(2)}) %collective-permute-start.5) | collective-permute-done | bytes 131104 | tf_op jit(solution)/shard_map/ppermute | solution.py:20
  22.8 4.4 %second_image.1 = (f32[512,128]{1,0:T(8,128)S(1)}, f32[64,8,128]{2,1,0:T(8,128)S(1)}, f32[16,1,128]{2,1,0:T(1,128)S(1)}) custom-call(bf16[1024,192]{1,0:T(8,128)(2,1)S(1)} %get-tuple-element.20.env, bf16[416,512]{1,0:T(8,128)(2,1)S(1)} %get-tuple-element.21.coupling, bf16[3328,128]{1,0:T(8,128)(2,1)S(1)} %bitcast.8, ...), custom_call_target="tpu_custom_call" | custom-call | tf_op jit(solution)/shard_map/second_image/pallas_call | solution.py:296
  27.2 0.2 collective-permute-start.8
  27.4 11.2 %all_to_all.5.refs_4_ = f32[16,1,128]{2,1,0:T(1,128)S(1)} all-to-all(f32[16,1,128]{2,1,0:T(1,128)S(1)} %get-tuple-element.29), channel_id=1, replica_groups=mesh['groups'=2,'brow'=4,'bcol'=2,'mpo'=2] {'brow','bcol','mpo'}, dimensions={0} | all-to-all | bytes 16384 | tf_op jit(solution)/shard_map/all_to_all | solution.py:391
  38.6 0.0 collective-permute-done.8.refs_2_
  38.6 0.9 %outputs.1 = (bf16[512,128]{1,0:T(8,128)(2,1)}, bf16[512,128]{1,0:T(8,128)(2,1)}, f32[2,2]{1,0:T(2,128)}) custom-call(f32[512,128]{1,0:T(8,128)S(1)} %get-tuple-element.25.image.first.refs_0_, f32[512,128]{1,0:T(8,128)S(1)} %get-tuple-element.27.refs_1_, f32[64,8,128]{2,1,0:T(8,128)S(1)} %collective-permute-done.8.refs_2_, bf16[1024,128]{1,0:T(8,128)(2,1)S(1)} %bitcast.13, ...), custom_call_target="tpu_custom_call" | custom-call | tf_op jit(solution)/shard_map/outputs/pallas_call | solution.py:296
  (1 shorter events, 0.0 us)
Async XLA Ops:
  0.6 7.7 %collective-permute-start = (bf16[1024,128]{1,0:T(8,128)(2,1)}, bf16[1024,128]{1,0:T(8,128)(2,1)S(1)}, u32[]{:S(2)}, u32[]{:S(2)}) collective-permute-start(bf16[1024,128]{1,0:T(8,128)(2,1)} %bitcast.9), channel_id=1, source_target_pairs={{0,4},{1,3},{2,6},{3,1},{4,0},{5,9},{6,2},{7,11},{8,12},{9,5},{10,... | collective-permute-start | bytes 786440 | tf_op jit(solution)/shard_map/ppermute | solution.py:42
  3.7 2.2 %collective-permute-start.1 = (bf16[13,64,192]{2,1,0:T(8,128)(2,1)}, bf16[13,64,192]{2,1,0:T(8,128)(2,1)S(1)}, u32[]{:S(2)}, u32[]{:S(2)}) collective-permute-start(bf16[13,64,192]{2,1,0:T(8,128)(2,1)} %env_mine.1), channel_id=1, source_target_pairs={{0,1},{1,0},{2,3},{3,2},{4,5},{5,4},{6,7},{7,6},{8,9},{9,8},{10,11... | collective-permute-start | bytes 958472 | tf_op jit(solution)/shard_map/ppermute | solution.py:20
  3.7 0.7 %copy-start.3 = (s32[256]{0:T(256)S(1)}, s32[256]{0:T(256)}, u32[]{:S(2)}) copy-start(s32[256]{0:T(256)} %param.11) | copy-start | bytes 3076
  4.6 1.3 %copy-start.2 = (bf16[13,64,192]{2,1,0:T(8,128)(2,1)S(1)}, bf16[13,64,192]{2,1,0:T(8,128)(2,1)}, u32[]{:S(2)}) copy-start(bf16[13,64,192]{2,1,0:T(8,128)(2,1)} %env_mine.1) | copy-start | bytes 958468
  5.9 2.7 %copy-start.1 = (bf16[64,16,128]{2,1,0:T(8,128)(2,1)S(1)}, bf16[64,16,128]{2,1,0:T(8,128)(2,1)}, u32[]{:S(2)}) copy-start(bf16[64,16,128]{2,1,0:T(8,128)(2,1)} %param.6) | copy-start | bytes 786436
  8.3 1.5 %copy-start = (bf16[26,128,128]{2,1,0:T(8,128)(2,1)S(1)}, bf16[26,128,128]{2,1,0:T(8,128)(2,1)}, u32[]{:S(2)}) copy-start(bf16[26,128,128]{2,1,0:T(8,128)(2,1)} %param.8) | copy-start | bytes 2555908
  8.3 1.5 %collective-permute-start.2 = (bf16[1024,128]{1,0:T(8,128)(2,1)S(1)}, bf16[1024,128]{1,0:T(8,128)(2,1)S(1)}, u32[]{:S(2)}, u32[]{:S(2)}) collective-permute-start(bf16[1024,128]{1,0:T(8,128)(2,1)S(1)} %collective-permute-done.direct), channel_id=1, source_target_pairs={{0,1},{1,0},{2,3},{3,2},{4,5},{5,4},{6,7},{7,6},{8,9},{9,8},{10,11... | collective-permute-start | bytes 786440 | tf_op jit(solution)/shard_map/ppermute | solution.py:20
  14.2 5.8 %collective-permute-start.6 = (bf16[32,2048]{1,0:T(8,128)(2,1)S(1)}, bf16[32,2048]{1,0:T(8,128)(2,1)S(1)}, u32[]{:S(2)}, u32[]{:S(2)}) collective-permute-start(bf16[32,2048]{1,0:T(8,128)(2,1)S(1)} %get-tuple-element.26.own_here), channel_id=1, source_target_pairs={{0,2},{1,3},{2,0},{3,1},{4,8},{5,9},{6,10},{7,11},{8,4},{9,5},{10,... | collective-permute-start | bytes 393224 | tf_op jit(solution)/shard_map/ppermute | solution.py:42
  16.2 5.3 %collective-permute-start.4 = (bf16[32,2048]{1,0:T(8,128)(2,1)S(1)}, bf16[32,2048]{1,0:T(8,128)(2,1)S(1)}, u32[]{:S(2)}, u32[]{:S(2)}) collective-permute-start(bf16[32,2048]{1,0:T(8,128)(2,1)S(1)} %get-tuple-element.26.own_here), channel_id=1, source_target_pairs={{0,4},{1,5},{2,6},{3,7},{4,0},{5,1},{6,2},{7,3},{8,12},{9,13},{10,... | collective-permute-start | bytes 393224 | tf_op jit(solution)/shard_map/ppermute | solution.py:42
  17.9 3.7 %collective-permute-start.3 = (bf16[32,2048]{1,0:T(8,128)(2,1)S(1)}, bf16[32,2048]{1,0:T(8,128)(2,1)S(1)}, u32[]{:S(2)}, u32[]{:S(2)}) collective-permute-start(bf16[32,2048]{1,0:T(8,128)(2,1)S(1)} %get-tuple-element.26.own_here), channel_id=1, source_target_pairs={{0,1},{1,0},{2,3},{3,2},{4,5},{5,4},{6,7},{7,6},{8,9},{9,8},{10,11... | collective-permute-start | bytes 393224 | tf_op jit(solution)/shard_map/ppermute | solution.py:20
  20.0 1.6 %collective-permute-start.7 = (bf16[32,2048]{1,0:T(8,128)(2,1)S(1)}, bf16[32,2048]{1,0:T(8,128)(2,1)S(1)}, u32[]{:S(2)}, u32[]{:S(2)}) collective-permute-start(bf16[32,2048]{1,0:T(8,128)(2,1)S(1)} %collective-permute-done.6.odd_here), channel_id=1, source_target_pairs={{0,1},{1,0},{2,3},{3,2},{4,5},{5,4},{6,7},{7,6},{8,9},{9,8},{10,11... | collective-permute-start | bytes 393224 | tf_op jit(solution)/shard_map/ppermute | solution.py:20
  21.4 1.3 %collective-permute-start.5 = (bf16[32,2048]{1,0:T(8,128)(2,1)S(1)}, bf16[32,2048]{1,0:T(8,128)(2,1)S(1)}, u32[]{:S(2)}, u32[]{:S(2)}) collective-permute-start(bf16[32,2048]{1,0:T(8,128)(2,1)S(1)} %collective-permute-done.4.even_here), channel_id=1, source_target_pairs={{0,1},{1,0},{2,3},{3,2},{4,5},{5,4},{6,7},{7,6},{8,9},{9,8},{10,11... | collective-permute-start | bytes 393224 | tf_op jit(solution)/shard_map/ppermute | solution.py:20
  27.2 11.4 %collective-permute-start.8 = (f32[64,8,128]{2,1,0:T(8,128)S(1)}, f32[64,8,128]{2,1,0:T(8,128)S(1)}, u32[]{:S(2)}, u32[]{:S(2)}) collective-permute-start(f32[64,8,128]{2,1,0:T(8,128)S(1)} %get-tuple-element.28), channel_id=1, source_target_pairs={{0,1},{1,0},{2,3},{3,2},{4,5},{5,4},{6,7},{7,6},{8,9},{9,8},{10,11... | collective-permute-start | bytes 786440 | tf_op jit(solution)/shard_map/ppermute | solution.py:20

commit v8 on v7

--- a/solution.py
+++ b/solution.py
@@ -10,7 +10,7 @@
 GROW = 1.0 / SHRINK
 SLOT = 32
 LOCAL = 4
-GROUP = 8
+GROUP = 16
 VMEM_LIMIT = 40 * 2**20
 SHORT = pl.CostEstimate(flops=10**9, bytes_accessed=2**21, transcendentals=0)
 WHOLE = pl.BlockSpec(memory_space=pltpu.VMEM)

time: 39.7 us -> 39.6 us (level)
  no operation moved by 1% of the time
where the time goes in v8:
time: 39.6 us; the launch traced here: 39.4 us
  Pallas kernels  12.2 us (31%)
  blocking collectives  11.3 us (29%)
  starting transfers between devices  7.28 us (18%)
  waiting for transfers between devices  5.82 us (15%)
  other arithmetic  1.35 us (3%)
  local copies, waits for them, and re-layouts  0.84 us (2%)
  between operations  0.7 us (2%)
    pallas_call x6, Pallas kernels, call(): pl.pallas_call(kernel, out_shape=tuple((jax.ShapeDtypeStruct(shape, dtype...  12.2 us
    all_to_all x1, blocking collectives, per_device(): gathered = lax.all_to_all(totals, axes, 0, 0)  11.3 us
    ppermute x3, starting transfers between devices, trade(): return lax.ppermute(x, ('brow', 'bcol', 'mpo'), pairs)  6.75 us
    ppermute x3, waiting for transfers between devices, trade(): return lax.ppermute(x, ('brow', 'bcol', 'mpo'), pairs)  3.82 us
    ppermute x6, waiting for transfers between devices, swap_cores(): return lax.ppermute(x, 'mpo', [(0, 1), (1, 0)])  1.99 us
    concatenate x1, other arithmetic, per_device(): both = jnp.concatenate([mpo_left, mpo_right], axis=0)  1.2 us
  transfers between devices with their start and end apart: 9, of which 5 were waited for; matrix products, arithmetic and copies ran while one was open for 4% of the time, Pallas kernels for 7%

profile of v8, /device:TPU:0, one launch (start us, length us, event | category | flops | bytes accessed | tf_op | source)
XLA Modules:
  0.0 39.4 jit_solution(16593204348630037531)
XLA Ops:
  0.6 3.1 %collective-permute-start = (bf16[1024,128]{1,0:T(8,128)(2,1)}, bf16[1024,128]{1,0:T(8,128)(2,1)S(1)}, u32[]{:S(2)}, u32[]{:S(2)}) collective-permute-start(bf16[1024,128]{1,0:T(8,128)(2,1)} %bitcast.9), channel_id=1, source_target_pairs={{0,4},{1,3},{2,6},{3,1},{4,0},{5,9},{6,2},{7,11},{8,12},{9,5},{10,... | collective-permute-start | bytes 786440 | tf_op jit(solution)/shard_map/ppermute | solution.py:42
  3.7 0.0 collective-permute-start.1
  3.7 0.0 copy-start.3
  3.7 0.7 %copy-done.3 = s32[256]{0:T(256)S(1)} copy-done((s32[256]{0:T(256)S(1)}, s32[256]{0:T(256)}, u32[]{:S(2)}) %copy-start.3) | copy-done | bytes 1048
  4.4 0.1 pad_add_fusion
  4.5 0.1 dynamic_slice.6
  4.6 0.1 dynamic_slice.7
  4.6 0.0 copy-start.2
  4.6 1.2 %pad_maximum_fusion = f32[52,26,4,4]{1,3,2,0:T(4,128)S(1)} fusion(f32[26,26,4,4]{1,3,2,0:T(4,128)} %param.10, f32[26,26,4,4]{1,3,2,0:T(4,128)} %param.9), kind=kLoop, calls=%fused_computation | loop fusion | flops 21632 | bytes 173056 | tf_op jit(solution)/shard_map/concatenate | solution.py:331
  5.8 0.1 compare_convert_fusion.mask
  5.9 0.0 collective-permute-done.1.env_there
  5.9 0.0 copy-done.2
  5.9 0.0 copy-start.1
  5.9 2.1 %operands.1 = (bf16[1024,192]{1,0:T(8,128)(2,1)S(1)}, bf16[416,512]{1,0:T(8,128)(2,1)S(1)}) custom-call(bf16[13,64,192]{2,1,0:T(8,128)(2,1)S(1)} %copy-done.2, bf16[13,64,192]{2,1,0:T(8,128)(2,1)S(1)} %collective-permute-done.1.env_there, f32[32,192]{1,0:T(8,128)S(1)} %compare_convert_fusion.mask, f32[832,26]{1,0:T(8,128)S(1)} %bitcast.14), custom_call_target="tpu_custom_call" | custom-call | flops 4000000000 | bytes 8388608 | tf_op jit(solution)/shard_map/operands/pallas_call | solution.py:296
  8.0 0.2 collective-permute-done.direct
  8.3 0.0 copy-start
  8.3 0.4 collective-permute-start.2
  8.6 0.0 copy-done.1
  8.6 0.4 %rows.1 = (bf16[64,2048]{1,0:T(8,128)(2,1)S(1)}, bf16[64,2048]{1,0:T(8,128)(2,1)S(1)}) custom-call(bf16[1024,128]{1,0:T(8,128)(2,1)S(1)} %bitcast.10, bf16[1024,128]{1,0:T(8,128)(2,1)S(1)} %collective-permute-done.direct), custom_call_target="tpu_custom_call" | custom-call | flops 1000000000 | bytes 2097152 | tf_op jit(solution)/shard_map/rows/pallas_call | solution.py:296
  9.1 0.8 %collective-permute-done.2.passed_in = bf16[1024,128]{1,0:T(8,128)(2,1)S(1)} collective-permute-done((bf16[1024,128]{1,0:T(8,128)(2,1)S(1)}, bf16[1024,128]{1,0:T(8,128)(2,1)S(1)}, u32[]{:S(2)}, u32[]{:S(2)}) %collective-permute-start.2) | collective-permute-done | bytes 262176 | tf_op jit(solution)/shard_map/ppermute | solution.py:20
  9.8 0.0 copy-done
  9.8 4.3 %first_image.1 = (f32[512,128]{1,0:T(8,128)S(1)}, bf16[32,2048]{1,0:T(8,128)(2,1)S(1)}) custom-call(bf16[1024,192]{1,0:T(8,128)(2,1)S(1)} %get-tuple-element.20.env, bf16[416,512]{1,0:T(8,128)(2,1)S(1)} %get-tuple-element.21.coupling, bf16[3328,128]{1,0:T(8,128)(2,1)S(1)} %bitcast.7, bf16[64,2048]{1,0:T(8,128)(2,1)S(1)} %get-tuple-element.23.vector_rows, ...), custom_call_target="tpu_custom_call" | custom-call | tf_op jit(solution)/shard_map/first_image/pallas_call | solution.py:296
  14.2 2.0 %collective-permute-start.6 = (bf16[32,2048]{1,0:T(8,128)(2,1)S(1)}, bf16[32,2048]{1,0:T(8,128)(2,1)S(1)}, u32[]{:S(2)}, u32[]{:S(2)}) collective-permute-start(bf16[32,2048]{1,0:T(8,128)(2,1)S(1)} %get-tuple-element.26.own_here), channel_id=1, source_target_pairs={{0,2},{1,3},{2,0},{3,1},{4,8},{5,9},{6,10},{7,11},{8,4},{9,5},{10,... | collective-permute-start | bytes 393224 | tf_op jit(solution)/shard_map/ppermute | solution.py:42
  16.2 1.7 %collective-permute-start.4 = (bf16[32,2048]{1,0:T(8,128)(2,1)S(1)}, bf16[32,2048]{1,0:T(8,128)(2,1)S(1)}, u32[]{:S(2)}, u32[]{:S(2)}) collective-permute-start(bf16[32,2048]{1,0:T(8,128)(2,1)S(1)} %get-tuple-element.26.own_here), channel_id=1, source_target_pairs={{0,4},{1,5},{2,6},{3,7},{4,0},{5,1},{6,2},{7,3},{8,12},{9,13},{10,... | collective-permute-start | bytes 393224 | tf_op jit(solution)/shard_map/ppermute | solution.py:42
  17.8 0.0 collective-permute-start.3
  17.8 2.2 %collective-permute-done.6.odd_here = bf16[32,2048]{1,0:T(8,128)(2,1)S(1)} collective-permute-done((bf16[32,2048]{1,0:T(8,128)(2,1)S(1)}, bf16[32,2048]{1,0:T(8,128)(2,1)S(1)}, u32[]{:S(2)}, u32[]{:S(2)}) %collective-permute-start.6) | collective-permute-done | bytes 131104 | tf_op jit(solution)/shard_map/ppermute | solution.py:42
  20.0 0.0 collective-permute-start.7
  20.0 1.4 %collective-permute-done.4.even_here = bf16[32,2048]{1,0:T(8,128)(2,1)S(1)} collective-permute-done((bf16[32,2048]{1,0:T(8,128)(2,1)S(1)}, bf16[32,2048]{1,0:T(8,128)(2,1)S(1)}, u32[]{:S(2)}, u32[]{:S(2)}) %collective-permute-start.4) | collective-permute-done | bytes 131104 | tf_op jit(solution)/shard_map/ppermute | solution.py:42
  21.4 0.0 collective-permute-start.5
  21.4 0.1 sums.1
  21.5 0.0 collective-permute-done.3.own_there
  21.5 0.0 collective-permute-done.7.odd_there
  21.6 1.2 %collective-permute-done.5.even_there = bf16[32,2048]{1,0:T(8,128)(2,1)S(1)} collective-permute-done((bf16[32,2048]{1,0:T(8,128)(2,1)S(1)}, bf16[32,2048]{1,0:T(8,128)(2,1)S(1)}, u32[]{:S(2)}, u32[]{:S(2)}) %collective-permute-start.5) | collective-permute-done | bytes 131104 | tf_op jit(solution)/shard_map/ppermute | solution.py:20
  22.8 4.3 %second_image.1 = (f32[512,128]{1,0:T(8,128)S(1)}, f32[64,8,128]{2,1,0:T(8,128)S(1)}, f32[16,1,128]{2,1,0:T(1,128)S(1)}) custom-call(bf16[1024,192]{1,0:T(8,128)(2,1)S(1)} %get-tuple-element.20.env, bf16[416,512]{1,0:T(8,128)(2,1)S(1)} %get-tuple-element.21.coupling, bf16[3328,128]{1,0:T(8,128)(2,1)S(1)} %bitcast.8, ...), custom_call_target="tpu_custom_call" | custom-call | tf_op jit(solution)/shard_map/second_image/pallas_call | solution.py:296
  27.1 0.2 collective-permute-start.8
  27.3 11.3 %all_to_all.5.refs_4_ = f32[16,1,128]{2,1,0:T(1,128)S(1)} all-to-all(f32[16,1,128]{2,1,0:T(1,128)S(1)} %get-tuple-element.29), channel_id=1, replica_groups=mesh['groups'=2,'brow'=4,'bcol'=2,'mpo'=2] {'brow','bcol','mpo'}, dimensions={0} | all-to-all | bytes 16384 | tf_op jit(solution)/shard_map/all_to_all | solution.py:391
  38.5 0.0 collective-permute-done.8.refs_2_
  38.5 0.9 %outputs.1 = (bf16[512,128]{1,0:T(8,128)(2,1)}, bf16[512,128]{1,0:T(8,128)(2,1)}, f32[2,2]{1,0:T(2,128)}) custom-call(f32[512,128]{1,0:T(8,128)S(1)} %get-tuple-element.25.image.first.refs_0_, f32[512,128]{1,0:T(8,128)S(1)} %get-tuple-element.27.refs_1_, f32[64,8,128]{2,1,0:T(8,128)S(1)} %collective-permute-done.8.refs_2_, bf16[1024,128]{1,0:T(8,128)(2,1)S(1)} %bitcast.13, ...), custom_call_target="tpu_custom_call" | custom-call | tf_op jit(solution)/shard_map/outputs/pallas_call | solution.py:296
  (1 shorter events, 0.0 us)
Async XLA Ops:
  0.6 7.7 %collective-permute-start = (bf16[1024,128]{1,0:T(8,128)(2,1)}, bf16[1024,128]{1,0:T(8,128)(2,1)S(1)}, u32[]{:S(2)}, u32[]{:S(2)}) collective-permute-start(bf16[1024,128]{1,0:T(8,128)(2,1)} %bitcast.9), channel_id=1, source_target_pairs={{0,4},{1,3},{2,6},{3,1},{4,0},{5,9},{6,2},{7,11},{8,12},{9,5},{10,... | collective-permute-start | bytes 786440 | tf_op jit(solution)/shard_map/ppermute | solution.py:42
  3.7 2.2 %collective-permute-start.1 = (bf16[13,64,192]{2,1,0:T(8,128)(2,1)}, bf16[13,64,192]{2,1,0:T(8,128)(2,1)S(1)}, u32[]{:S(2)}, u32[]{:S(2)}) collective-permute-start(bf16[13,64,192]{2,1,0:T(8,128)(2,1)} %env_mine.1), channel_id=1, source_target_pairs={{0,1},{1,0},{2,3},{3,2},{4,5},{5,4},{6,7},{7,6},{8,9},{9,8},{10,11... | collective-permute-start | bytes 958472 | tf_op jit(solution)/shard_map/ppermute | solution.py:20
  3.7 0.7 %copy-start.3 = (s32[256]{0:T(256)S(1)}, s32[256]{0:T(256)}, u32[]{:S(2)}) copy-start(s32[256]{0:T(256)} %param.11) | copy-start | bytes 3076
  4.6 1.3 %copy-start.2 = (bf16[13,64,192]{2,1,0:T(8,128)(2,1)S(1)}, bf16[13,64,192]{2,1,0:T(8,128)(2,1)}, u32[]{:S(2)}) copy-start(bf16[13,64,192]{2,1,0:T(8,128)(2,1)} %env_mine.1) | copy-start | bytes 958468
  5.9 2.7 %copy-start.1 = (bf16[64,16,128]{2,1,0:T(8,128)(2,1)S(1)}, bf16[64,16,128]{2,1,0:T(8,128)(2,1)}, u32[]{:S(2)}) copy-start(bf16[64,16,128]{2,1,0:T(8,128)(2,1)} %param.6) | copy-start | bytes 786436
  8.3 1.5 %copy-start = (bf16[26,128,128]{2,1,0:T(8,128)(2,1)S(1)}, bf16[26,128,128]{2,1,0:T(8,128)(2,1)}, u32[]{:S(2)}) copy-start(bf16[26,128,128]{2,1,0:T(8,128)(2,1)} %param.8) | copy-start | bytes 2555908
  8.3 1.5 %collective-permute-start.2 = (bf16[1024,128]{1,0:T(8,128)(2,1)S(1)}, bf16[1024,128]{1,0:T(8,128)(2,1)S(1)}, u32[]{:S(2)}, u32[]{:S(2)}) collective-permute-start(bf16[1024,128]{1,0:T(8,128)(2,1)S(1)} %collective-permute-done.direct), channel_id=1, source_target_pairs={{0,1},{1,0},{2,3},{3,2},{4,5},{5,4},{6,7},{7,6},{8,9},{9,8},{10,11... | collective-permute-start | bytes 786440 | tf_op jit(solution)/shard_map/ppermute | solution.py:20
  14.2 5.8 %collective-permute-start.6 = (bf16[32,2048]{1,0:T(8,128)(2,1)S(1)}, bf16[32,2048]{1,0:T(8,128)(2,1)S(1)}, u32[]{:S(2)}, u32[]{:S(2)}) collective-permute-start(bf16[32,2048]{1,0:T(8,128)(2,1)S(1)} %get-tuple-element.26.own_here), channel_id=1, source_target_pairs={{0,2},{1,3},{2,0},{3,1},{4,8},{5,9},{6,10},{7,11},{8,4},{9,5},{10,... | collective-permute-start | bytes 393224 | tf_op jit(solution)/shard_map/ppermute | solution.py:42
  16.2 5.3 %collective-permute-start.4 = (bf16[32,2048]{1,0:T(8,128)(2,1)S(1)}, bf16[32,2048]{1,0:T(8,128)(2,1)S(1)}, u32[]{:S(2)}, u32[]{:S(2)}) collective-permute-start(bf16[32,2048]{1,0:T(8,128)(2,1)S(1)} %get-tuple-element.26.own_here), channel_id=1, source_target_pairs={{0,4},{1,5},{2,6},{3,7},{4,0},{5,1},{6,2},{7,3},{8,12},{9,13},{10,... | collective-permute-start | bytes 393224 | tf_op jit(solution)/shard_map/ppermute | solution.py:42
  17.8 3.7 %collective-permute-start.3 = (bf16[32,2048]{1,0:T(8,128)(2,1)S(1)}, bf16[32,2048]{1,0:T(8,128)(2,1)S(1)}, u32[]{:S(2)}, u32[]{:S(2)}) collective-permute-start(bf16[32,2048]{1,0:T(8,128)(2,1)S(1)} %get-tuple-element.26.own_here), channel_id=1, source_target_pairs={{0,1},{1,0},{2,3},{3,2},{4,5},{5,4},{6,7},{7,6},{8,9},{9,8},{10,11... | collective-permute-start | bytes 393224 | tf_op jit(solution)/shard_map/ppermute | solution.py:20
  20.0 1.6 %collective-permute-start.7 = (bf16[32,2048]{1,0:T(8,128)(2,1)S(1)}, bf16[32,2048]{1,0:T(8,128)(2,1)S(1)}, u32[]{:S(2)}, u32[]{:S(2)}) collective-permute-start(bf16[32,2048]{1,0:T(8,128)(2,1)S(1)} %collective-permute-done.6.odd_here), channel_id=1, source_target_pairs={{0,1},{1,0},{2,3},{3,2},{4,5},{5,4},{6,7},{7,6},{8,9},{9,8},{10,11... | collective-permute-start | bytes 393224 | tf_op jit(solution)/shard_map/ppermute | solution.py:20
  21.4 1.3 %collective-permute-start.5 = (bf16[32,2048]{1,0:T(8,128)(2,1)S(1)}, bf16[32,2048]{1,0:T(8,128)(2,1)S(1)}, u32[]{:S(2)}, u32[]{:S(2)}) collective-permute-start(bf16[32,2048]{1,0:T(8,128)(2,1)S(1)} %collective-permute-done.4.even_here), channel_id=1, source_target_pairs={{0,1},{1,0},{2,3},{3,2},{4,5},{5,4},{6,7},{7,6},{8,9},{9,8},{10,11... | collective-permute-start | bytes 393224 | tf_op jit(solution)/shard_map/ppermute | solution.py:20
  27.1 11.4 %collective-permute-start.8 = (f32[64,8,128]{2,1,0:T(8,128)S(1)}, f32[64,8,128]{2,1,0:T(8,128)S(1)}, u32[]{:S(2)}, u32[]{:S(2)}) collective-permute-start(f32[64,8,128]{2,1,0:T(8,128)S(1)} %get-tuple-element.28), channel_id=1, source_target_pairs={{0,1},{1,0},{2,3},{3,2},{4,5},{5,4},{6,7},{7,6},{8,9},{9,8},{10,11... | collective-permute-start | bytes 786440 | tf_op jit(solution)/shard_map/ppermute | solution.py:20

commit v9 on v7

--- a/solution.py
+++ b/solution.py
@@ -57,8 +57,8 @@
 
 def prepare_kernel(
     env_mine, env_there, mask, both_mpo,
-    env, coupling,
-    by_bond, left_pad, right_pad, left_rows, right_rows, spread,
+    env_one, env_two, coupling,
+    env, by_bond, left_pad, right_pad, left_rows, right_rows, spread,
 ):
     core = lax.axis_index("mpo")
     share, rows, _ = env_mine.shape
@@ -116,14 +116,31 @@
             kept = jnp.where(mask[row : row + 1, low : low + width] > 0.0, piece, 0.0)
             env[row * SLOT : (row + 1) * SLOT, low : low + width] = kept.astype(jnp.bfloat16)
 
-
-def apply_steps(env, coupling, right, extended, contracted, mixed, image):
+    direct, passed = halo_places(rows)
+    even = lax.rem(lax.axis_index("brow"), 2) == 0
+    above, below = jnp.where(even, 2 * rows, 0), jnp.where(even, 0, 2 * rows)
+    shares = [base + share * half for base in (rows, above, below) for share in (core, 1 - core)]
+    for target, starts in ((env_one, (rows, direct, passed)), (env_two, shares)):
+        size = band // len(starts)
+        taken = lax.broadcasted_iota(jnp.int32, (band, band), 0)
+        place = lax.broadcasted_iota(jnp.int32, (band, band), 1)
+        chosen = jnp.zeros((band, band), jnp.bool_)
+        for index, start in enumerate(starts):
+            inside = (place >= index * size) & (place < (index + 1) * size)
+            chosen = chosen | (inside & (taken == place + (start - index * size)))
+        order = jnp.where(chosen, 1.0, 0.0).astype(jnp.bfloat16)
+        moved = jnp.dot(env[...], order, preferred_element_type=jnp.float32)
+        target[...] = moved.astype(jnp.bfloat16)
+
+
+def apply_steps(env, coupling, right, pieces, contracted, mixed, image):
     groups, depth, width = contracted.shape
     lanes = right.shape[1]
     group = width // lanes
     states = depth // SLOT
     bonds = mixed.shape[1] // lanes
-    product = jnp.dot(env[...], extended[...], preferred_element_type=jnp.float32)
+    extended = jnp.concatenate([piece[...] for piece in pieces], axis=0)
+    product = jnp.dot(env[...], extended, preferred_element_type=jnp.float32)
     product = product.astype(jnp.bfloat16)
     for state in range(states):
         place = state % LOCAL * LOCAL + state // LOCAL
@@ -181,21 +198,19 @@
 def first_kernel(
     env, coupling, right, vector_rows, direct_rows, passed_in,
     image, image_rows,
-    wide, extended, contracted, mixed,
+    wide, passed_rows, contracted, mixed,
 ):
     rows = vector_rows.shape[0]
     states = passed_in.shape[0] // rows
     half = image.shape[0]
-    direct, passed = halo_places(rows)
-    extended[rows : 2 * rows, :] = vector_rows[...]
-    extended[pl.ds(direct, rows), :] = direct_rows[...]
     wide[...] = passed_in[...].astype(jnp.float32)
 
     def store(columns, piece):
-        extended[pl.ds(passed, rows), columns] = piece
+        passed_rows[:, columns] = piece
 
     states_apart(wide, rows, states, store)
-    apply_steps(env, coupling, right, extended, contracted, mixed, image)
+    pieces = (vector_rows, direct_rows, passed_rows)
+    apply_steps(env, coupling, right, pieces, contracted, mixed, image)
 
     def store_rows(columns, piece):
         image_rows[:, columns] = piece
@@ -219,20 +234,13 @@
     env, coupling, right, own_here, own_there, even_here, even_there, odd_here, odd_there,
     first, vector, sums,
     image, sent, totals,
-    extended, contracted, mixed,
+    contracted, mixed,
 ):
     part = own_here.shape[0]
-    rows = 2 * part
     half = first.shape[0]
     core = lax.axis_index("mpo")
-    even = lax.rem(lax.axis_index("brow"), 2) == 0
-    above, below = jnp.where(even, 2 * rows, 0), jnp.where(even, 0, 2 * rows)
-    for base, here, there in (
-        (rows, own_here, own_there), (above, even_here, even_there), (below, odd_here, odd_there)
-    ):
-        extended[pl.ds(pl.multiple_of(base + core * part, part), part), :] = here[...]
-        extended[pl.ds(pl.multiple_of(base + (1 - core) * part, part), part), :] = there[...]
-    apply_steps(env, coupling, right, extended, contracted, mixed, image)
+    pieces = (own_here, own_there, even_here, even_there, odd_here, odd_there)
+    apply_steps(env, coupling, right, pieces, contracted, mixed, image)
     out = image[...]
     states = half // part
     sent[0:part] = state_half(first[...], states, 1 - core)
@@ -330,14 +338,16 @@
     mask = (own_labels[:, None] == partner[None, :]).astype(f32)
     both = jnp.concatenate([mpo_left, mpo_right], axis=0)
     both = jnp.transpose(both, (0, 2, 3, 1)).reshape(2 * bonds * states, bonds)
-    env, coupling = call(
+    env_one, env_two, coupling = call(
         prepare_kernel,
         (left_env, env_there, mask, both),
         (
             ((half * SLOT, band), bf16),
+            ((half * SLOT, band), bf16),
             ((bonds * states, states * SLOT), bf16),
         ),
         (
+            ((half * SLOT, band), bf16),
             ((-(-band // 128) * SLOT * half, 128), f32),
             ((SLOT * states, 128), f32),
             ((SLOT * states, 128), f32),
@@ -348,12 +358,11 @@
         "operands",
         cost=pl.CostEstimate(flops=4 * 10**9, bytes_accessed=2**23, transcendentals=0),
     )
-    direct_one, env, coupling = lax.optimization_barrier((direct_one, env, coupling))
+    direct_one, env_one, coupling = lax.optimization_barrier((direct_one, env_one, coupling))
     passed_one = swap_cores(direct_one)
     right = right_env.reshape(bonds * columns, columns)
 
     work = (
-        ((3 * rows, states * columns), bf16),
         ((half // GROUP, states * SLOT, GROUP * columns), bf16),
         ((size, bonds * columns), bf16),
     )
@@ -364,9 +373,9 @@
     )
     first, first_rows = call(
         first_kernel,
-        (env, coupling, right, vector_rows, direct_rows, passed_one),
+        (env_one, coupling, right, vector_rows, direct_rows, passed_one),
         (((size, columns), f32), ((half, states * columns), bf16)),
-        (wide,) + work,
+        (wide, laid) + work,
         "first_image",
     )
     (sums,) = call(sums_kernel, (first, flat), (((8, columns), f32),), (), "sums", cost=SHORT)
@@ -378,7 +387,7 @@
 
     second, sent, totals = call(
         second_kernel,
-        (env, coupling, right, *pieces, first, flat, sums),
+        (env_two, coupling, right, *pieces, first, flat, sums),
         (
             ((size, columns), f32),
             ((2 * half, half_states, columns), f32),

time: 39.7 us -> 39.6 us (level)
  transfers between devices with their start and end apart: 9 -> 9, of which waited for: 5 -> 4; matrix products, arithmetic and copies ran while one was open for 4% -> 4% of each run, Pallas kernels for 7% -> 8%
where the time goes in v9:
time: 39.6 us; the launch traced here: 39.4 us
  Pallas kernels  12.5 us (32%)
  blocking collectives  11.1 us (28%)
  starting transfers between devices  7.18 us (18%)
  waiting for transfers between devices  5.7 us (14%)
  other arithmetic  1.35 us (3%)
  local copies, waits for them, and re-layouts  0.84 us (2%)
  between operations  0.68 us (2%)
    pallas_call x6, Pallas kernels, call(): pl.pallas_call(kernel, out_shape=tuple((jax.ShapeDtypeStruct(shape, dtype...  12.5 us
    all_to_all x1, blocking collectives, per_device(): gathered = lax.all_to_all(totals, axes, 0, 0)  11.1 us
    ppermute x3, starting transfers between devices, trade(): return lax.ppermute(x, ('brow', 'bcol', 'mpo'), pairs)  6.42 us
    ppermute x3, waiting for transfers between devices, trade(): return lax.ppermute(x, ('brow', 'bcol', 'mpo'), pairs)  3.72 us
    ppermute x6, waiting for transfers between devices, swap_cores(): return lax.ppermute(x, 'mpo', [(0, 1), (1, 0)])  1.98 us
    concatenate x1, other arithmetic, per_device(): both = jnp.concatenate([mpo_left, mpo_right], axis=0)  1.2 us
  transfers between devices with their start and end apart: 9, of which 4 were waited for; matrix products, arithmetic and copies ran while one was open for 4% of the time, Pallas kernels for 8%

profile of v9, /device:TPU:0, one launch (start us, length us, event | category | flops | bytes accessed | tf_op | source)
XLA Modules:
  0.0 39.4 jit_solution(2060064614801419795)
XLA Ops:
  0.6 3.1 %collective-permute-start = (bf16[1024,128]{1,0:T(8,128)(2,1)}, bf16[1024,128]{1,0:T(8,128)(2,1)S(1)}, u32[]{:S(2)}, u32[]{:S(2)}) collective-permute-start(bf16[1024,128]{1,0:T(8,128)(2,1)} %bitcast.9), channel_id=1, source_target_pairs={{0,4},{1,3},{2,6},{3,1},{4,0},{5,9},{6,2},{7,11},{8,12},{9,5},{10,... | collective-permute-start | bytes 786440 | tf_op jit(solution)/shard_map/ppermute | solution.py:42
  3.7 0.0 collective-permute-start.1
  3.7 0.0 copy-start.3
  3.7 0.7 %copy-done.3 = s32[256]{0:T(256)S(1)} copy-done((s32[256]{0:T(256)S(1)}, s32[256]{0:T(256)}, u32[]{:S(2)}) %copy-start.3) | copy-done | bytes 1048
  4.4 0.1 pad_add_fusion
  4.5 0.1 dynamic_slice.6
  4.6 0.1 dynamic_slice.7
  4.6 0.0 copy-start.2
  4.6 1.2 %pad_maximum_fusion = f32[52,26,4,4]{1,3,2,0:T(4,128)S(1)} fusion(f32[26,26,4,4]{1,3,2,0:T(4,128)} %param.10, f32[26,26,4,4]{1,3,2,0:T(4,128)} %param.9), kind=kLoop, calls=%fused_computation | loop fusion | flops 21632 | bytes 173056 | tf_op jit(solution)/shard_map/concatenate | solution.py:339
  5.8 0.1 compare_convert_fusion.mask
  5.9 0.0 collective-permute-done.1.env_there
  5.9 0.0 copy-done.2
  5.9 0.0 copy-start.1
  5.9 2.5 %operands.1 = (bf16[1024,192]{1,0:T(8,128)(2,1)S(1)}, bf16[1024,192]{1,0:T(8,128)(2,1)S(1)}, bf16[416,512]{1,0:T(8,128)(2,1)S(1)}) custom-call(bf16[13,64,192]{2,1,0:T(8,128)(2,1)S(1)} %copy-done.2, bf16[13,64,192]{2,1,0:T(8,128)(2,1)S(1)} %collective-permute-done.1.env_there, f32[32,192]{1,0:T(8,128)S(1)} %compare_convert_fusion.mask, f32[832,26]{1,0:T(8,128)S(1)} %bitcast.14), custom_call_target="tpu_custom_call" | custom-call | flops 4000000000 | bytes 8388608 | tf_op jit(solution)/shard_map/operands/pallas_call | solution.py:304
  8.4 0.0 collective-permute-done.direct
  8.4 0.0 copy-start
  8.4 0.6 %collective-permute-start.2 = (bf16[1024,128]{1,0:T(8,128)(2,1)S(1)}, bf16[1024,128]{1,0:T(8,128)(2,1)S(1)}, u32[]{:S(2)}, u32[]{:S(2)}) collective-permute-start(bf16[1024,128]{1,0:T(8,128)(2,1)S(1)} %collective-permute-done.direct), channel_id=1, source_target_pairs={{0,1},{1,0},{2,3},{3,2},{4,5},{5,4},{6,7},{7,6},{8,9},{9,8},{10,11... | collective-permute-start | bytes 786440 | tf_op jit(solution)/shard_map/ppermute | solution.py:20
  9.0 0.0 copy-done.1
  9.0 0.4 %rows.1 = (bf16[64,2048]{1,0:T(8,128)(2,1)S(1)}, bf16[64,2048]{1,0:T(8,128)(2,1)S(1)}) custom-call(bf16[1024,128]{1,0:T(8,128)(2,1)S(1)} %bitcast.10, bf16[1024,128]{1,0:T(8,128)(2,1)S(1)} %collective-permute-done.direct), custom_call_target="tpu_custom_call" | custom-call | flops 1000000000 | bytes 2097152 | tf_op jit(solution)/shard_map/rows/pallas_call | solution.py:304
  9.4 0.7 %collective-permute-done.2.passed_in = bf16[1024,128]{1,0:T(8,128)(2,1)S(1)} collective-permute-done((bf16[1024,128]{1,0:T(8,128)(2,1)S(1)}, bf16[1024,128]{1,0:T(8,128)(2,1)S(1)}, u32[]{:S(2)}, u32[]{:S(2)}) %collective-permute-start.2) | collective-permute-done | bytes 262176 | tf_op jit(solution)/shard_map/ppermute | solution.py:20
  10.2 0.0 copy-done
  10.2 4.4 %first_image.1 = (f32[512,128]{1,0:T(8,128)S(1)}, bf16[32,2048]{1,0:T(8,128)(2,1)S(1)}) custom-call(bf16[1024,192]{1,0:T(8,128)(2,1)S(1)} %get-tuple-element.21.env, bf16[416,512]{1,0:T(8,128)(2,1)S(1)} %get-tuple-element.22.coupling, bf16[3328,128]{1,0:T(8,128)(2,1)S(1)} %bitcast.7, bf16[64,2048]{1,0:T(8,128)(2,1)S(1)} %get-tuple-element.24.vector_rows, ...), custom_call_target="tpu_custom_call" | custom-call | tf_op jit(solution)/shard_map/first_image/pallas_call | solution.py:304
  14.5 1.7 %collective-permute-start.6 = (bf16[32,2048]{1,0:T(8,128)(2,1)S(1)}, bf16[32,2048]{1,0:T(8,128)(2,1)S(1)}, u32[]{:S(2)}, u32[]{:S(2)}) collective-permute-start(bf16[32,2048]{1,0:T(8,128)(2,1)S(1)} %get-tuple-element.28.own_here), channel_id=1, source_target_pairs={{0,2},{1,3},{2,0},{3,1},{4,8},{5,9},{6,10},{7,11},{8,4},{9,5},{10,... | collective-permute-start | bytes 393224 | tf_op jit(solution)/shard_map/ppermute | solution.py:42
  16.2 1.7 %collective-permute-start.4 = (bf16[32,2048]{1,0:T(8,128)(2,1)S(1)}, bf16[32,2048]{1,0:T(8,128)(2,1)S(1)}, u32[]{:S(2)}, u32[]{:S(2)}) collective-permute-start(bf16[32,2048]{1,0:T(8,128)(2,1)S(1)} %get-tuple-element.28.own_here), channel_id=1, source_target_pairs={{0,4},{1,5},{2,6},{3,7},{4,0},{5,1},{6,2},{7,3},{8,12},{9,13},{10,... | collective-permute-start | bytes 393224 | tf_op jit(solution)/shard_map/ppermute | solution.py:42
  17.9 0.0 collective-permute-start.3
  17.9 2.5 %collective-permute-done.6.odd_here = bf16[32,2048]{1,0:T(8,128)(2,1)S(1)} collective-permute-done((bf16[32,2048]{1,0:T(8,128)(2,1)S(1)}, bf16[32,2048]{1,0:T(8,128)(2,1)S(1)}, u32[]{:S(2)}, u32[]{:S(2)}) %collective-permute-start.6) | collective-permute-done | bytes 131104 | tf_op jit(solution)/shard_map/ppermute | solution.py:42
  20.4 0.0 collective-permute-start.7
  20.4 1.2 %collective-permute-done.4.even_here = bf16[32,2048]{1,0:T(8,128)(2,1)S(1)} collective-permute-done((bf16[32,2048]{1,0:T(8,128)(2,1)S(1)}, bf16[32,2048]{1,0:T(8,128)(2,1)S(1)}, u32[]{:S(2)}, u32[]{:S(2)}) %collective-permute-start.4) | collective-permute-done | bytes 131104 | tf_op jit(solution)/shard_map/ppermute | solution.py:42
  21.6 0.0 collective-permute-start.5
  21.6 0.1 sums.1
  21.7 0.0 collective-permute-done.3.own_there
  21.7 0.0 collective-permute-done.7.odd_there
  21.7 1.2 %collective-permute-done.5.even_there = bf16[32,2048]{1,0:T(8,128)(2,1)S(1)} collective-permute-done((bf16[32,2048]{1,0:T(8,128)(2,1)S(1)}, bf16[32,2048]{1,0:T(8,128)(2,1)S(1)}, u32[]{:S(2)}, u32[]{:S(2)}) %collective-permute-start.5) | collective-permute-done | bytes 131104 | tf_op jit(solution)/shard_map/ppermute | solution.py:20
  22.9 4.3 %second_image.1 = (f32[512,128]{1,0:T(8,128)S(1)}, f32[64,8,128]{2,1,0:T(8,128)S(1)}, f32[16,1,128]{2,1,0:T(1,128)S(1)}) custom-call(bf16[1024,192]{1,0:T(8,128)(2,1)S(1)} %get-tuple-element.27.env, bf16[416,512]{1,0:T(8,128)(2,1)S(1)} %get-tuple-element.22.coupling, bf16[3328,128]{1,0:T(8,128)(2,1)S(1)} %bitcast.8, ...), custom_call_target="tpu_custom_call" | custom-call | tf_op jit(solution)/shard_map/second_image/pallas_call | solution.py:304
  27.2 0.2 collective-permute-start.8
  27.4 11.1 %all_to_all.5.refs_4_ = f32[16,1,128]{2,1,0:T(1,128)S(1)} all-to-all(f32[16,1,128]{2,1,0:T(1,128)S(1)} %get-tuple-element.31), channel_id=1, replica_groups=mesh['groups'=2,'brow'=4,'bcol'=2,'mpo'=2] {'brow','bcol','mpo'}, dimensions={0} | all-to-all | bytes 16384 | tf_op jit(solution)/shard_map/all_to_all | solution.py:400
  38.5 0.0 collective-permute-done.8.refs_2_
  38.6 0.9 %outputs.1 = (bf16[512,128]{1,0:T(8,128)(2,1)}, bf16[512,128]{1,0:T(8,128)(2,1)}, f32[2,2]{1,0:T(2,128)}) custom-call(f32[512,128]{1,0:T(8,128)S(1)} %get-tuple-element.26.image.first.refs_0_, f32[512,128]{1,0:T(8,128)S(1)} %get-tuple-element.29.refs_1_, f32[64,8,128]{2,1,0:T(8,128)S(1)} %collective-permute-done.8.refs_2_, bf16[1024,128]{1,0:T(8,128)(2,1)S(1)} %bitcast.13, ...), custom_call_target="tpu_custom_call" | custom-call | tf_op jit(solution)/shard_map/outputs/pallas_call | solution.py:304
  (1 shorter events, 0.0 us)
Async XLA Ops:
  0.6 7.8 %collective-permute-start = (bf16[1024,128]{1,0:T(8,128)(2,1)}, bf16[1024,128]{1,0:T(8,128)(2,1)S(1)}, u32[]{:S(2)}, u32[]{:S(2)}) collective-permute-start(bf16[1024,128]{1,0:T(8,128)(2,1)} %bitcast.9), channel_id=1, source_target_pairs={{0,4},{1,3},{2,6},{3,1},{4,0},{5,9},{6,2},{7,11},{8,12},{9,5},{10,... | collective-permute-start | bytes 786440 | tf_op jit(solution)/shard_map/ppermute | solution.py:42
  3.7 2.2 %collective-permute-start.1 = (bf16[13,64,192]{2,1,0:T(8,128)(2,1)}, bf16[13,64,192]{2,1,0:T(8,128)(2,1)S(1)}, u32[]{:S(2)}, u32[]{:S(2)}) collective-permute-start(bf16[13,64,192]{2,1,0:T(8,128)(2,1)} %env_mine.1), channel_id=1, source_target_pairs={{0,1},{1,0},{2,3},{3,2},{4,5},{5,4},{6,7},{7,6},{8,9},{9,8},{10,11... | collective-permute-start | bytes 958472 | tf_op jit(solution)/shard_map/ppermute | solution.py:20
  3.7 0.7 %copy-start.3 = (s32[256]{0:T(256)S(1)}, s32[256]{0:T(256)}, u32[]{:S(2)}) copy-start(s32[256]{0:T(256)} %param.11) | copy-start | bytes 3076
  4.6 1.3 %copy-start.2 = (bf16[13,64,192]{2,1,0:T(8,128)(2,1)S(1)}, bf16[13,64,192]{2,1,0:T(8,128)(2,1)}, u32[]{:S(2)}) copy-start(bf16[13,64,192]{2,1,0:T(8,128)(2,1)} %env_mine.1) | copy-start | bytes 958468
  5.9 3.1 %copy-start.1 = (bf16[64,16,128]{2,1,0:T(8,128)(2,1)S(1)}, bf16[64,16,128]{2,1,0:T(8,128)(2,1)}, u32[]{:S(2)}) copy-start(bf16[64,16,128]{2,1,0:T(8,128)(2,1)} %param.6) | copy-start | bytes 786436
  8.4 1.7 %copy-start = (bf16[26,128,128]{2,1,0:T(8,128)(2,1)S(1)}, bf16[26,128,128]{2,1,0:T(8,128)(2,1)}, u32[]{:S(2)}) copy-start(bf16[26,128,128]{2,1,0:T(8,128)(2,1)} %param.8) | copy-start | bytes 2555908
  8.4 1.7 %collective-permute-start.2 = (bf16[1024,128]{1,0:T(8,128)(2,1)S(1)}, bf16[1024,128]{1,0:T(8,128)(2,1)S(1)}, u32[]{:S(2)}, u32[]{:S(2)}) collective-permute-start(bf16[1024,128]{1,0:T(8,128)(2,1)S(1)} %collective-permute-done.direct), channel_id=1, source_target_pairs={{0,1},{1,0},{2,3},{3,2},{4,5},{5,4},{6,7},{7,6},{8,9},{9,8},{10,11... | collective-permute-start | bytes 786440 | tf_op jit(solution)/shard_map/ppermute | solution.py:20
  14.5 5.8 %collective-permute-start.6 = (bf16[32,2048]{1,0:T(8,128)(2,1)S(1)}, bf16[32,2048]{1,0:T(8,128)(2,1)S(1)}, u32[]{:S(2)}, u32[]{:S(2)}) collective-permute-start(bf16[32,2048]{1,0:T(8,128)(2,1)S(1)} %get-tuple-element.28.own_here), channel_id=1, source_target_pairs={{0,2},{1,3},{2,0},{3,1},{4,8},{5,9},{6,10},{7,11},{8,4},{9,5},{10,... | collective-permute-start | bytes 393224 | tf_op jit(solution)/shard_map/ppermute | solution.py:42
  16.2 5.4 %collective-permute-start.4 = (bf16[32,2048]{1,0:T(8,128)(2,1)S(1)}, bf16[32,2048]{1,0:T(8,128)(2,1)S(1)}, u32[]{:S(2)}, u32[]{:S(2)}) collective-permute-start(bf16[32,2048]{1,0:T(8,128)(2,1)S(1)} %get-tuple-element.28.own_here), channel_id=1, source_target_pairs={{0,4},{1,5},{2,6},{3,7},{4,0},{5,1},{6,2},{7,3},{8,12},{9,13},{10,... | collective-permute-start | bytes 393224 | tf_op jit(solution)/shard_map/ppermute | solution.py:42
  17.9 3.8 %collective-permute-start.3 = (bf16[32,2048]{1,0:T(8,128)(2,1)S(1)}, bf16[32,2048]{1,0:T(8,128)(2,1)S(1)}, u32[]{:S(2)}, u32[]{:S(2)}) collective-permute-start(bf16[32,2048]{1,0:T(8,128)(2,1)S(1)} %get-tuple-element.28.own_here), channel_id=1, source_target_pairs={{0,1},{1,0},{2,3},{3,2},{4,5},{5,4},{6,7},{7,6},{8,9},{9,8},{10,11... | collective-permute-start | bytes 393224 | tf_op jit(solution)/shard_map/ppermute | solution.py:20
  20.4 1.3 %collective-permute-start.7 = (bf16[32,2048]{1,0:T(8,128)(2,1)S(1)}, bf16[32,2048]{1,0:T(8,128)(2,1)S(1)}, u32[]{:S(2)}, u32[]{:S(2)}) collective-permute-start(bf16[32,2048]{1,0:T(8,128)(2,1)S(1)} %collective-permute-done.6.odd_here), channel_id=1, source_target_pairs={{0,1},{1,0},{2,3},{3,2},{4,5},{5,4},{6,7},{7,6},{8,9},{9,8},{10,11... | collective-permute-start | bytes 393224 | tf_op jit(solution)/shard_map/ppermute | solution.py:20
  21.6 1.3 %collective-permute-start.5 = (bf16[32,2048]{1,0:T(8,128)(2,1)S(1)}, bf16[32,2048]{1,0:T(8,128)(2,1)S(1)}, u32[]{:S(2)}, u32[]{:S(2)}) collective-permute-start(bf16[32,2048]{1,0:T(8,128)(2,1)S(1)} %collective-permute-done.4.even_here), channel_id=1, source_target_pairs={{0,1},{1,0},{2,3},{3,2},{4,5},{5,4},{6,7},{7,6},{8,9},{9,8},{10,11... | collective-permute-start | bytes 393224 | tf_op jit(solution)/shard_map/ppermute | solution.py:20
  27.2 11.3 %collective-permute-start.8 = (f32[64,8,128]{2,1,0:T(8,128)S(1)}, f32[64,8,128]{2,1,0:T(8,128)S(1)}, u32[]{:S(2)}, u32[]{:S(2)}) collective-permute-start(f32[64,8,128]{2,1,0:T(8,128)S(1)} %get-tuple-element.30), channel_id=1, source_target_pairs={{0,1},{1,0},{2,3},{3,2},{4,5},{5,4},{6,7},{7,6},{8,9},{9,8},{10,11... | collective-permute-start | bytes 786440 | tf_op jit(solution)/shard_map/ppermute | solution.py:20

commit v10 on v9

--- a/solution.py
+++ b/solution.py
@@ -10,7 +10,7 @@
 GROW = 1.0 / SHRINK
 SLOT = 32
 LOCAL = 4
-GROUP = 8
+GROUP = 16
 VMEM_LIMIT = 40 * 2**20
 SHORT = pl.CostEstimate(flops=10**9, bytes_accessed=2**21, transcendentals=0)
 WHOLE = pl.BlockSpec(memory_space=pltpu.VMEM)

time: 39.6 us -> 39.6 us (level)
  no operation moved by 1% of the time
where the time goes in v10:
time: 39.6 us; the launch traced here: 39.4 us
  Pallas kernels  12.5 us (32%)
  blocking collectives  11.1 us (28%)
  starting transfers between devices  7.17 us (18%)
  waiting for transfers between devices  5.7 us (14%)
  other arithmetic  1.35 us (3%)
  local copies, waits for them, and re-layouts  0.84 us (2%)
  between operations  0.68 us (2%)
    pallas_call x6, Pallas kernels, call(): pl.pallas_call(kernel, out_shape=tuple((jax.ShapeDtypeStruct(shape, dtype...  12.5 us
    all_to_all x1, blocking collectives, per_device(): gathered = lax.all_to_all(totals, axes, 0, 0)  11.1 us
    ppermute x3, starting transfers between devices, trade(): return lax.ppermute(x, ('brow', 'bcol', 'mpo'), pairs)  6.41 us
    ppermute x3, waiting for transfers between devices, trade(): return lax.ppermute(x, ('brow', 'bcol', 'mpo'), pairs)  3.72 us
    ppermute x6, waiting for transfers between devices, swap_cores(): return lax.ppermute(x, 'mpo', [(0, 1), (1, 0)])  1.98 us
    concatenate x1, other arithmetic, per_device(): both = jnp.concatenate([mpo_left, mpo_right], axis=0)  1.2 us
  transfers between devices with their start and end apart: 9, of which 4 were waited for; matrix products, arithmetic and copies ran while one was open for 4% of the time, Pallas kernels for 8%

profile of v10, /device:TPU:0, one launch (start us, length us, event | category | flops | bytes accessed | tf_op | source)
XLA Modules:
  0.0 39.4 jit_solution(9973002544189449701)
XLA Ops:
  0.6 3.1 %collective-permute-start = (bf16[1024,128]{1,0:T(8,128)(2,1)}, bf16[1024,128]{1,0:T(8,128)(2,1)S(1)}, u32[]{:S(2)}, u32[]{:S(2)}) collective-permute-start(bf16[1024,128]{1,0:T(8,128)(2,1)} %bitcast.9), channel_id=1, source_target_pairs={{0,4},{1,3},{2,6},{3,1},{4,0},{5,9},{6,2},{7,11},{8,12},{9,5},{10,... | collective-permute-start | bytes 786440 | tf_op jit(solution)/shard_map/ppermute | solution.py:42
  3.7 0.0 collective-permute-start.1
  3.7 0.0 copy-start.3
  3.7 0.7 %copy-done.3 = s32[256]{0:T(256)S(1)} copy-done((s32[256]{0:T(256)S(1)}, s32[256]{0:T(256)}, u32[]{:S(2)}) %copy-start.3) | copy-done | bytes 1048
  4.4 0.1 pad_add_fusion
  4.5 0.1 dynamic_slice.6
  4.6 0.1 dynamic_slice.7
  4.6 0.0 copy-start.2
  4.6 1.2 %pad_maximum_fusion = f32[52,26,4,4]{1,3,2,0:T(4,128)S(1)} fusion(f32[26,26,4,4]{1,3,2,0:T(4,128)} %param.10, f32[26,26,4,4]{1,3,2,0:T(4,128)} %param.9), kind=kLoop, calls=%fused_computation | loop fusion | flops 21632 | bytes 173056 | tf_op jit(solution)/shard_map/concatenate | solution.py:339
  5.8 0.1 compare_convert_fusion.mask
  5.9 0.0 collective-permute-done.1.env_there
  5.9 0.0 copy-done.2
  5.9 0.0 copy-start.1
  5.9 2.5 %operands.1 = (bf16[1024,192]{1,0:T(8,128)(2,1)S(1)}, bf16[1024,192]{1,0:T(8,128)(2,1)S(1)}, bf16[416,512]{1,0:T(8,128)(2,1)S(1)}) custom-call(bf16[13,64,192]{2,1,0:T(8,128)(2,1)S(1)} %copy-done.2, bf16[13,64,192]{2,1,0:T(8,128)(2,1)S(1)} %collective-permute-done.1.env_there, f32[32,192]{1,0:T(8,128)S(1)} %compare_convert_fusion.mask, f32[832,26]{1,0:T(8,128)S(1)} %bitcast.14), custom_call_target="tpu_custom_call" | custom-call | flops 4000000000 | bytes 8388608 | tf_op jit(solution)/shard_map/operands/pallas_call | solution.py:304
  8.4 0.0 collective-permute-done.direct
  8.4 0.0 copy-start
  8.4 0.6 %collective-permute-start.2 = (bf16[1024,128]{1,0:T(8,128)(2,1)S(1)}, bf16[1024,128]{1,0:T(8,128)(2,1)S(1)}, u32[]{:S(2)}, u32[]{:S(2)}) collective-permute-start(bf16[1024,128]{1,0:T(8,128)(2,1)S(1)} %collective-permute-done.direct), channel_id=1, source_target_pairs={{0,1},{1,0},{2,3},{3,2},{4,5},{5,4},{6,7},{7,6},{8,9},{9,8},{10,11... | collective-permute-start | bytes 786440 | tf_op jit(solution)/shard_map/ppermute | solution.py:20
  9.0 0.0 copy-done.1
  9.0 0.4 %rows.1 = (bf16[64,2048]{1,0:T(8,128)(2,1)S(1)}, bf16[64,2048]{1,0:T(8,128)(2,1)S(1)}) custom-call(bf16[1024,128]{1,0:T(8,128)(2,1)S(1)} %bitcast.10, bf16[1024,128]{1,0:T(8,128)(2,1)S(1)} %collective-permute-done.direct), custom_call_target="tpu_custom_call" | custom-call | flops 1000000000 | bytes 2097152 | tf_op jit(solution)/shard_map/rows/pallas_call | solution.py:304
  9.4 0.7 %collective-permute-done.2.passed_in = bf16[1024,128]{1,0:T(8,128)(2,1)S(1)} collective-permute-done((bf16[1024,128]{1,0:T(8,128)(2,1)S(1)}, bf16[1024,128]{1,0:T(8,128)(2,1)S(1)}, u32[]{:S(2)}, u32[]{:S(2)}) %collective-permute-start.2) | collective-permute-done | bytes 262176 | tf_op jit(solution)/shard_map/ppermute | solution.py:20
  10.2 0.0 copy-done
  10.2 4.3 %first_image.1 = (f32[512,128]{1,0:T(8,128)S(1)}, bf16[32,2048]{1,0:T(8,128)(2,1)S(1)}) custom-call(bf16[1024,192]{1,0:T(8,128)(2,1)S(1)} %get-tuple-element.21.env, bf16[416,512]{1,0:T(8,128)(2,1)S(1)} %get-tuple-element.22.coupling, bf16[3328,128]{1,0:T(8,128)(2,1)S(1)} %bitcast.7, bf16[64,2048]{1,0:T(8,128)(2,1)S(1)} %get-tuple-element.24.vector_rows, ...), custom_call_target="tpu_custom_call" | custom-call | tf_op jit(solution)/shard_map/first_image/pallas_call | solution.py:304
  14.5 1.7 %collective-permute-start.6 = (bf16[32,2048]{1,0:T(8,128)(2,1)S(1)}, bf16[32,2048]{1,0:T(8,128)(2,1)S(1)}, u32[]{:S(2)}, u32[]{:S(2)}) collective-permute-start(bf16[32,2048]{1,0:T(8,128)(2,1)S(1)} %get-tuple-element.28.own_here), channel_id=1, source_target_pairs={{0,2},{1,3},{2,0},{3,1},{4,8},{5,9},{6,10},{7,11},{8,4},{9,5},{10,... | collective-permute-start | bytes 393224 | tf_op jit(solution)/shard_map/ppermute | solution.py:42
  16.1 1.7 %collective-permute-start.4 = (bf16[32,2048]{1,0:T(8,128)(2,1)S(1)}, bf16[32,2048]{1,0:T(8,128)(2,1)S(1)}, u32[]{:S(2)}, u32[]{:S(2)}) collective-permute-start(bf16[32,2048]{1,0:T(8,128)(2,1)S(1)} %get-tuple-element.28.own_here), channel_id=1, source_target_pairs={{0,4},{1,5},{2,6},{3,7},{4,0},{5,1},{6,2},{7,3},{8,12},{9,13},{10,... | collective-permute-start | bytes 393224 | tf_op jit(solution)/shard_map/ppermute | solution.py:42
  17.8 0.0 collective-permute-start.3
  17.8 2.5 %collective-permute-done.6.odd_here = bf16[32,2048]{1,0:T(8,128)(2,1)S(1)} collective-permute-done((bf16[32,2048]{1,0:T(8,128)(2,1)S(1)}, bf16[32,2048]{1,0:T(8,128)(2,1)S(1)}, u32[]{:S(2)}, u32[]{:S(2)}) %collective-permute-start.6) | collective-permute-done | bytes 131104 | tf_op jit(solution)/shard_map/ppermute | solution.py:42
  20.3 0.0 collective-permute-start.7
  20.3 1.2 %collective-permute-done.4.even_here = bf16[32,2048]{1,0:T(8,128)(2,1)S(1)} collective-permute-done((bf16[32,2048]{1,0:T(8,128)(2,1)S(1)}, bf16[32,2048]{1,0:T(8,128)(2,1)S(1)}, u32[]{:S(2)}, u32[]{:S(2)}) %collective-permute-start.4) | collective-permute-done | bytes 131104 | tf_op jit(solution)/shard_map/ppermute | solution.py:42
  21.5 0.0 collective-permute-start.5
  21.5 0.1 sums.1
  21.6 0.0 collective-permute-done.3.own_there
  21.7 0.0 collective-permute-done.7.odd_there
  21.7 1.2 %collective-permute-done.5.even_there = bf16[32,2048]{1,0:T(8,128)(2,1)S(1)} collective-permute-done((bf16[32,2048]{1,0:T(8,128)(2,1)S(1)}, bf16[32,2048]{1,0:T(8,128)(2,1)S(1)}, u32[]{:S(2)}, u32[]{:S(2)}) %collective-permute-start.5) | collective-permute-done | bytes 131104 | tf_op jit(solution)/shard_map/ppermute | solution.py:20
  22.9 4.3 %second_image.1 = (f32[512,128]{1,0:T(8,128)S(1)}, f32[64,8,128]{2,1,0:T(8,128)S(1)}, f32[16,1,128]{2,1,0:T(1,128)S(1)}) custom-call(bf16[1024,192]{1,0:T(8,128)(2,1)S(1)} %get-tuple-element.27.env, bf16[416,512]{1,0:T(8,128)(2,1)S(1)} %get-tuple-element.22.coupling, bf16[3328,128]{1,0:T(8,128)(2,1)S(1)} %bitcast.8, ...), custom_call_target="tpu_custom_call" | custom-call | tf_op jit(solution)/shard_map/second_image/pallas_call | solution.py:304
  27.2 0.2 collective-permute-start.8
  27.4 11.1 %all_to_all.5.refs_4_ = f32[16,1,128]{2,1,0:T(1,128)S(1)} all-to-all(f32[16,1,128]{2,1,0:T(1,128)S(1)} %get-tuple-element.31), channel_id=1, replica_groups=mesh['groups'=2,'brow'=4,'bcol'=2,'mpo'=2] {'brow','bcol','mpo'}, dimensions={0} | all-to-all | bytes 16384 | tf_op jit(solution)/shard_map/all_to_all | solution.py:400
  38.5 0.0 collective-permute-done.8.refs_2_
  38.5 0.9 %outputs.1 = (bf16[512,128]{1,0:T(8,128)(2,1)}, bf16[512,128]{1,0:T(8,128)(2,1)}, f32[2,2]{1,0:T(2,128)}) custom-call(f32[512,128]{1,0:T(8,128)S(1)} %get-tuple-element.26.image.first.refs_0_, f32[512,128]{1,0:T(8,128)S(1)} %get-tuple-element.29.refs_1_, f32[64,8,128]{2,1,0:T(8,128)S(1)} %collective-permute-done.8.refs_2_, bf16[1024,128]{1,0:T(8,128)(2,1)S(1)} %bitcast.13, ...), custom_call_target="tpu_custom_call" | custom-call | tf_op jit(solution)/shard_map/outputs/pallas_call | solution.py:304
  (1 shorter events, 0.0 us)
Async XLA Ops:
  0.6 7.8 %collective-permute-start = (bf16[1024,128]{1,0:T(8,128)(2,1)}, bf16[1024,128]{1,0:T(8,128)(2,1)S(1)}, u32[]{:S(2)}, u32[]{:S(2)}) collective-permute-start(bf16[1024,128]{1,0:T(8,128)(2,1)} %bitcast.9), channel_id=1, source_target_pairs={{0,4},{1,3},{2,6},{3,1},{4,0},{5,9},{6,2},{7,11},{8,12},{9,5},{10,... | collective-permute-start | bytes 786440 | tf_op jit(solution)/shard_map/ppermute | solution.py:42
  3.7 2.2 %collective-permute-start.1 = (bf16[13,64,192]{2,1,0:T(8,128)(2,1)}, bf16[13,64,192]{2,1,0:T(8,128)(2,1)S(1)}, u32[]{:S(2)}, u32[]{:S(2)}) collective-permute-start(bf16[13,64,192]{2,1,0:T(8,128)(2,1)} %env_mine.1), channel_id=1, source_target_pairs={{0,1},{1,0},{2,3},{3,2},{4,5},{5,4},{6,7},{7,6},{8,9},{9,8},{10,11... | collective-permute-start | bytes 958472 | tf_op jit(solution)/shard_map/ppermute | solution.py:20
  3.7 0.7 %copy-start.3 = (s32[256]{0:T(256)S(1)}, s32[256]{0:T(256)}, u32[]{:S(2)}) copy-start(s32[256]{0:T(256)} %param.11) | copy-start | bytes 3076
  4.6 1.3 %copy-start.2 = (bf16[13,64,192]{2,1,0:T(8,128)(2,1)S(1)}, bf16[13,64,192]{2,1,0:T(8,128)(2,1)}, u32[]{:S(2)}) copy-start(bf16[13,64,192]{2,1,0:T(8,128)(2,1)} %env_mine.1) | copy-start | bytes 958468
  5.9 3.1 %copy-start.1 = (bf16[64,16,128]{2,1,0:T(8,128)(2,1)S(1)}, bf16[64,16,128]{2,1,0:T(8,128)(2,1)}, u32[]{:S(2)}) copy-start(bf16[64,16,128]{2,1,0:T(8,128)(2,1)} %param.6) | copy-start | bytes 786436
  8.4 1.7 %copy-start = (bf16[26,128,128]{2,1,0:T(8,128)(2,1)S(1)}, bf16[26,128,128]{2,1,0:T(8,128)(2,1)}, u32[]{:S(2)}) copy-start(bf16[26,128,128]{2,1,0:T(8,128)(2,1)} %param.8) | copy-start | bytes 2555908
  8.4 1.7 %collective-permute-start.2 = (bf16[1024,128]{1,0:T(8,128)(2,1)S(1)}, bf16[1024,128]{1,0:T(8,128)(2,1)S(1)}, u32[]{:S(2)}, u32[]{:S(2)}) collective-permute-start(bf16[1024,128]{1,0:T(8,128)(2,1)S(1)} %collective-permute-done.direct), channel_id=1, source_target_pairs={{0,1},{1,0},{2,3},{3,2},{4,5},{5,4},{6,7},{7,6},{8,9},{9,8},{10,11... | collective-permute-start | bytes 786440 | tf_op jit(solution)/shard_map/ppermute | solution.py:20
  14.5 5.8 %collective-permute-start.6 = (bf16[32,2048]{1,0:T(8,128)(2,1)S(1)}, bf16[32,2048]{1,0:T(8,128)(2,1)S(1)}, u32[]{:S(2)}, u32[]{:S(2)}) collective-permute-start(bf16[32,2048]{1,0:T(8,128)(2,1)S(1)} %get-tuple-element.28.own_here), channel_id=1, source_target_pairs={{0,2},{1,3},{2,0},{3,1},{4,8},{5,9},{6,10},{7,11},{8,4},{9,5},{10,... | collective-permute-start | bytes 393224 | tf_op jit(solution)/shard_map/ppermute | solution.py:42
  16.1 5.4 %collective-permute-start.4 = (bf16[32,2048]{1,0:T(8,128)(2,1)S(1)}, bf16[32,2048]{1,0:T(8,128)(2,1)S(1)}, u32[]{:S(2)}, u32[]{:S(2)}) collective-permute-start(bf16[32,2048]{1,0:T(8,128)(2,1)S(1)} %get-tuple-element.28.own_here), channel_id=1, source_target_pairs={{0,4},{1,5},{2,6},{3,7},{4,0},{5,1},{6,2},{7,3},{8,12},{9,13},{10,... | collective-permute-start | bytes 393224 | tf_op jit(solution)/shard_map/ppermute | solution.py:42
  17.8 3.8 %collective-permute-start.3 = (bf16[32,2048]{1,0:T(8,128)(2,1)S(1)}, bf16[32,2048]{1,0:T(8,128)(2,1)S(1)}, u32[]{:S(2)}, u32[]{:S(2)}) collective-permute-start(bf16[32,2048]{1,0:T(8,128)(2,1)S(1)} %get-tuple-element.28.own_here), channel_id=1, source_target_pairs={{0,1},{1,0},{2,3},{3,2},{4,5},{5,4},{6,7},{7,6},{8,9},{9,8},{10,11... | collective-permute-start | bytes 393224 | tf_op jit(solution)/shard_map/ppermute | solution.py:20
  20.3 1.3 %collective-permute-start.7 = (bf16[32,2048]{1,0:T(8,128)(2,1)S(1)}, bf16[32,2048]{1,0:T(8,128)(2,1)S(1)}, u32[]{:S(2)}, u32[]{:S(2)}) collective-permute-start(bf16[32,2048]{1,0:T(8,128)(2,1)S(1)} %collective-permute-done.6.odd_here), channel_id=1, source_target_pairs={{0,1},{1,0},{2,3},{3,2},{4,5},{5,4},{6,7},{7,6},{8,9},{9,8},{10,11... | collective-permute-start | bytes 393224 | tf_op jit(solution)/shard_map/ppermute | solution.py:20
  21.5 1.3 %collective-permute-start.5 = (bf16[32,2048]{1,0:T(8,128)(2,1)S(1)}, bf16[32,2048]{1,0:T(8,128)(2,1)S(1)}, u32[]{:S(2)}, u32[]{:S(2)}) collective-permute-start(bf16[32,2048]{1,0:T(8,128)(2,1)S(1)} %collective-permute-done.4.even_here), channel_id=1, source_target_pairs={{0,1},{1,0},{2,3},{3,2},{4,5},{5,4},{6,7},{7,6},{8,9},{9,8},{10,11... | collective-permute-start | bytes 393224 | tf_op jit(solution)/shard_map/ppermute | solution.py:20
  27.2 11.3 %collective-permute-start.8 = (f32[64,8,128]{2,1,0:T(8,128)S(1)}, f32[64,8,128]{2,1,0:T(8,128)S(1)}, u32[]{:S(2)}, u32[]{:S(2)}) collective-permute-start(f32[64,8,128]{2,1,0:T(8,128)S(1)} %get-tuple-element.30), channel_id=1, source_target_pairs={{0,1},{1,0},{2,3},{3,2},{4,5},{5,4},{6,7},{7,6},{8,9},{9,8},{10,11... | collective-permute-start | bytes 786440 | tf_op jit(solution)/shard_map/ppermute | solution.py:20

commit v11 on v10

--- a/solution.py
+++ b/solution.py
@@ -20,12 +20,14 @@
     return lax.ppermute(x, "mpo", [(0, 1), (1, 0)])
 
 
-def partner_of(block, slab, odd):
+def partner_of(block, slab, core, odd):
     blocks, slabs = lax.axis_size("brow"), lax.axis_size("bcol")
-    other = (block + 1 if block % 2 else block - 1) if odd else block ^ 1
+    other = (block + 1 if block % 2 else block - 1) if odd[core] else block ^ 1
     if 0 <= other < blocks:
-        return other, slab
-    return block, slab ^ 1 if slab ^ 1 < slabs else slab
+        return other, slab, core
+    if odd[0] == odd[1]:
+        return block, slab, 1 - core
+    return block, slab ^ 1 if slab ^ 1 < slabs else slab, core
 
 
 def place_of(block, slab, core):
@@ -37,8 +39,8 @@
     for block in range(lax.axis_size("brow")):
         for slab in range(lax.axis_size("bcol")):
             for core in range(2):
-                other = partner_of(block, slab, odd[core])
-                pairs.append((place_of(block, slab, core), place_of(*other, core)))
+                other = partner_of(block, slab, core, odd)
+                pairs.append((place_of(block, slab, core), place_of(*other)))
     return lax.ppermute(x, ("brow", "bcol", "mpo"), pairs)
 
 

time: 39.6 us -> 39.6 us (level)
  waiting for transfers between devices: 5.7 us -> 5.11 us
  starting transfers between devices: 7.17 us -> 7.68 us
    ppermute x3, waiting for transfers between devices: 3.72 us -> 3.13 us  [trade(): return lax.ppermute(x, ('brow', 'bcol', 'mpo'), pairs)]
    ppermute x6, starting transfers between devices: 0.76 us -> 1.27 us  [swap_cores(): return lax.ppermute(x, 'mpo', [(0, 1), (1, 0)])]
  transfers between devices with their start and end apart: 9 -> 9, of which waited for: 4 -> 3; matrix products, arithmetic and copies ran while one was open for 4% -> 4% of each run, Pallas kernels for 8% -> 8%
where the time goes in v11:
time: 39.6 us; the launch traced here: 39.4 us
  Pallas kernels  12.5 us (32%)
  blocking collectives  11.2 us (28%)
  starting transfers between devices  7.68 us (19%)
  waiting for transfers between devices  5.11 us (13%)
  other arithmetic  1.35 us (3%)
  local copies, waits for them, and re-layouts  0.84 us (2%)
  between operations  0.69 us (2%)
    pallas_call x6, Pallas kernels, call(): pl.pallas_call(kernel, out_shape=tuple((jax.ShapeDtypeStruct(shape, dtype...  12.5 us
    all_to_all x1, blocking collectives, per_device(): gathered = lax.all_to_all(totals, axes, 0, 0)  11.2 us
    ppermute x3, starting transfers between devices, trade(): return lax.ppermute(x, ('brow', 'bcol', 'mpo'), pairs)  6.41 us
    ppermute x3, waiting for transfers between devices, trade(): return lax.ppermute(x, ('brow', 'bcol', 'mpo'), pairs)  3.13 us
    ppermute x6, waiting for transfers between devices, swap_cores(): return lax.ppermute(x, 'mpo', [(0, 1), (1, 0)])  1.97 us
    ppermute x6, starting transfers between devices, swap_cores(): return lax.ppermute(x, 'mpo', [(0, 1), (1, 0)])  1.27 us
    concatenate x1, other arithmetic, per_device(): both = jnp.concatenate([mpo_left, mpo_right], axis=0)  1.2 us
  transfers between devices with their start and end apart: 9, of which 3 were waited for; matrix products, arithmetic and copies ran while one was open for 4% of the time, Pallas kernels for 8%

profile of v11, /device:TPU:0, one launch (start us, length us, event | category | flops | bytes accessed | tf_op | source)
XLA Modules:
  0.0 39.4 jit_solution(2536414920735462421)
XLA Ops:
  0.6 3.1 %collective-permute-start = (bf16[1024,128]{1,0:T(8,128)(2,1)}, bf16[1024,128]{1,0:T(8,128)(2,1)S(1)}, u32[]{:S(2)}, u32[]{:S(2)}) collective-permute-start(bf16[1024,128]{1,0:T(8,128)(2,1)} %bitcast.9), channel_id=1, source_target_pairs={{0,4},{1,3},{2,6},{3,1},{4,0},{5,9},{6,2},{7,11},{8,12},{9,5},{10,... | collective-permute-start | bytes 786440 | tf_op jit(solution)/shard_map/ppermute | solution.py:44
  3.7 0.0 collective-permute-start.1
  3.7 0.0 copy-start.3
  3.7 0.7 %copy-done.3 = s32[256]{0:T(256)S(1)} copy-done((s32[256]{0:T(256)S(1)}, s32[256]{0:T(256)}, u32[]{:S(2)}) %copy-start.3) | copy-done | bytes 1048
  4.4 0.1 pad_add_fusion
  4.5 0.1 dynamic_slice.6
  4.6 0.1 dynamic_slice.7
  4.6 0.0 copy-start.2
  4.6 1.2 %pad_maximum_fusion = f32[52,26,4,4]{1,3,2,0:T(4,128)S(1)} fusion(f32[26,26,4,4]{1,3,2,0:T(4,128)} %param.10, f32[26,26,4,4]{1,3,2,0:T(4,128)} %param.9), kind=kLoop, calls=%fused_computation | loop fusion | flops 21632 | bytes 173056 | tf_op jit(solution)/shard_map/concatenate | solution.py:341
  5.8 0.1 compare_convert_fusion.mask
  5.9 0.0 collective-permute-done.1.env_there
  5.9 0.0 copy-done.2
  5.9 0.0 copy-start.1
  5.9 2.5 %operands.1 = (bf16[1024,192]{1,0:T(8,128)(2,1)S(1)}, bf16[1024,192]{1,0:T(8,128)(2,1)S(1)}, bf16[416,512]{1,0:T(8,128)(2,1)S(1)}) custom-call(bf16[13,64,192]{2,1,0:T(8,128)(2,1)S(1)} %copy-done.2, bf16[13,64,192]{2,1,0:T(8,128)(2,1)S(1)} %collective-permute-done.1.env_there, f32[32,192]{1,0:T(8,128)S(1)} %compare_convert_fusion.mask, f32[832,26]{1,0:T(8,128)S(1)} %bitcast.14), custom_call_target="tpu_custom_call" | custom-call | flops 4000000000 | bytes 8388608 | tf_op jit(solution)/shard_map/operands/pallas_call | solution.py:306
  8.4 0.0 collective-permute-done.direct
  8.4 0.0 copy-start
  8.4 0.6 %collective-permute-start.2 = (bf16[1024,128]{1,0:T(8,128)(2,1)S(1)}, bf16[1024,128]{1,0:T(8,128)(2,1)S(1)}, u32[]{:S(2)}, u32[]{:S(2)}) collective-permute-start(bf16[1024,128]{1,0:T(8,128)(2,1)S(1)} %collective-permute-done.direct), channel_id=1, source_target_pairs={{0,1},{1,0},{2,3},{3,2},{4,5},{5,4},{6,7},{7,6},{8,9},{9,8},{10,11... | collective-permute-start | bytes 786440 | tf_op jit(solution)/shard_map/ppermute | solution.py:20
  9.0 0.0 copy-done.1
  9.0 0.4 %rows.1 = (bf16[64,2048]{1,0:T(8,128)(2,1)S(1)}, bf16[64,2048]{1,0:T(8,128)(2,1)S(1)}) custom-call(bf16[1024,128]{1,0:T(8,128)(2,1)S(1)} %bitcast.10, bf16[1024,128]{1,0:T(8,128)(2,1)S(1)} %collective-permute-done.direct), custom_call_target="tpu_custom_call" | custom-call | flops 1000000000 | bytes 2097152 | tf_op jit(solution)/shard_map/rows/pallas_call | solution.py:306
  9.4 0.7 %collective-permute-done.2.passed_in = bf16[1024,128]{1,0:T(8,128)(2,1)S(1)} collective-permute-done((bf16[1024,128]{1,0:T(8,128)(2,1)S(1)}, bf16[1024,128]{1,0:T(8,128)(2,1)S(1)}, u32[]{:S(2)}, u32[]{:S(2)}) %collective-permute-start.2) | collective-permute-done | bytes 262176 | tf_op jit(solution)/shard_map/ppermute | solution.py:20
  10.2 0.0 copy-done
  10.2 4.3 %first_image.1 = (f32[512,128]{1,0:T(8,128)S(1)}, bf16[32,2048]{1,0:T(8,128)(2,1)S(1)}) custom-call(bf16[1024,192]{1,0:T(8,128)(2,1)S(1)} %get-tuple-element.21.env, bf16[416,512]{1,0:T(8,128)(2,1)S(1)} %get-tuple-element.22.coupling, bf16[3328,128]{1,0:T(8,128)(2,1)S(1)} %bitcast.7, bf16[64,2048]{1,0:T(8,128)(2,1)S(1)} %get-tuple-element.24.vector_rows, ...), custom_call_target="tpu_custom_call" | custom-call | tf_op jit(solution)/shard_map/first_image/pallas_call | solution.py:306
  14.5 0.4 %collective-permute-start.6 = (bf16[32,2048]{1,0:T(8,128)(2,1)S(1)}, bf16[32,2048]{1,0:T(8,128)(2,1)S(1)}, u32[]{:S(2)}, u32[]{:S(2)}) collective-permute-start(bf16[32,2048]{1,0:T(8,128)(2,1)S(1)} %get-tuple-element.28.own_here), channel_id=1, source_target_pairs={{0,1},{1,0},{2,3},{3,2},{4,8},{5,9},{6,10},{7,11},{8,4},{9,5},{10,... | collective-permute-start | bytes 393224 | tf_op jit(solution)/shard_map/ppermute | solution.py:44
  14.9 2.9 %collective-permute-start.4 = (bf16[32,2048]{1,0:T(8,128)(2,1)S(1)}, bf16[32,2048]{1,0:T(8,128)(2,1)S(1)}, u32[]{:S(2)}, u32[]{:S(2)}) collective-permute-start(bf16[32,2048]{1,0:T(8,128)(2,1)S(1)} %get-tuple-element.28.own_here), channel_id=1, source_target_pairs={{0,4},{1,5},{2,6},{3,7},{4,0},{5,1},{6,2},{7,3},{8,12},{9,13},{10,... | collective-permute-start | bytes 393224 | tf_op jit(solution)/shard_map/ppermute | solution.py:44
  17.8 0.0 collective-permute-start.3
  17.8 0.0 collective-permute-done.6.odd_here
  17.8 0.5 %collective-permute-start.7 = (bf16[32,2048]{1,0:T(8,128)(2,1)S(1)}, bf16[32,2048]{1,0:T(8,128)(2,1)S(1)}, u32[]{:S(2)}, u32[]{:S(2)}) collective-permute-start(bf16[32,2048]{1,0:T(8,128)(2,1)S(1)} %collective-permute-done.6.odd_here), channel_id=1, source_target_pairs={{0,1},{1,0},{2,3},{3,2},{4,5},{5,4},{6,7},{7,6},{8,9},{9,8},{10,11... | collective-permute-start | bytes 393224 | tf_op jit(solution)/shard_map/ppermute | solution.py:20
  18.3 3.1 %collective-permute-done.4.even_here = bf16[32,2048]{1,0:T(8,128)(2,1)S(1)} collective-permute-done((bf16[32,2048]{1,0:T(8,128)(2,1)S(1)}, bf16[32,2048]{1,0:T(8,128)(2,1)S(1)}, u32[]{:S(2)}, u32[]{:S(2)}) %collective-permute-start.4) | collective-permute-done | bytes 131104 | tf_op jit(solution)/shard_map/ppermute | solution.py:44
  21.5 0.0 collective-permute-start.5
  21.5 0.1 sums.1
  21.6 0.0 collective-permute-done.3.own_there
  21.6 0.0 collective-permute-done.7.odd_there
  21.6 1.2 %collective-permute-done.5.even_there = bf16[32,2048]{1,0:T(8,128)(2,1)S(1)} collective-permute-done((bf16[32,2048]{1,0:T(8,128)(2,1)S(1)}, bf16[32,2048]{1,0:T(8,128)(2,1)S(1)}, u32[]{:S(2)}, u32[]{:S(2)}) %collective-permute-start.5) | collective-permute-done | bytes 131104 | tf_op jit(solution)/shard_map/ppermute | solution.py:20
  22.8 4.3 %second_image.1 = (f32[512,128]{1,0:T(8,128)S(1)}, f32[64,8,128]{2,1,0:T(8,128)S(1)}, f32[16,1,128]{2,1,0:T(1,128)S(1)}) custom-call(bf16[1024,192]{1,0:T(8,128)(2,1)S(1)} %get-tuple-element.27.env, bf16[416,512]{1,0:T(8,128)(2,1)S(1)} %get-tuple-element.22.coupling, bf16[3328,128]{1,0:T(8,128)(2,1)S(1)} %bitcast.8, ...), custom_call_target="tpu_custom_call" | custom-call | tf_op jit(solution)/shard_map/second_image/pallas_call | solution.py:306
  27.1 0.2 collective-permute-start.8
  27.3 11.2 %all_to_all.5.refs_4_ = f32[16,1,128]{2,1,0:T(1,128)S(1)} all-to-all(f32[16,1,128]{2,1,0:T(1,128)S(1)} %get-tuple-element.31), channel_id=1, replica_groups=mesh['groups'=2,'brow'=4,'bcol'=2,'mpo'=2] {'brow','bcol','mpo'}, dimensions={0} | all-to-all | bytes 16384 | tf_op jit(solution)/shard_map/all_to_all | solution.py:402
  38.5 0.0 collective-permute-done.8.refs_2_
  38.5 0.9 %outputs.1 = (bf16[512,128]{1,0:T(8,128)(2,1)}, bf16[512,128]{1,0:T(8,128)(2,1)}, f32[2,2]{1,0:T(2,128)}) custom-call(f32[512,128]{1,0:T(8,128)S(1)} %get-tuple-element.26.image.first.refs_0_, f32[512,128]{1,0:T(8,128)S(1)} %get-tuple-element.29.refs_1_, f32[64,8,128]{2,1,0:T(8,128)S(1)} %collective-permute-done.8.refs_2_, bf16[1024,128]{1,0:T(8,128)(2,1)S(1)} %bitcast.13, ...), custom_call_target="tpu_custom_call" | custom-call | tf_op jit(solution)/shard_map/outputs/pallas_call | solution.py:306
  (1 shorter events, 0.0 us)
Async XLA Ops:
  0.6 7.8 %collective-permute-start = (bf16[1024,128]{1,0:T(8,128)(2,1)}, bf16[1024,128]{1,0:T(8,128)(2,1)S(1)}, u32[]{:S(2)}, u32[]{:S(2)}) collective-permute-start(bf16[1024,128]{1,0:T(8,128)(2,1)} %bitcast.9), channel_id=1, source_target_pairs={{0,4},{1,3},{2,6},{3,1},{4,0},{5,9},{6,2},{7,11},{8,12},{9,5},{10,... | collective-permute-start | bytes 786440 | tf_op jit(solution)/shard_map/ppermute | solution.py:44
  3.7 2.2 %collective-permute-start.1 = (bf16[13,64,192]{2,1,0:T(8,128)(2,1)}, bf16[13,64,192]{2,1,0:T(8,128)(2,1)S(1)}, u32[]{:S(2)}, u32[]{:S(2)}) collective-permute-start(bf16[13,64,192]{2,1,0:T(8,128)(2,1)} %env_mine.1), channel_id=1, source_target_pairs={{0,1},{1,0},{2,3},{3,2},{4,5},{5,4},{6,7},{7,6},{8,9},{9,8},{10,11... | collective-permute-start | bytes 958472 | tf_op jit(solution)/shard_map/ppermute | solution.py:20
  3.7 0.7 %copy-start.3 = (s32[256]{0:T(256)S(1)}, s32[256]{0:T(256)}, u32[]{:S(2)}) copy-start(s32[256]{0:T(256)} %param.11) | copy-start | bytes 3076
  4.6 1.3 %copy-start.2 = (bf16[13,64,192]{2,1,0:T(8,128)(2,1)S(1)}, bf16[13,64,192]{2,1,0:T(8,128)(2,1)}, u32[]{:S(2)}) copy-start(bf16[13,64,192]{2,1,0:T(8,128)(2,1)} %env_mine.1) | copy-start | bytes 958468
  5.9 3.1 %copy-start.1 = (bf16[64,16,128]{2,1,0:T(8,128)(2,1)S(1)}, bf16[64,16,128]{2,1,0:T(8,128)(2,1)}, u32[]{:S(2)}) copy-start(bf16[64,16,128]{2,1,0:T(8,128)(2,1)} %param.6) | copy-start | bytes 786436
  8.4 1.7 %copy-start = (bf16[26,128,128]{2,1,0:T(8,128)(2,1)S(1)}, bf16[26,128,128]{2,1,0:T(8,128)(2,1)}, u32[]{:S(2)}) copy-start(bf16[26,128,128]{2,1,0:T(8,128)(2,1)} %param.8) | copy-start | bytes 2555908
  8.4 1.7 %collective-permute-start.2 = (bf16[1024,128]{1,0:T(8,128)(2,1)S(1)}, bf16[1024,128]{1,0:T(8,128)(2,1)S(1)}, u32[]{:S(2)}, u32[]{:S(2)}) collective-permute-start(bf16[1024,128]{1,0:T(8,128)(2,1)S(1)} %collective-permute-done.direct), channel_id=1, source_target_pairs={{0,1},{1,0},{2,3},{3,2},{4,5},{5,4},{6,7},{7,6},{8,9},{9,8},{10,11... | collective-permute-start | bytes 786440 | tf_op jit(solution)/shard_map/ppermute | solution.py:20
  14.5 3.3 %collective-permute-start.6 = (bf16[32,2048]{1,0:T(8,128)(2,1)S(1)}, bf16[32,2048]{1,0:T(8,128)(2,1)S(1)}, u32[]{:S(2)}, u32[]{:S(2)}) collective-permute-start(bf16[32,2048]{1,0:T(8,128)(2,1)S(1)} %get-tuple-element.28.own_here), channel_id=1, source_target_pairs={{0,1},{1,0},{2,3},{3,2},{4,8},{5,9},{6,10},{7,11},{8,4},{9,5},{10,... | collective-permute-start | bytes 393224 | tf_op jit(solution)/shard_map/ppermute | solution.py:44
  14.9 6.5 %collective-permute-start.4 = (bf16[32,2048]{1,0:T(8,128)(2,1)S(1)}, bf16[32,2048]{1,0:T(8,128)(2,1)S(1)}, u32[]{:S(2)}, u32[]{:S(2)}) collective-permute-start(bf16[32,2048]{1,0:T(8,128)(2,1)S(1)} %get-tuple-element.28.own_here), channel_id=1, source_target_pairs={{0,4},{1,5},{2,6},{3,7},{4,0},{5,1},{6,2},{7,3},{8,12},{9,13},{10,... | collective-permute-start | bytes 393224 | tf_op jit(solution)/shard_map/ppermute | solution.py:44
  17.8 3.8 %collective-permute-start.3 = (bf16[32,2048]{1,0:T(8,128)(2,1)S(1)}, bf16[32,2048]{1,0:T(8,128)(2,1)S(1)}, u32[]{:S(2)}, u32[]{:S(2)}) collective-permute-start(bf16[32,2048]{1,0:T(8,128)(2,1)S(1)} %get-tuple-element.28.own_here), channel_id=1, source_target_pairs={{0,1},{1,0},{2,3},{3,2},{4,5},{5,4},{6,7},{7,6},{8,9},{9,8},{10,11... | collective-permute-start | bytes 393224 | tf_op jit(solution)/shard_map/ppermute | solution.py:20
  17.8 3.8 %collective-permute-start.7 = (bf16[32,2048]{1,0:T(8,128)(2,1)S(1)}, bf16[32,2048]{1,0:T(8,128)(2,1)S(1)}, u32[]{:S(2)}, u32[]{:S(2)}) collective-permute-start(bf16[32,2048]{1,0:T(8,128)(2,1)S(1)} %collective-permute-done.6.odd_here), channel_id=1, source_target_pairs={{0,1},{1,0},{2,3},{3,2},{4,5},{5,4},{6,7},{7,6},{8,9},{9,8},{10,11... | collective-permute-start | bytes 393224 | tf_op jit(solution)/shard_map/ppermute | solution.py:20
  21.5 1.3 %collective-permute-start.5 = (bf16[32,2048]{1,0:T(8,128)(2,1)S(1)}, bf16[32,2048]{1,0:T(8,128)(2,1)S(1)}, u32[]{:S(2)}, u32[]{:S(2)}) collective-permute-start(bf16[32,2048]{1,0:T(8,128)(2,1)S(1)} %collective-permute-done.4.even_here), channel_id=1, source_target_pairs={{0,1},{1,0},{2,3},{3,2},{4,5},{5,4},{6,7},{7,6},{8,9},{9,8},{10,11... | collective-permute-start | bytes 393224 | tf_op jit(solution)/shard_map/ppermute | solution.py:20
  27.1 11.4 %collective-permute-start.8 = (f32[64,8,128]{2,1,0:T(8,128)S(1)}, f32[64,8,128]{2,1,0:T(8,128)S(1)}, u32[]{:S(2)}, u32[]{:S(2)}) collective-permute-start(f32[64,8,128]{2,1,0:T(8,128)S(1)} %get-tuple-element.30), channel_id=1, source_target_pairs={{0,1},{1,0},{2,3},{3,2},{4,5},{5,4},{6,7},{7,6},{8,9},{9,8},{10,11... | collective-permute-start | bytes 786440 | tf_op jit(solution)/shard_map/ppermute | solution.py:20
